TPU v7x, 32 devices: a whole 2x2x4 slice. The times are simulated.
32 devices in a mesh: samp: 8 (over z, y), head: 4 (over x, core).
Axes of the slice: x: 2, y: 2, z: 4, core: 2. Of those that a mesh axis runs over, the one named last changes fastest.
Arguments:
- queries: bfloat16 [8, 768, 512], P('samp', 'head'), may hold values from -10 to 10
- keys: bfloat16 [8, 768, 512], P('samp', 'head'), may hold values from -10 to 10
- values: bfloat16 [8, 768, 512], P('samp', 'head'), may hold values from -6 to 6
- out_grad: bfloat16 [8, 768, 512], P('samp', 'head'), may hold values from -6 to 6
- pair: bfloat16 [512, 512, 128], P('head', 'samp'), may hold values from -6 to 6
- ln_gain: float32 [128], replicated, may hold values from 0.25 to 1.75
- proj_weight: bfloat16 [128, 16], replicated, may hold values from -0.5 to 0.5
- token_mask: int32 [512], replicated, may hold values from 0 to 1, as said below
- atom_map: int32 [4096], replicated, may hold values from 0 to 511, never falling along the last dimension, each value on 1 to 24 neighbouring positions
Outputs:
- attended: bfloat16 [8, 768, 512], P('samp', 'head')
- query_grad: bfloat16 [8, 768, 512], P('samp', 'head')
- key_grad: bfloat16 [8, 768, 512], P('samp', 'head')
- value_grad: bfloat16 [8, 768, 512], P('samp', 'head')
- pair_grad: bfloat16 [512, 512, 128], P('head', 'samp')
- weight_grad: float32 [128, 16], replicated
- gain_grad: float32 [128], replicated
Inputs may be any that keep to these rules, and one draw needn't show every extreme that they name: `token_mask`: real tokens form a prefix of 256 or more tokens; the last token is padding.
All inputs are finite; a program needn't handle non-finite values.
Results may differ from a plain program's by a relative error of at most 0.02.
Values may be sent and summed in bfloat16 or wider, within the bound.
No kernel may reach another device: no remote copies, remote signals or barrier semaphores. Data moves between devices by JAX's collectives and lax.ppermute only.
A program may use at most 64 MiB of HBM per device.

v0:
```python
import jax
import jax.numpy as jnp
from jax import lax
from jax.sharding import PartitionSpec as P


def token_weights(atom_map, token_mask):
    count = token_mask.shape[0]
    ends = jnp.searchsorted(atom_map, jnp.arange(count, dtype=jnp.int32), side="right")
    starts = jnp.concatenate([jnp.zeros((1,), jnp.int32), ends[:-1]])
    return (
        (ends - starts).astype(jnp.float32)
        * (count / atom_map.shape[0])
        * token_mask.astype(jnp.float32)
    )


def attend(query_row, key_row, value_row, grad_row, bias, key_keep, tok_weight):
    count = query_row.shape[1]
    local_heads = bias.shape[0]
    query_h = query_row.reshape(local_heads, -1, count)
    key_h = key_row.reshape(local_heads, -1, count)
    value_h = value_row.reshape(local_heads, -1, count)
    inv_root = 1.0 / jnp.sqrt(jnp.float32(query_h.shape[1]))
    scores = jnp.einsum(
        "hdi,hdj->hij", query_h, key_h, preferred_element_type=jnp.float32
    ) * inv_root + bias.astype(jnp.float32)
    scores = jnp.where(key_keep[None, None, :], scores, jnp.float32(-1000000000.0))
    largest = jnp.max(scores, axis=-1, keepdims=True)
    expo = jnp.exp(scores - largest)
    prob = expo / jnp.sum(expo, axis=-1, keepdims=True)
    prob_b = prob.astype(jnp.bfloat16)
    attended = jnp.einsum(
        "hij,hdj->hdi", prob_b, value_h, preferred_element_type=jnp.float32
    ).astype(jnp.bfloat16)
    grad_in = (grad_row.astype(jnp.float32) * tok_weight[None, :]).astype(jnp.bfloat16)
    grad_h = grad_in.reshape(local_heads, -1, count)
    dprob = jnp.einsum("hdi,hdj->hij", grad_h, value_h, preferred_element_type=jnp.float32)
    row_dot = jnp.sum(prob * dprob, axis=-1, keepdims=True)
    dscore = prob * (dprob - row_dot)
    dscore_b = dscore.astype(jnp.bfloat16)
    query_grad = (
        jnp.einsum("hij,hdj->hdi", dscore_b, key_h, preferred_element_type=jnp.float32) * inv_root
    ).astype(jnp.bfloat16)
    key_grad = (
        jnp.einsum("hij,hdi->hdj", dscore_b, query_h, preferred_element_type=jnp.float32) * inv_root
    ).astype(jnp.bfloat16)
    value_grad = jnp.einsum(
        "hij,hdi->hdj", prob_b, grad_h, preferred_element_type=jnp.float32
    ).astype(jnp.bfloat16)
    shape = (-1, count)
    return (
        attended.reshape(shape),
        query_grad.reshape(shape),
        key_grad.reshape(shape),
        value_grad.reshape(shape),
        dscore,
    )


def local(queries, keys, values, out_grad, pair, ln_gain, proj_weight, token_mask, atom_map):
    count = queries.shape[2]
    key_keep = token_mask > 0
    tok_weight = token_weights(atom_map, token_mask)
    wide = pair.astype(jnp.float32)
    center = jnp.mean(wide, axis=-1, keepdims=True)
    spread = jnp.mean(jnp.square(wide - center), axis=-1, keepdims=True)
    inv_std = 1.0 / jnp.sqrt(spread + 1e-05)
    normed = (wide - center) * inv_std
    lnout = (normed * ln_gain).astype(jnp.bfloat16)
    tile_bias = jnp.einsum(
        "ijc,ch->hij", lnout, proj_weight, preferred_element_type=jnp.float32
    ).astype(jnp.bfloat16)
    owned = lax.all_to_all(tile_bias, "head", split_axis=0, concat_axis=1, tiled=True)
    bias = lax.all_gather(owned, "samp", axis=2, tiled=True)

    def one_sample(total, items):
        query_row, key_row, value_row, grad_row = items
        attended, query_grad, key_grad, value_grad, dscore = attend(
            query_row, key_row, value_row, grad_row, bias, key_keep, tok_weight
        )
        return (total + dscore, (attended, query_grad, key_grad, value_grad))

    start = jnp.zeros(bias.shape, jnp.float32)
    bias_partial, outs = lax.scan(one_sample, start, (queries, keys, values, out_grad))
    attended, query_grad, key_grad, value_grad = outs
    summed = lax.psum_scatter(
        bias_partial.astype(jnp.bfloat16), "samp", scatter_dimension=2, tiled=True
    ).astype(jnp.float32)
    bias_grad = lax.all_to_all(
        summed.astype(jnp.bfloat16), "head", split_axis=1, concat_axis=0, tiled=True
    ).astype(summed.dtype)
    highest = lax.Precision.HIGHEST
    lnout_grad = jnp.einsum(
        "hij,ch->ijc", bias_grad, proj_weight.astype(jnp.float32), precision=highest
    )
    weight_part = jnp.einsum("ijc,hij->ch", lnout.astype(jnp.float32), bias_grad, precision=highest)
    gain_part = jnp.sum(lnout_grad * normed, axis=(0, 1))
    weight_sum, gain_sum = lax.psum((weight_part, gain_part), ("samp", "head"))
    scaled = lnout_grad * ln_gain
    pair_grad = (
        scaled
        - jnp.mean(scaled, axis=-1, keepdims=True)
        - normed * jnp.mean(scaled * normed, axis=-1, keepdims=True)
    ) * inv_std
    return (
        attended,
        query_grad,
        key_grad,
        value_grad,
        pair_grad.astype(jnp.bfloat16),
        weight_sum / count,
        gain_sum / count,
    )


def solution(mesh):
    placed = (
        P("samp", "head", None),
        P("samp", "head", None),
        P("samp", "head", None),
        P("samp", "head", None),
        P("head", "samp", None),
        P(),
        P(),
        P(),
        P(),
    )
    return jax.shard_map(
        local,
        mesh=mesh,
        in_specs=placed,
        out_specs=(
            P("samp", "head", None),
            P("samp", "head", None),
            P("samp", "head", None),
            P("samp", "head", None),
            P("head", "samp", None),
            P(),
            P(),
        ),
        check_vma=False,
    )
```

profile of v0, /device:TPU:0, one launch (start us, length us, event | category | flops | bytes accessed | tf_op | source)
XLA Modules:
  0.0 225.5 jit_solution(7275205180806087989)
XLA Ops:
  7.2 3.4 %copy.36 = bf16[128,64,128]{0,2,1:T(8,128)(2,1)S(1)} copy(bf16[128,64,128]{2,1,0:T(8,128)(2,1)} %param.15) | data formatting | bytes 4194304 | tf_op args[4]
  13.5 4.2 %all-to-all-start = ((bf16[16,128,64]{1,2,0:T(8,128)(2,1)}), bf16[16,128,64]{1,2,0:T(8,128)(2,1)S(1)}, u32[]{:S(2)}, u32[]{:S(2)}) async-start(bf16[16,128,64]{1,2,0:T(8,128)(2,1)} %copy.38), calls=%async_computation | async-start | bytes 524288 | tf_op jit(solution)/shard_map/all_to_all | solution.py:74
  17.7 6.0 %all-to-all-done = bf16[16,128,64]{1,2,0:T(8,128)(2,1)S(1)} async-done(((bf16[16,128,64]{1,2,0:T(8,128)(2,1)}), bf16[16,128,64]{1,2,0:T(8,128)(2,1)S(1)}, u32[]{:S(2)}, u32[]{:S(2)}) %all-to-all-start) | async-done | bytes 262176 | tf_op jit(solution)/shard_map/all_to_all | solution.py:74
  24.8 42.1 %while.32 = (s32[]{:T(128)}, u32[512]{0:T(512)S(1)}, u32[512]{0:T(512)S(1)}, s32[4096]{0:T(1024)S(1)}, s32[]{:T(128)}, /*index=5*/s32[]{:T(128)}, s32[]{}) while((s32[]{:T(128)}, u32[512]{0:T(512)S(1)}, u32[512]{0:T(512)S(1)}, s32[4096]{0:T(1024)S(1)}, s32[]{:T(128)}, /*index=5*/s32[]{:T(128)}, s32[]{}) %tuple.55), condition=%wide.region_5.6_spmd.clone, body=%wide.region_4.5_spmd.clone.sunk | while | flops 10244 | bytes 37989 | solution.py:9
  24.9 3.1 %gather_fusion = s32[512]{0:T(512)S(1)} fusion(s32[4096]{0:T(1024)S(1)} %get-tuple-element.218, u32[1024]{0:T(1024)S(1)} %pad_clamp_fusion.2), kind=kCustom, calls=%fused_computation.clone.clone.1 | custom fusion | bytes 6144 | tf_op jit(solution)/shard_map/jit(searchsorted)/jit(_searchsorted_scan_impl)/vmap(jit(_searchsorted_scan_impl))/while/body/eval_jaxpr/gather | solution.py:9
  28.1 3.1 %gather_fusion = s32[512]{0:T(512)S(1)} fusion(s32[4096]{0:T(1024)S(1)} %get-tuple-element.218, u32[1024]{0:T(1024)S(1)} %pad_clamp_fusion.2), kind=kCustom, calls=%fused_computation.clone.clone.1 | custom fusion | bytes 6144 | tf_op jit(solution)/shard_map/jit(searchsorted)/jit(_searchsorted_scan_impl)/vmap(jit(_searchsorted_scan_impl))/while/body/eval_jaxpr/gather | solution.py:9
  31.4 3.1 %gather_fusion = s32[512]{0:T(512)S(1)} fusion(s32[4096]{0:T(1024)S(1)} %get-tuple-element.218, u32[1024]{0:T(1024)S(1)} %pad_clamp_fusion.2), kind=kCustom, calls=%fused_computation.clone.clone.1 | custom fusion | bytes 6144 | tf_op jit(solution)/shard_map/jit(searchsorted)/jit(_searchsorted_scan_impl)/vmap(jit(_searchsorted_scan_impl))/while/body/eval_jaxpr/gather | solution.py:9
  34.6 3.1 %gather_fusion = s32[512]{0:T(512)S(1)} fusion(s32[4096]{0:T(1024)S(1)} %get-tuple-element.218, u32[1024]{0:T(1024)S(1)} %pad_clamp_fusion.2), kind=kCustom, calls=%fused_computation.clone.clone.1 | custom fusion | bytes 6144 | tf_op jit(solution)/shard_map/jit(searchsorted)/jit(_searchsorted_scan_impl)/vmap(jit(_searchsorted_scan_impl))/while/body/eval_jaxpr/gather | solution.py:9
  37.8 3.1 %gather_fusion = s32[512]{0:T(512)S(1)} fusion(s32[4096]{0:T(1024)S(1)} %get-tuple-element.218, u32[1024]{0:T(1024)S(1)} %pad_clamp_fusion.2), kind=kCustom, calls=%fused_computation.clone.clone.1 | custom fusion | bytes 6144 | tf_op jit(solution)/shard_map/jit(searchsorted)/jit(_searchsorted_scan_impl)/vmap(jit(_searchsorted_scan_impl))/while/body/eval_jaxpr/gather | solution.py:9
  41.1 3.1 %gather_fusion = s32[512]{0:T(512)S(1)} fusion(s32[4096]{0:T(1024)S(1)} %get-tuple-element.218, u32[1024]{0:T(1024)S(1)} %pad_clamp_fusion.2), kind=kCustom, calls=%fused_computation.clone.clone.1 | custom fusion | bytes 6144 | tf_op jit(solution)/shard_map/jit(searchsorted)/jit(_searchsorted_scan_impl)/vmap(jit(_searchsorted_scan_impl))/while/body/eval_jaxpr/gather | solution.py:9
  44.3 3.1 %gather_fusion = s32[512]{0:T(512)S(1)} fusion(s32[4096]{0:T(1024)S(1)} %get-tuple-element.218, u32[1024]{0:T(1024)S(1)} %pad_clamp_fusion.2), kind=kCustom, calls=%fused_computation.clone.clone.1 | custom fusion | bytes 6144 | tf_op jit(solution)/shard_map/jit(searchsorted)/jit(_searchsorted_scan_impl)/vmap(jit(_searchsorted_scan_impl))/while/body/eval_jaxpr/gather | solution.py:9
  50.8 3.1 %gather_fusion = s32[512]{0:T(512)S(1)} fusion(s32[4096]{0:T(1024)S(1)} %get-tuple-element.218, u32[1024]{0:T(1024)S(1)} %pad_clamp_fusion.2), kind=kCustom, calls=%fused_computation.clone.clone.1 | custom fusion | bytes 6144 | tf_op jit(solution)/shard_map/jit(searchsorted)/jit(_searchsorted_scan_impl)/vmap(jit(_searchsorted_scan_impl))/while/body/eval_jaxpr/gather | solution.py:9
  54.0 3.1 %gather_fusion = s32[512]{0:T(512)S(1)} fusion(s32[4096]{0:T(1024)S(1)} %get-tuple-element.218, u32[1024]{0:T(1024)S(1)} %pad_clamp_fusion.2), kind=kCustom, calls=%fused_computation.clone.clone.1 | custom fusion | bytes 6144 | tf_op jit(solution)/shard_map/jit(searchsorted)/jit(_searchsorted_scan_impl)/vmap(jit(_searchsorted_scan_impl))/while/body/eval_jaxpr/gather | solution.py:9
  60.5 3.1 %gather_fusion = s32[512]{0:T(512)S(1)} fusion(s32[4096]{0:T(1024)S(1)} %get-tuple-element.218, u32[1024]{0:T(1024)S(1)} %pad_clamp_fusion.2), kind=kCustom, calls=%fused_computation.clone.clone.1 | custom fusion | bytes 6144 | tf_op jit(solution)/shard_map/jit(searchsorted)/jit(_searchsorted_scan_impl)/vmap(jit(_searchsorted_scan_impl))/while/body/eval_jaxpr/gather | solution.py:9
  67.0 8.1 %all-gather.2.cloned.1.call-done = bf16[4,512,512]{1,2,0:T(8,128)(2,1)} async-done(((bf16[4,512,64]{1,2,0:T(8,128)(2,1)}), bf16[4,512,512]{1,2,0:T(8,128)(2,1)}) %all-gather.2.cloned.1.call-update) | async-done | bytes 2097168 | tf_op jit(solution)/shard_map/all_gather | solution.py:75
  75.1 5.3 %fusion.41 = (f32[4,512]{1,0:T(4,128)S(1)}, f32[4,512,512]{1,2,0:T(8,128)}) fusion(bf16[4,512,512]{1,2,0:T(8,128)(2,1)} %all-gather.2.cloned.1.call-done, pred[512]{0:T(512)(128)(4,1)S(1)} %broadcast_compare_fusion, bf16[4,48,512]{2,1,0:T(8,128)(2,1)S(1)} %bitcast.55, bf16[4,48,512]{2,1,0:T(8,128)(2,1)S(1)} %bitcast.63), kind=kOutput, calls=%fused_computation.65 | convolution fusion | flops 106955264 | bytes 6693376 | tf_op jit(solution)/shard_map/while/body/eval_jaxpr/sub | solution.py:30
  86.5 4.6 %convolution_convert_fusion.2 = bf16[4,48,512]{2,1,0:T(8,128)(2,1)} fusion(bf16[4,48,512]{2,1,0:T(8,128)(2,1)S(1)} %bitcast.71, f32[512]{0:T(512)S(1)} %fusion.38, f32[4,512]{1,0:T(4,128)S(1)} %get-tuple-element.165, bf16[4,512,512]{1,2,0:T(8,128)(2,1)} %all-gather.2.cloned.1.call-done, pred[512]{0:T(512)(128)(4,1)S(1)} %broadcast_compare_fusion, ...), kind=kOutput, calls=%fused_computation.39 | convolution fusion | flops 209062400 | bytes 2894336 | tf_op jit(solution)/shard_map/while/body/eval_jaxpr/hij,hdi->hdj/dot_general | solution.py:48
  93.5 59.5 %reduce-scatter.2.cloned.1.call-done = bf16[4,512,64]{1,2,0:T(8,128)(2,1)} async-done(((bf16[4,512,512]{1,2,0:T(8,128)(2,1)}), bf16[4,512,64]{1,2,0:T(8,128)(2,1)}) %reduce-scatter.2.cloned.1.call-update) | async-done | bytes 262160 | tf_op jit(solution)/shard_map/reduce_scatter | solution.py:87
  155.4 3.6 %all-to-all-start.1 = ((bf16[4,2,16384]{2,1,0:T(2,128)(2,1)}), bf16[4,2,16384]{2,1,0:T(2,128)(2,1)S(1)}, u32[]{:S(2)}, u32[]{:S(2)}) async-start(bf16[4,2,16384]{2,1,0:T(2,128)(2,1)} %reshape.96), calls=%async_computation.2 | async-start | bytes 524288 | tf_op jit(solution)/shard_map/all_to_all | solution.py:90
  159.0 4.5 %convolution_convert_fusion.1 = bf16[4,512,48]{1,2,0:T(8,128)(2,1)} fusion(bf16[4,48,512]{2,1,0:T(8,128)(2,1)S(1)} %bitcast.73, f32[4,512]{1,0:T(4,128)S(1)} %get-tuple-element.165, bf16[4,512,512]{1,2,0:T(8,128)(2,1)} %all-gather.2.cloned.1.call-done, pred[512]{0:T(512)(128)(4,1)S(1)} %broadcast_compare_fusion, bf16[4,48,512]{2,1,0:T(8,128)(2,1)S(1)} %bitcast.53, ...), kind=kOutput, calls=%fused_computation.38 | convolution fusion | flops 208767488 | bytes 2892288 | tf_op jit(solution)/shard_map/while/body/eval_jaxpr/hij,hdj->hdi/dot_general | solution.py:33
  166.3 3.5 %fusion.14 = (f32[128]{0:T(128)S(1)}, f32[128,64]{0,1:T(8,128)S(1)}, f32[128,64]{0,1:T(8,128)S(1)}, f32[128,64,128]{0,2,1:T(8,128)}) fusion(bf16[128,64,128]{0,2,1:T(8,128)(2,1)S(1)} %copy-done.4, f32[128,64]{0,1:T(8,128)S(1)} %add_rsqrt_fusion, f32[128,64]{0,1:T(8,128)S(1)} %broadcast_multiply_fusion.2, f32[128]{0:T(128)S(1)} %copy-done.8, ...), kind=kOutput, calls=%fused_computation.21 | convolution fusion | flops 42975104 | bytes 6689792 | tf_op jit(solution)/shard_map/hij,ch->ijc/dot_general | solution.py:94
  169.8 38.8 %all-reduce = (f32[128,16]{0,1:T(8,128)S(1)}, f32[128]{0:T(128)S(1)}) all-reduce(f32[128,16]{0,1:T(8,128)S(1)} %convolution_bitcast_fusion, f32[128]{0:T(128)S(1)} %get-tuple-element.150), channel_id=1, replica_groups=mesh['samp'=8,'head'=4] {'samp','head'}, use_global_device_ids=true, to_apply=%region_10.11 | all-reduce | flops 2176 | bytes 17408 | tf_op jit(solution)/shard_map/psum | solution.py:99
  209.7 4.8 %fusion.13 = bf16[128,64,128]{0,2,1:T(8,128)(2,1)} fusion(bf16[128,64,128]{0,2,1:T(8,128)(2,1)S(1)} %copy-done.4, f32[128,64,128]{0,2,1:T(8,128)} %get-tuple-element.169, f32[128,64]{0,1:T(8,128)S(1)} %get-tuple-element.170, f32[128,64]{0,1:T(8,128)S(1)} %get-tuple-element.171, f32[128]{0:T(128)S(1)} %copy-done.8, f32[128,64]{0,1:T(8,128)S(1)} %add_rsqrt_fusion, ...), kind=kLoop, calls=%fused_computation.20 | loop fusion | flops 9437184 | bytes 8520192 | tf_op jit(solution)/shard_map/convert_element_type | solution.py:111
  214.5 4.1 %copy.47 = bf16[128,64,128]{2,1,0:T(8,128)(2,1)} copy(bf16[128,64,128]{0,2,1:T(8,128)(2,1)} %fusion.13) | data formatting | bytes 4194304
  (122 shorter events, 28.7 us)
Async XLA Ops:
  7.2 68.0 %copy-start = (bf16[1,192,512]{2,1,0:T(8,128)(2,1)S(1)}, bf16[1,192,512]{2,1,0:T(8,128)(2,1)}, u32[]{:S(2)}) copy-start(bf16[1,192,512]{2,1,0:T(8,128)(2,1)} %param.11) | copy-start | bytes 589828
  7.2 4.7 %copy-start.8 = (f32[128]{0:T(128)S(1)}, f32[128]{0:T(128)}, u32[]{:S(2)}) copy-start(f32[128]{0:T(128)} %param.16) | copy-start | bytes 1540
  7.2 4.7 %copy-start.11 = (bf16[128,16]{0,1:T(8,128)(2,1)S(1)}, bf16[128,16]{0,1:T(8,128)(2,1)}, u32[]{:S(2)}) copy-start(bf16[128,16]{0,1:T(8,128)(2,1)} %param.17) | copy-start | bytes 12292
  10.6 2.1 copy-start.3
  11.1 13.7 %copy-start.1 = (s32[4096]{0:T(1024)S(1)}, s32[4096]{0:T(1024)}, u32[]{:S(2)}) copy-start(s32[4096]{0:T(1024)} %param.19) | copy-start | bytes 49156
  13.5 10.2 %all-to-all-start = ((bf16[16,128,64]{1,2,0:T(8,128)(2,1)}), bf16[16,128,64]{1,2,0:T(8,128)(2,1)S(1)}, u32[]{:S(2)}, u32[]{:S(2)}) async-start(bf16[16,128,64]{1,2,0:T(8,128)(2,1)} %copy.38), calls=%async_computation | async-start | bytes 524288 | tf_op jit(solution)/shard_map/all_to_all | solution.py:74
  17.7 57.4 %all-gather.2.cloned.1.call-start = ((), (), s32[]{:S(2)}) async-start(), calls=%async_computation.3 | async-start | bytes 2359296 | tf_op jit(solution)/shard_map/all_gather | solution.py:75
  24.8 128.3 %reduce-scatter.2.cloned.1.call-start = ((), (), s32[]{:S(2)}) async-start(), calls=%async_computation.4 | async-start | bytes 2359296 | tf_op jit(solution)/shard_map/reduce_scatter | solution.py:87
  24.8 42.1 %copy-start.7 = (s32[512]{0:T(512)S(1)}, s32[512]{0:T(512)}, u32[]{:S(2)}) copy-start(s32[512]{0:T(512)} %param.18) | copy-start | bytes 6148
  24.8 50.3 %copy-start.6 = (bf16[1,192,512]{2,1,0:T(8,128)(2,1)S(1)}, bf16[1,192,512]{2,1,0:T(8,128)(2,1)}, u32[]{:S(2)}) copy-start(bf16[1,192,512]{2,1,0:T(8,128)(2,1)} %param.12) | copy-start | bytes 589828
  75.1 5.3 %copy-start.9 = (bf16[1,192,512]{2,1,0:T(8,128)(2,1)S(1)}, bf16[1,192,512]{2,1,0:T(8,128)(2,1)}, u32[]{:S(2)}) copy-start(bf16[1,192,512]{2,1,0:T(8,128)(2,1)} %param.14) | copy-start | bytes 589828
  75.1 5.3 %copy-start.10 = (bf16[1,192,512]{2,1,0:T(8,128)(2,1)S(1)}, bf16[1,192,512]{2,1,0:T(8,128)(2,1)}, u32[]{:S(2)}) copy-start(bf16[1,192,512]{2,1,0:T(8,128)(2,1)} %param.13) | copy-start | bytes 589828
  80.5 3.5 %copy-start.5 = (f32[4,512,512]{1,2,0:T(8,128)S(1)}, f32[4,512,512]{1,2,0:T(8,128)}, u32[]{:S(2)}) copy-start(f32[4,512,512]{1,2,0:T(8,128)} %get-tuple-element.166) | copy-start | bytes 12582916
  86.4 4.6 %copy-start.2 = (bf16[4,512,512]{1,2,0:T(8,128)(2,1)S(1)}, bf16[4,512,512]{1,2,0:T(8,128)(2,1)}, u32[]{:S(2)}) copy-start(bf16[4,512,512]{1,2,0:T(8,128)(2,1)} %multiply_convert_fusion) | copy-start | bytes 6291460
  155.4 9.4 %all-to-all-start.1 = ((bf16[4,2,16384]{2,1,0:T(2,128)(2,1)}), bf16[4,2,16384]{2,1,0:T(2,128)(2,1)S(1)}, u32[]{:S(2)}, u32[]{:S(2)}) async-start(bf16[4,2,16384]{2,1,0:T(2,128)(2,1)} %reshape.96), calls=%async_computation.2 | async-start | bytes 524288 | tf_op jit(solution)/shard_map/all_to_all | solution.py:90
  159.0 6.5 %copy-start.4 = (bf16[128,64,128]{0,2,1:T(8,128)(2,1)S(1)}, bf16[128,64,128]{0,2,1:T(8,128)(2,1)}, u32[]{:S(2)}) copy-start(bf16[128,64,128]{0,2,1:T(8,128)(2,1)} %copy-done.3) | copy-start | bytes 6291460
Sparse Core Ops, SparseCore 0:
  24.9 50.2 all-gather.1
  86.6 66.4 reduce-scatter.1
where the time goes:
time: 226 us; the launch traced here: 225 us
  waiting for transfers between devices  74.9 us (33%)
  local copies, waits for them, and re-layouts  53.6 us (24%)
  blocking collectives  38.8 us (17%)
  matrix products  25.1 us (11%)
  between operations  14.3 us (6%)
  other arithmetic  10.3 us (5%)
  starting transfers between devices  7.84 us (3%)
    reduce_scatter x1, waiting for transfers between devices, local(): lax.psum_scatter(bias_partial.astype(jnp.bfloat16), 'samp', scatter_dimen...  59.5 us
    gather x13, local copies, waits for them, and re-layouts, token_weights(): jnp.searchsorted(atom_map, jnp.arange(count, dtype=jnp.int32), side='right')  40.9 us
    psum x1, blocking collectives, local(): weight_sum, gain_sum = lax.psum((weight_part, gain_part), ('samp', 'head'))  38.8 us
    unnamed x28, local copies, waits for them, and re-layouts  9.28 us
    all_gather x1, waiting for transfers between devices, local(): bias = lax.all_gather(owned, 'samp', axis=2, tiled=True)  8.08 us
    all_to_all x1, waiting for transfers between devices, local(): lax.all_to_all(tile_bias, 'head', split_axis=0, concat_axis=1, tiled=True)  6.03 us
    sub x1, matrix products, attend(): expo = jnp.exp(scores - largest)  5.34 us
    convert_element_type x1, other arithmetic, local(): pair_grad.astype(jnp.bfloat16)  4.81 us
  transfers between devices with their start and end apart: 4, of which 4 were waited for; matrix products, arithmetic and copies ran while one was open for 24% of the time, Pallas kernels for 0%

commit v1 on v0

v1 whole, which is shorter than its diff:
```python
import functools
import math

import jax
import jax.numpy as jnp
from jax import lax
from jax.experimental import pallas as pl
from jax.experimental.pallas import tpu as pltpu
from jax.sharding import Mesh
from jax.sharding import PartitionSpec as P

F32 = jnp.float32
BF16 = jnp.bfloat16
LOG2E = math.log2(math.e)
EPS = 1e-05
MASKED = -1000000000.0
PARAMS = pltpu.CompilerParams(vmem_limit_bytes=48 * 1024 * 1024)
NT = (((1,), (1,)), ((), ()))
TN = (((0,), (0,)), ((), ()))


def dot(a, b, dims=(((1,), (0,)), ((), ()))):
    return lax.dot_general(a, b, dims, preferred_element_type=F32)


def call(kernel, name, flops, moved, **kw):
    return pl.pallas_call(
        kernel,
        name=name,
        compiler_params=PARAMS,
        cost_estimate=pl.CostEstimate(flops=flops, bytes_accessed=moved, transcendentals=0),
        **kw,
    )


def step_of(count, most):
    return max(n for n in range(1, most + 1) if count % n == 0)


def pack_kernel(mates, dim, q_ref, k_ref, v_ref, g_ref, map_ref, mask_ref, send_ref):
    count = mask_ref.shape[1]
    atoms = map_ref.shape[1]
    rows = pl.cdiv(count, 128)
    tall = pl.cdiv(rows, 16) * 16
    token = map_ref[...]
    high = lax.shift_right_logical(token, 7)
    low = jnp.bitwise_and(token, 127)
    is_row = (lax.broadcasted_iota(jnp.int32, (tall, atoms), 0) == high).astype(F32).astype(BF16)
    is_lane = (lax.broadcasted_iota(jnp.int32, (128, atoms), 0) == low).astype(F32).astype(BF16)
    counts = dot(is_row, is_lane, NT)
    line = jnp.concatenate([counts[r : r + 1, :] for r in range(rows)], axis=1)[:, :count]
    weight = line * (count / atoms) * mask_ref[...].astype(F32)
    for m in range(mates):
        part = pl.ds(m * dim, dim)
        send_ref[m, 0:dim, :] = q_ref[0, part, :]
        send_ref[m, dim : 2 * dim, :] = k_ref[0, part, :]
        send_ref[m, 2 * dim : 3 * dim, :] = v_ref[0, part, :]
        send_ref[m, 3 * dim : 4 * dim, :] = (g_ref[0, part, :].astype(F32) * weight).astype(BF16)


def unpack_kernel(mates, dim, got_ref, *out_refs):
    for m in range(mates):
        for n, out_ref in enumerate(out_refs):
            out_ref[0, pl.ds(m * dim, dim), :] = got_ref[m, n * dim : (n + 1) * dim, :]


def norm_kernel(groups, mates, pair_ref, gain_ref, proj_ref, cent_ref, send_ref, inv_ref, bias_s, var_s):
    step = pl.program_id(0)
    block, cols, chan = pair_ref.shape
    heads = proj_ref.shape[0]
    rows = var_s.shape[0]
    wide = pair_ref[...].astype(F32).reshape(block * cols, chan)
    cent = wide - jnp.mean(wide, axis=-1, keepdims=True)
    square = cent * cent
    inv_std = lax.rsqrt(jnp.mean(square, axis=-1, keepdims=True) + EPS)
    lnout = (cent * inv_std * gain_ref[...]).astype(BF16)
    cent_ref[...] = cent.astype(BF16).reshape(block, cols, chan)
    square = square.astype(BF16)
    ones = jnp.full((16, chan), 1.0, BF16)
    for a in range(block):
        part = slice(a * cols, (a + 1) * cols)
        bias_s[pl.ds(step * block + a, heads, stride=rows), :] = dot(proj_ref[...], lnout[part], NT)
        var_s[pl.ds(step * block + a, 1), :] = dot(ones, square[part], NT)[:1] * (1.0 / chan)

    @pl.when(step == pl.num_programs(0) - 1)
    def _():
        inv_ref[...] = lax.rsqrt(var_s[...].T + EPS)
        local = send_ref.shape[0] // (groups * mates)
        for h in range(heads):
            block_t = bias_s[h * rows : (h + 1) * rows, :].T.astype(BF16)
            owner, mate = h // mates, h % mates
            for g in range(groups):
                send_ref[(g * mates + mate) * local + owner] = block_t


def attend_kernel(wide, got_ref, bias_ref, mask_ref, back_ref, grad_ref, key_s, value_s, dk_s, dv_s):
    samples, four, count = got_ref.shape
    dim = four // 4
    root = 1.0 / math.sqrt(dim)
    samp, heads, cols, rows = bias_ref.shape
    first = lax.broadcasted_iota(jnp.int32, (16, count), 0) == 0
    mask_rows = jnp.where(first & (mask_ref[...] <= 0), MASKED, 0.0).astype(BF16)
    one_rows = jnp.where(lax.broadcasted_iota(jnp.int32, (16, wide), 0) == 0, 1.0, 0.0).astype(BF16)
    for s in range(samples):
        keys = got_ref[s, dim : 2 * dim, :]
        key_s[s] = jnp.concatenate([keys, keys, mask_rows], axis=0).T
        value_s[s] = got_ref[s, 2 * dim : 3 * dim, :].T
    per = wide // rows
    for a in range(count // wide):
        lanes = slice(a * wide, (a + 1) * wide)
        bias = jnp.concatenate(
            [bias_ref[:, a * per + p].reshape(count, rows) for p in range(per)], axis=1
        ).astype(F32) * LOG2E
        total = None
        for s in range(samples):
            query = got_ref[s, 0:dim, lanes]
            scaled = query.astype(F32) * (LOG2E * root)
            upper = scaled.astype(BF16)
            lower = (scaled - upper.astype(F32)).astype(BF16)
            scores = dot(key_s[s], jnp.concatenate([upper, lower, one_rows], axis=0)) + bias
            expo = jnp.exp2(scores - jnp.max(scores, axis=0, keepdims=True))
            inv_sum = 1.0 / jnp.sum(expo, axis=0, keepdims=True)
            expo_b = expo.astype(BF16)
            out = dot(got_ref[s, 2 * dim : 3 * dim, :], expo_b) * inv_sum
            back_ref[s, 0:dim, lanes] = out.astype(BF16)
            grad = (got_ref[s, 3 * dim : 4 * dim, lanes].astype(F32) * inv_sum).astype(BF16)
            row_dot = jnp.sum(grad.astype(F32) * out, axis=0, keepdims=True)
            dscore = expo * (dot(value_s[s], grad) - row_dot)
            total = dscore if total is None else total + dscore
            dscore_b = dscore.astype(BF16)
            back_ref[s, dim : 2 * dim, lanes] = (
                dot(got_ref[s, dim : 2 * dim, :], dscore_b) * root
            ).astype(BF16)
            dk = dot(query, dscore_b, NT)
            dv = dot(grad, expo_b, NT)
            if a == 0:
                dk_s[s] = dk
                dv_s[s] = dv
            else:
                dk_s[s] += dk
                dv_s[s] += dv
        total = total.astype(BF16)
        for p in range(per):
            grad_ref[:, a * per + p] = total[:, p * rows : (p + 1) * rows].reshape(samp, cols, rows)
    for s in range(samples):
        back_ref[s, 2 * dim : 3 * dim, :] = (dk_s[s] * root).astype(BF16)
        back_ref[s, 3 * dim : 4 * dim, :] = dv_s[s].astype(BF16)


def reduce_kernel(groups, mates, got_ref, bias_ref, inv_ref, cent_ref, left_ref, sum_ref, plain_s, biased_s):
    step = pl.program_id(0)
    block, cols, chan = cent_ref.shape
    rows = inv_ref.shape[1]
    heads = sum_ref.shape[0]
    local = heads // mates

    @pl.when(step == 0)
    def _():
        sum_ref[...] = jnp.zeros_like(sum_ref)
        inv_std = inv_ref[...]
        for h in range(heads):
            at = (h % mates) * local + h // mates
            grad = got_ref[at].astype(F32)
            for g in range(1, groups):
                grad += got_ref[g * heads + at].astype(F32)
            plain = grad * inv_std
            biased = plain * inv_std * bias_ref[at].astype(F32) * (1.0 / chan)
            plain_s[h * rows : (h + 1) * rows, :] = plain.T
            biased_s[h * rows : (h + 1) * rows, :] = biased.T

    total = sum_ref[...]
    for a in range(block):
        take = pl.ds(step * block + a, heads, stride=rows)
        plain = plain_s[take, :].astype(BF16)
        left_ref[a, 0:heads, :] = plain
        left_ref[a, heads : 2 * heads, :] = biased_s[take, :].astype(BF16)
        total += dot(plain, cent_ref[a])
    sum_ref[...] = total


def pair_kernel(left_ref, right_ref, cent_ref, out_ref):
    block, cols, chan = cent_ref.shape
    for a in range(block):
        both = dot(left_ref[a], right_ref[...], TN)
        out_ref[a] = (both[:, :chan] - cent_ref[a].astype(F32) * both[:, chan:]).astype(BF16)


def final_kernel(scale, sums_ref, gain_ref, proj_ref, weight_ref, gain_grad_ref):
    total = sums_ref[0].astype(F32)
    for n in range(1, sums_ref.shape[0]):
        total += sums_ref[n].astype(F32)
    total = total * scale
    weight_ref[...] = (total * gain_ref[...]).T
    gain_grad_ref[...] = jnp.sum(total * proj_ref[...], axis=0, keepdims=True)


def local(groups, mates, axes, queries, keys, values, out_grad, pair, ln_gain, proj_weight, token_mask, atom_map):
    _, width, count = queries.shape
    rows, cols, chan = pair.shape
    heads = proj_weight.shape[1]
    dim = width // mates
    head_parts = heads // mates
    devices = groups * mates * head_parts
    entries = rows * cols
    gain_row = ln_gain.reshape(1, chan)
    proj_rows = proj_weight.T
    mask_row = token_mask.reshape(1, count)
    whole = lambda *shape: pl.BlockSpec(shape, lambda *_: (0,) * len(shape))

    chunks = jax.ShapeDtypeStruct((mates, 4 * dim, count), BF16)
    tiles = jax.ShapeDtypeStruct((devices, cols, rows), BF16)
    send = call(
        functools.partial(pack_kernel, mates, dim), "pack", 2 * 16 * 128 * atom_map.shape[0],
        16 * width * count, out_shape=chunks,
    )(queries, keys, values, out_grad, atom_map.reshape(1, -1), mask_row)
    got = lax.all_to_all(send, axes[1], 0, 0, tiled=True) if mates > 1 else send

    block = step_of(rows, 16)
    cent, bias_send, inv_std = call(
        functools.partial(norm_kernel, groups, mates), "norm", 2 * entries * chan * heads,
        4 * entries * chan,
        out_shape=(
            jax.ShapeDtypeStruct((rows, cols, chan), BF16),
            tiles,
            jax.ShapeDtypeStruct((cols, rows), F32),
        ),
        grid=(rows // block,),
        in_specs=[
            pl.BlockSpec((block, cols, chan), lambda i: (i, 0, 0)),
            whole(1, chan),
            whole(heads, chan),
        ],
        out_specs=(
            pl.BlockSpec((block, cols, chan), lambda i: (i, 0, 0)),
            whole(devices, cols, rows),
            whole(cols, rows),
        ),
        scratch_shapes=[pltpu.VMEM((heads * rows, cols), F32), pltpu.VMEM((rows, cols), F32)],
    )(pair, gain_row, proj_rows)
    bias = lax.all_to_all(bias_send, axes, 0, 0, tiled=True)

    fine = rows % 128 == 0
    samp = groups * mates
    if fine:
        bias = bias.reshape(samp, head_parts, cols, rows)
    else:
        bias = bias.reshape(samp, head_parts, cols, rows).transpose(0, 2, 1, 3)
        bias = bias.reshape(1, 1, count, count)
    wide = max(bias.shape[3], step_of(count, 256)) if fine else count
    back, grads = call(
        functools.partial(attend_kernel, wide), "attend", 12 * mates * dim * count * count,
        8 * mates * dim * count * 2 + 4 * count * count,
        out_shape=(chunks, jax.ShapeDtypeStruct(bias.shape, BF16)),
        scratch_shapes=[
            pltpu.VMEM((mates, count, 2 * dim + 16), BF16),
            pltpu.VMEM((mates, count, dim), BF16),
            pltpu.VMEM((mates, dim, count), F32),
            pltpu.VMEM((mates, dim, count), F32),
        ],
    )(got, bias, mask_row)
    if not fine:
        grads = grads.reshape(samp, cols, head_parts, rows).transpose(0, 2, 1, 3)
    grads = lax.all_to_all(grads.reshape(devices, cols, rows), axes, 0, 0, tiled=True)
    outs = lax.all_to_all(back, axes[1], 0, 0, tiled=True) if mates > 1 else back
    attended, query_grad, key_grad, value_grad = call(
        functools.partial(unpack_kernel, mates, dim), "unpack", 0, 16 * width * count,
        out_shape=(jax.ShapeDtypeStruct(queries.shape, BF16),) * 4,
    )(outs)

    left, part = call(
        functools.partial(reduce_kernel, groups, mates), "reduce", 2 * entries * chan * heads,
        2 * entries * chan,
        out_shape=(
            jax.ShapeDtypeStruct((rows, 2 * heads, cols), BF16),
            jax.ShapeDtypeStruct((heads, chan), F32),
        ),
        grid=(rows // block,),
        in_specs=[
            whole(devices, cols, rows),
            whole(heads, cols, rows),
            whole(cols, rows),
            pl.BlockSpec((block, cols, chan), lambda i: (i, 0, 0)),
        ],
        out_specs=(
            pl.BlockSpec((block, 2 * heads, cols), lambda i: (i, 0, 0)),
            whole(heads, chan),
        ),
        scratch_shapes=[pltpu.VMEM((heads * rows, cols), F32)] * 2,
    )(grads, bias_send, inv_std, cent)
    parts = jnp.broadcast_to(part[None], (devices, heads, chan))
    sums = lax.all_to_all(parts, axes, 0, 0, tiled=True)

    scaled = proj_rows.astype(F32) * gain_row
    scaled = scaled - jnp.mean(scaled, axis=1, keepdims=True)
    none = jnp.zeros_like(scaled)
    right = jnp.concatenate(
        [jnp.concatenate([scaled, none], axis=1), jnp.concatenate([none, none + 1.0], axis=1)], axis=0
    ).astype(BF16)
    pair_grad = call(
        pair_kernel, "pair_grad", 2 * entries * chan * heads * 4, 4 * entries * chan,
        out_shape=jax.ShapeDtypeStruct(pair.shape, BF16),
        grid=(rows // block,),
        in_specs=[
            pl.BlockSpec((block, 2 * heads, cols), lambda i: (i, 0, 0)),
            whole(2 * heads, 2 * chan),
            pl.BlockSpec((block, cols, chan), lambda i: (i, 0, 0)),
        ],
        out_specs=pl.BlockSpec((block, cols, chan), lambda i: (i, 0, 0)),
    )(left, right, cent)
    weight_grad, gain_grad = call(
        functools.partial(final_kernel, 1.0 / count), "final", 0, 4 * devices * heads * chan,
        out_shape=(
            jax.ShapeDtypeStruct((chan, heads), F32),
            jax.ShapeDtypeStruct((1, chan), F32),
        ),
    )(sums, gain_row, proj_rows.astype(F32))
    return attended, query_grad, key_grad, value_grad, pair_grad, weight_grad, gain_grad.reshape(chan)


def solution(mesh):
    samp, head = mesh.axis_names
    samp_size, head_size = mesh.shape[samp], mesh.shape[head]

    def run(*args):
        heads = args[6].shape[1]
        mates = math.gcd(heads // head_size, samp_size)
        groups = samp_size // mates
        axes = ("group", "mate", "part")
        fine = Mesh(mesh.devices.reshape(groups, mates, head_size), axes)
        by_sample = P(("group", "mate"), "part", None)
        by_pair = P("part", ("group", "mate"), None)
        return jax.shard_map(
            functools.partial(local, groups, mates, axes),
            mesh=fine,
            in_specs=(by_sample,) * 4 + (by_pair,) + (P(),) * 4,
            out_specs=(by_sample,) * 4 + (by_pair, P(), P()),
            check_vma=False,
        )(*args)

    return run
```

time: 226 us -> 102 us (0.45)
  waiting for transfers between devices: 74.9 us -> 21.4 us
  local copies, waits for them, and re-layouts: 53.6 us -> 10.2 us
  matrix products: 25.1 us -> 0 us
  Pallas kernels: 0 us -> 23.3 us
  between operations: 14.3 us -> 0.77 us
  other arithmetic: 10.3 us -> 0.2 us
  blocking collectives: 38.8 us -> 31.7 us
  starting transfers between devices: 7.84 us -> 13.5 us
    reduce_scatter x1 -> x0, waiting for transfers between devices: 59.5 us -> none  [local(): lax.psum_scatter(bias_partial.astype(jnp.bfloat16), 'samp', scatter_dimen...]
    gather x13 -> x0, local copies, waits for them, and re-layouts: 40.9 us -> none  [token_weights(): jnp.searchsorted(atom_map, jnp.arange(count, dtype=jnp.int32), side='right')]
    psum x1 -> x0, blocking collectives: 38.8 us -> none  [local(): weight_sum, gain_sum = lax.psum((weight_part, gain_part), ('samp', 'head'))]
    all_to_all x0 -> x2, blocking collectives: none -> 31.7 us  [the longest x1 17.6 us: local(): lax.all_to_all(grads.reshape(devices, cols, rows), axes, 0, 0, tiled=True)]
    pallas_call x0 -> x7, Pallas kernels: none -> 23.3 us  [the longest x1 7.37 us: local(): call(functools.partial(norm_kernel, groups, mates), 'norm', 2 * entries *...]
    dot_general x8 -> x0, matrix products: 19.7 us -> none  [the longest x1 4.56 us: attend(): jnp.einsum('hij,hdi->hdj', prob_b, grad_h, preferred_element_type=jnp.flo...]
    all_to_all x2 -> x3, waiting for transfers between devices: 7.31 us -> 21.4 us  [the longest x1 11.4 us: local(): bias = lax.all_to_all(bias_send, axes, 0, 0, tiled=True)]
    all_gather x1 -> x0, waiting for transfers between devices: 8.08 us -> none  [local(): bias = lax.all_gather(owned, 'samp', axis=2, tiled=True)]
  transfers between devices with their start and end apart: 4 -> 3, of which waited for: 4 -> 3; matrix products, arithmetic and copies ran while one was open for 24% -> 0% of each run, Pallas kernels for 0% -> 10%
where the time goes in v1:
time: 102 us; the launch traced here: 101 us
  blocking collectives  31.7 us (31%)
  Pallas kernels  23.3 us (23%)
  waiting for transfers between devices  21.4 us (21%)
  starting transfers between devices  13.5 us (13%)
  local copies, waits for them, and re-layouts  10.2 us (10%)
    all_to_all x1, blocking collectives, local(): lax.all_to_all(grads.reshape(devices, cols, rows), axes, 0, 0, tiled=True)  17.6 us
    all_to_all x1, blocking collectives, local(): got = lax.all_to_all(send, axes[1], 0, 0, tiled=True) if mates > 1 else send  14.1 us
    all_to_all x1, waiting for transfers between devices, local(): bias = lax.all_to_all(bias_send, axes, 0, 0, tiled=True)  11.4 us
    unnamed x31, local copies, waits for them, and re-layouts  9.52 us
    pallas_call x1, Pallas kernels, local(): call(functools.partial(norm_kernel, groups, mates), 'norm', 2 * entries *...  7.37 us
    all_to_all x1, starting transfers between devices, local(): bias = lax.all_to_all(bias_send, axes, 0, 0, tiled=True)  7.3 us
    all_to_all x1, waiting for transfers between devices, local(): lax.all_to_all(back, axes[1], 0, 0, tiled=True)  6.17 us
    pallas_call x1, Pallas kernels, local(): call(functools.partial(attend_kernel, wide), 'attend', 12 * mates * dim *...  5.71 us
  transfers between devices with their start and end apart: 3, of which 3 were waited for; matrix products, arithmetic and copies ran while one was open for 0% of the time, Pallas kernels for 10%

profile of v1, /device:TPU:0, one launch (start us, length us, event | category | flops | bytes accessed | tf_op | source)
XLA Modules:
  0.0 101.1 jit_solution(3709848307333786344)
XLA Ops:
  0.7 1.6 %copy-done = bf16[128,64,128]{2,1,0:T(8,128)(2,1)S(1)} copy-done((bf16[128,64,128]{2,1,0:T(8,128)(2,1)S(1)}, bf16[128,64,128]{2,1,0:T(8,128)(2,1)}, u32[]{:S(2)}) %copy-start) | copy-done | bytes 2097176
  2.2 0.7 copy-done.8
  2.9 0.7 copy-done.11
  3.6 7.4 %norm.1 = (bf16[128,64,128]{2,1,0:T(8,128)(2,1)S(1)}, bf16[32,64,128]{2,1,0:T(8,128)(2,1)}, f32[64,128]{1,0:T(8,128)S(1)}) custom-call(bf16[128,64,128]{2,1,0:T(8,128)(2,1)S(1)} %copy-done, f32[1,128]{1,0:T(1,128)S(1)} %bitcast.14, bf16[16,128]{1,0:T(8,128)(2,1)S(1)} %bitcast.12), custom_call_target="tpu_custom_call" | custom-call | flops 33554432 | bytes 4194304 | tf_op jit(solution)/shard_map/norm/pallas_call | solution.py:219
  11.0 7.3 %all-to-all-start.1 = ((bf16[32,64,128]{2,1,0:T(8,128)(2,1)}), bf16[32,64,128]{2,1,0:T(8,128)(2,1)S(1)}, u32[]{:S(2)}, u32[]{:S(2)}) async-start(bf16[32,64,128]{2,1,0:T(8,128)(2,1)} %get-tuple-element.20.bias_ref), calls=%async_computation.1 | async-start | bytes 1048576 | tf_op jit(solution)/shard_map/all_to_all | solution.py:240
  18.3 0.9 copy-done.4
  19.2 0.9 copy-done.5
  20.1 0.9 copy-done.6
  21.1 0.9 copy-done.7
  22.4 11.4 %all-to-all-done.1 = bf16[32,64,128]{2,1,0:T(8,128)(2,1)S(1)} async-done(((bf16[32,64,128]{2,1,0:T(8,128)(2,1)}), bf16[32,64,128]{2,1,0:T(8,128)(2,1)S(1)}, u32[]{:S(2)}, u32[]{:S(2)}) %all-to-all-start.1) | async-done | bytes 524320 | tf_op jit(solution)/shard_map/all_to_all | solution.py:240
  33.8 14.1 %all_to_all.25.got_ref = bf16[4,192,512]{2,1,0:T(8,128)(2,1)S(1)} all-to-all(bf16[4,192,512]{2,1,0:T(8,128)(2,1)S(1)} %pack.1), channel_id=1, replica_groups=mesh['group'=2,'mate'=4,'part'=4] {'mate'}, dimensions={0} | all-to-all | bytes 1572864 | tf_op jit(solution)/shard_map/all_to_all | solution.py:216
  47.9 5.7 %attend.1 = (bf16[4,192,512]{2,1,0:T(8,128)(2,1)S(1)}, bf16[8,4,64,128]{3,2,1,0:T(8,128)(2,1)S(1)}) custom-call(bf16[4,192,512]{2,1,0:T(8,128)(2,1)S(1)} %all_to_all.25.got_ref, bf16[8,4,64,128]{3,2,1,0:T(8,128)(2,1)S(1)} %bitcast.10, s32[1,512]{1,0:T(1,128)S(1)} %bitcast.17), custom_call_target="tpu_custom_call" | custom-call | flops 603979776 | bytes 2621440 | tf_op jit(solution)/shard_map/attend/pallas_call | solution.py:250
  53.6 17.6 %all_to_all.26.got_ref = bf16[32,64,128]{2,1,0:T(8,128)(2,1)S(1)} all-to-all(bf16[32,64,128]{2,1,0:T(8,128)(2,1)S(1)} %bitcast.11), channel_id=1, replica_groups=mesh['group'=2,'mate'=4,'part'=4] {'group','mate','part'}, dimensions={0} | all-to-all | bytes 1048576 | tf_op jit(solution)/shard_map/all_to_all | solution.py:263
  71.2 3.5 %all-to-all-start.2 = ((bf16[4,192,512]{2,1,0:T(8,128)(2,1)}), bf16[4,192,512]{2,1,0:T(8,128)(2,1)S(1)}, u32[]{:S(2)}, u32[]{:S(2)}) async-start(bf16[4,192,512]{2,1,0:T(8,128)(2,1)} %copy-done.3), calls=%async_computation.2 | async-start | bytes 1572864 | tf_op jit(solution)/shard_map/all_to_all | solution.py:264
  74.9 3.8 %reduce.1 = (bf16[128,32,64]{2,1,0:T(8,128)(2,1)S(1)}, f32[16,128]{1,0:T(8,128)S(1)}) custom-call(bf16[32,64,128]{2,1,0:T(8,128)(2,1)S(1)} %all_to_all.26.got_ref, bf16[32,64,128]{2,1,0:T(8,128)(2,1)} %get-tuple-element.20.bias_ref, f32[64,128]{1,0:T(8,128)S(1)} %get-tuple-element.27.inv_ref, bf16[128,64,128]{2,1,0:T(8,128)(2,1)S(1)} %get-tuple-element.28.cent_ref), custom_call_target="tpu_custom_call" | custom-call | flops 33554432 | bytes 2097152 | tf_op jit(solution)/shard_map/reduce/pallas_call | solution.py:270
  78.7 1.0 copy-done.1
  79.7 6.2 %all-to-all-done.2.got_ref = bf16[4,192,512]{2,1,0:T(8,128)(2,1)S(1)} async-done(((bf16[4,192,512]{2,1,0:T(8,128)(2,1)}), bf16[4,192,512]{2,1,0:T(8,128)(2,1)S(1)}, u32[]{:S(2)}, u32[]{:S(2)}) %all-to-all-start.2) | async-done | bytes 786464 | tf_op jit(solution)/shard_map/all_to_all | solution.py:264
  85.9 0.7 broadcast_in_dim.2
  86.6 2.7 %all-to-all-start.4 = ((f32[32,16,128]{2,1,0:T(8,128)}), f32[32,16,128]{2,1,0:T(8,128)S(1)}, u32[]{:S(2)}, u32[]{:S(2)}) async-start(f32[32,16,128]{2,1,0:T(8,128)} %broadcast_in_dim.2), calls=%async_computation.4 | async-start | bytes 524288 | tf_op jit(solution)/shard_map/all_to_all | solution.py:291
  89.4 1.2 %copy-done.2 = bf16[128,32,64]{2,1,0:T(8,128)(2,1)S(1)} copy-done((bf16[128,32,64]{2,1,0:T(8,128)(2,1)S(1)}, bf16[128,32,64]{2,1,0:T(8,128)(2,1)}, u32[]{:S(2)}) %copy-start.2) | copy-done | bytes 524312
  90.6 4.5 %pair_grad.1 = bf16[128,64,128]{2,1,0:T(8,128)(2,1)} custom-call(bf16[128,32,64]{2,1,0:T(8,128)(2,1)S(1)} %copy-done.2, bf16[32,256]{1,0:T(8,128)(2,1)S(1)} %fusion.1.right_ref, bf16[128,64,128]{2,1,0:T(8,128)(2,1)S(1)} %get-tuple-element.28.cent_ref), custom_call_target="tpu_custom_call" | custom-call | flops 134217728 | bytes 4194304 | tf_op jit(solution)/shard_map/pair_grad/pallas_call | solution.py:299
  95.1 0.9 unpack.1
  96.1 3.9 %all-to-all-done.4.sums_ref = f32[32,16,128]{2,1,0:T(8,128)S(1)} async-done(((f32[32,16,128]{2,1,0:T(8,128)}), f32[32,16,128]{2,1,0:T(8,128)S(1)}, u32[]{:S(2)}, u32[]{:S(2)}) %all-to-all-start.4) | async-done | bytes 262176 | tf_op jit(solution)/shard_map/all_to_all | solution.py:291
  100.5 0.7 copy.16
  (28 shorter events, 1.2 us)
Async XLA Ops:
  0.6 17.6 %copy-start.13 = (s32[512]{0:T(512)S(1)}, s32[512]{0:T(512)}, u32[]{:S(2)}) copy-start(s32[512]{0:T(512)} %param.16) | copy-start | bytes 6148
  0.6 1.6 %copy-start = (bf16[128,64,128]{2,1,0:T(8,128)(2,1)S(1)}, bf16[128,64,128]{2,1,0:T(8,128)(2,1)}, u32[]{:S(2)}) copy-start(bf16[128,64,128]{2,1,0:T(8,128)(2,1)} %pair_ref.1) | copy-start | bytes 6291460
  2.2 0.7 copy-start.8
  2.9 0.7 copy-start.11
  3.6 14.7 %copy-start.10 = (s32[4096]{0:T(1024)S(1)}, s32[4096]{0:T(1024)}, u32[]{:S(2)}) copy-start(s32[4096]{0:T(1024)} %param.17) | copy-start | bytes 49156
  11.0 22.9 %all-to-all-start.1 = ((bf16[32,64,128]{2,1,0:T(8,128)(2,1)}), bf16[32,64,128]{2,1,0:T(8,128)(2,1)S(1)}, u32[]{:S(2)}, u32[]{:S(2)}) async-start(bf16[32,64,128]{2,1,0:T(8,128)(2,1)} %get-tuple-element.20.bias_ref), calls=%async_computation.1 | async-start | bytes 1048576 | tf_op jit(solution)/shard_map/all_to_all | solution.py:240
  18.3 0.9 copy-start.4
  19.2 0.9 copy-start.5
  20.1 0.9 copy-start.6
  21.1 0.9 copy-start.7
  47.9 26.9 %copy-start.9 = (bf16[128,16]{0,1:T(8,128)(2,1)S(1)}, bf16[128,16]{0,1:T(8,128)(2,1)}, u32[]{:S(2)}) copy-start(bf16[128,16]{0,1:T(8,128)(2,1)} %param.15) | copy-start | bytes 12292
  47.9 26.9 %copy-start.12 = (f32[128]{0:T(128)S(1)}, f32[128]{0:T(128)}, u32[]{:S(2)}) copy-start(f32[128]{0:T(128)} %param.14) | copy-start | bytes 1540
  53.6 17.6 %copy-start.3 = (bf16[4,192,512]{2,1,0:T(8,128)(2,1)}, bf16[4,192,512]{2,1,0:T(8,128)(2,1)S(1)}, u32[]{:S(2)}) copy-start(bf16[4,192,512]{2,1,0:T(8,128)(2,1)S(1)} %get-tuple-element.21) | copy-start | bytes 2359300
  71.2 14.6 %all-to-all-start.2 = ((bf16[4,192,512]{2,1,0:T(8,128)(2,1)}), bf16[4,192,512]{2,1,0:T(8,128)(2,1)S(1)}, u32[]{:S(2)}, u32[]{:S(2)}) async-start(bf16[4,192,512]{2,1,0:T(8,128)(2,1)} %copy-done.3), calls=%async_computation.2 | async-start | bytes 1572864 | tf_op jit(solution)/shard_map/all_to_all | solution.py:264
  74.8 14.6 %copy-start.14 = (bf16[16,256]{1,0:T(8,128)(2,1)S(1)}, bf16[16,256]{1,0:T(8,128)(2,1)}, u32[]{:S(2)}) copy-start(bf16[16,256]{1,0:T(8,128)(2,1)} %constant.10.clone.1) | copy-start | bytes 24580
  78.7 1.0 copy-start.1
  86.6 13.3 %all-to-all-start.4 = ((f32[32,16,128]{2,1,0:T(8,128)}), f32[32,16,128]{2,1,0:T(8,128)S(1)}, u32[]{:S(2)}, u32[]{:S(2)}) async-start(f32[32,16,128]{2,1,0:T(8,128)} %broadcast_in_dim.2), calls=%async_computation.4 | async-start | bytes 524288 | tf_op jit(solution)/shard_map/all_to_all | solution.py:291
  89.4 1.2 %copy-start.2 = (bf16[128,32,64]{2,1,0:T(8,128)(2,1)S(1)}, bf16[128,32,64]{2,1,0:T(8,128)(2,1)}, u32[]{:S(2)}) copy-start(bf16[128,32,64]{2,1,0:T(8,128)(2,1)} %copy-done.1) | copy-start | bytes 1572868

commit v2 on v1

v2 whole, which is shorter than its diff:
```python
import functools
import math

import jax
import jax.numpy as jnp
from jax import lax
from jax.experimental import pallas as pl
from jax.experimental.pallas import tpu as pltpu
from jax.sharding import Mesh
from jax.sharding import PartitionSpec as P

F32 = jnp.float32
BF16 = jnp.bfloat16
LOG2E = math.log2(math.e)
EPS = 1e-05
MASKED = -1000000000.0
BIG = 60
NT = (((1,), (1,)), ((), ()))
TN = (((0,), (0,)), ((), ()))


def dot(a, b, dims=(((1,), (0,)), ((), ()))):
    return lax.dot_general(a, b, dims, preferred_element_type=F32)


def call(kernel, name, flops, moved, mebi, **kw):
    return pl.pallas_call(
        kernel,
        name=name,
        compiler_params=pltpu.CompilerParams(vmem_limit_bytes=mebi * 1024 * 1024),
        cost_estimate=pl.CostEstimate(flops=flops, bytes_accessed=moved, transcendentals=0),
        **kw,
    )


def step_of(count, most):
    return max(n for n in range(1, most + 1) if count % n == 0)


def pack_kernel(dim, mate_ref, q_ref, k_ref, v_ref, g_ref, map_ref, mask_ref, *send_refs):
    count = mask_ref.shape[1]
    atoms = map_ref.shape[1]
    rows = pl.cdiv(count, 128)
    tall = pl.cdiv(rows, 16) * 16
    token = map_ref[...]
    high = lax.shift_right_logical(token, 7)
    low = jnp.bitwise_and(token, 127)
    is_row = (lax.broadcasted_iota(jnp.int32, (tall, atoms), 0) == high).astype(F32).astype(BF16)
    is_lane = (lax.broadcasted_iota(jnp.int32, (128, atoms), 0) == low).astype(F32).astype(BF16)
    counts = dot(is_row, is_lane, NT)
    line = jnp.concatenate([counts[r : r + 1, :] for r in range(rows)], axis=1)[:, :count]
    weight = line * (count / atoms) * mask_ref[...].astype(F32)
    for k, send_ref in enumerate(send_refs):
        part = pl.ds(pl.multiple_of(jnp.bitwise_xor(mate_ref[0], k) * dim, 16), dim)
        send_ref[0:dim, :] = q_ref[0, part, :]
        send_ref[dim : 2 * dim, :] = k_ref[0, part, :]
        send_ref[2 * dim : 3 * dim, :] = v_ref[0, part, :]
        send_ref[3 * dim : 4 * dim, :] = (g_ref[0, part, :].astype(F32) * weight).astype(BF16)


def unpack_kernel(mates, dim, mate_ref, *refs):
    for k in range(mates):
        part = pl.ds(pl.multiple_of(jnp.bitwise_xor(mate_ref[0], k) * dim, 16), dim)
        for n, out_ref in enumerate(refs[mates:]):
            out_ref[0, part, :] = refs[k][n * dim : (n + 1) * dim, :]


def copies_in(far_ref, near_ref, sems, block):
    return [
        pltpu.make_async_copy(far_ref.at[:, pl.ds(p, block)], near_ref.at[:, pl.ds(p, block)], sems.at[n])
        for n, p in enumerate(range(0, near_ref.shape[1], block))
    ]


def centred(pair):
    halves, block, cols, chan = pair.shape
    rows = pair.astype(F32).reshape(halves * block * cols, chan)
    return rows - jnp.mean(rows, axis=-1, keepdims=True)


def pieces(values, halves, block, cols):
    many = 2 if block % 2 == 0 else 1
    for p in range(0, block, many):
        starts = [(h * block + p + n) * cols for n in range(many) for h in range(halves)]
        yield p, many, jnp.concatenate([values[x : x + cols] for x in starts], axis=0)


def from_halves(block, cols):
    turned = block.T
    return jnp.concatenate([turned[:cols], turned[cols:]], axis=1)


def to_halves(block):
    half = block.shape[1] // 2
    return jnp.concatenate([block[:, :half], block[:, half:]], axis=0).T


def norm_kernel(groups, mates, block, far_ref, gain_ref, proj_ref, send_ref, pair_s, sems, bias_s):
    halves, half, cols, chan = pair_s.shape
    heads = proj_ref.shape[0]
    copies = copies_in(far_ref, pair_s, sems, block)
    for copy in copies:
        copy.start()
    for step, copy in enumerate(copies):
        copy.wait()
        cent = centred(pair_s[:, step * block : (step + 1) * block])
        inv_std = lax.rsqrt(jnp.mean(cent * cent, axis=-1, keepdims=True) + EPS)
        lnout = (cent * inv_std * gain_ref[...]).astype(BF16)
        for p, many, piece in pieces(lnout, halves, block, cols):
            bias = dot(proj_ref[...], piece, NT)
            for n in range(many):
                bias_s[pl.ds(step * block + p + n, heads, stride=half), :] = bias[
                    :, n * halves * cols : (n + 1) * halves * cols
                ]
    local = send_ref.shape[0] // (groups * mates)
    for h in range(heads):
        tile = from_halves(bias_s[h * half : (h + 1) * half, :], cols).astype(BF16)
        for g in range(groups):
            send_ref[(g * mates + h % mates) * local + h // mates] = tile


def prepare_kernel(block, far_ref, cent_ref, inv_ref, pair_s, cent_s, sems, out_sems, var_s):
    halves, half, cols, chan = pair_s.shape
    copies = copies_in(far_ref, pair_s, sems, block)
    outs = copies_in(cent_s, cent_ref, out_sems, block)
    for copy in copies:
        copy.start()
    ones = jnp.full((16, chan), 1.0, BF16)
    for step, copy in enumerate(copies):
        copy.wait()
        part = slice(step * block, (step + 1) * block)
        cent = centred(pair_s[:, part])
        cent_s[:, part] = cent.astype(BF16).reshape(halves, block, cols, chan)
        outs[step].start()
        for p, many, piece in pieces((cent * cent).astype(BF16), halves, block, cols):
            var = dot(ones, piece, NT)[:1] * (1.0 / chan)
            for n in range(many):
                var_s[pl.ds(step * block + p + n, 1), :] = var[:, n * halves * cols : (n + 1) * halves * cols]
    inv_ref[...] = lax.rsqrt(from_halves(var_s[...], cols) + EPS)
    for copy in outs:
        copy.wait()


def attend_kernel(samples, wide, *refs):
    got_refs, refs = refs[:samples], refs[samples:]
    bias_ref, mask_ref, refs = refs[0], refs[1], refs[2:]
    back_refs, refs = refs[:samples], refs[samples:]
    grad_ref, key_s, value_s, dk_s, dv_s = refs
    four, count = got_refs[0].shape
    dim = four // 4
    root = 1.0 / math.sqrt(dim)
    samp, heads, cols, rows = bias_ref.shape
    first = lax.broadcasted_iota(jnp.int32, (16, count), 0) == 0
    mask_rows = jnp.where(first & (mask_ref[...] <= 0), MASKED, 0.0).astype(BF16)
    one_rows = jnp.where(lax.broadcasted_iota(jnp.int32, (16, wide), 0) == 0, 1.0, 0.0).astype(BF16)
    for s in range(samples):
        keys = got_refs[s][dim : 2 * dim, :]
        key_s[s] = jnp.concatenate([keys, keys, mask_rows], axis=0).T
        value_s[s] = got_refs[s][2 * dim : 3 * dim, :].T
    per = wide // rows
    for a in range(count // wide):
        lanes = slice(a * wide, (a + 1) * wide)
        bias = jnp.concatenate(
            [bias_ref[:, a * per + p].reshape(count, rows) for p in range(per)], axis=1
        ).astype(F32) * LOG2E
        total = None
        for s in range(samples):
            query = got_refs[s][0:dim, lanes]
            scaled = query.astype(F32) * (LOG2E * root)
            upper = scaled.astype(BF16)
            lower = (scaled - upper.astype(F32)).astype(BF16)
            scores = dot(key_s[s], jnp.concatenate([upper, lower, one_rows], axis=0)) + bias
            expo = jnp.exp2(scores - jnp.max(scores, axis=0, keepdims=True))
            inv_sum = 1.0 / jnp.sum(expo, axis=0, keepdims=True)
            expo_b = expo.astype(BF16)
            out = dot(got_refs[s][2 * dim : 3 * dim, :], expo_b) * inv_sum
            back_refs[s][0:dim, lanes] = out.astype(BF16)
            grad = (got_refs[s][3 * dim : 4 * dim, lanes].astype(F32) * inv_sum).astype(BF16)
            row_dot = jnp.sum(grad.astype(F32) * out, axis=0, keepdims=True)
            dscore = expo * (dot(value_s[s], grad) - row_dot)
            total = dscore if total is None else total + dscore
            dscore_b = dscore.astype(BF16)
            back_refs[s][dim : 2 * dim, lanes] = (
                dot(got_refs[s][dim : 2 * dim, :], dscore_b) * root
            ).astype(BF16)
            dk = dot(query, dscore_b, NT)
            dv = dot(grad, expo_b, NT)
            if a == 0:
                dk_s[s] = dk
                dv_s[s] = dv
            else:
                dk_s[s] += dk
                dv_s[s] += dv
        total = total.astype(BF16)
        for p in range(per):
            grad_ref[:, a * per + p] = total[:, p * rows : (p + 1) * rows].reshape(samp, cols, rows)
    for s in range(samples):
        back_refs[s][2 * dim : 3 * dim, :] = (dk_s[s] * root).astype(BF16)
        back_refs[s][3 * dim : 4 * dim, :] = dv_s[s].astype(BF16)


def reduce_kernel(groups, mates, block, got_ref, inv_ref, far_ref, sum_ref, cent_s, sems, plain_s):
    halves, half, cols, chan = cent_s.shape
    devices, heads, _ = sum_ref.shape
    copies = copies_in(far_ref, cent_s, sems, block)
    for copy in copies:
        copy.start()
    for h in range(heads):
        plain = gathered(groups, mates, heads, h, got_ref) * inv_ref[...]
        plain_s[h * half : (h + 1) * half, :] = to_halves(plain)
    total = jnp.zeros((heads, chan), F32)
    for step, copy in enumerate(copies):
        copy.wait()
        for p in range(step * block, (step + 1) * block):
            plain = plain_s[pl.ds(p, heads, stride=half), :].astype(BF16)
            total += dot(plain, jnp.concatenate([cent_s[h, p] for h in range(halves)], axis=0))
    rounded = total.astype(BF16)
    for n in range(devices):
        sum_ref[n] = rounded


def place(mates, heads, h):
    return (h % mates) * (heads // mates) + h // mates


def gathered(groups, mates, heads, h, got_ref):
    at = place(mates, heads, h)
    grad = got_ref[at].astype(F32)
    for g in range(1, groups):
        grad += got_ref[g * heads + at].astype(F32)
    return grad


def pair_kernel(
    groups, mates, block, got_ref, bias_ref, inv_ref, gain_ref, proj_ref, far_ref, out_ref,
    cent_s, out_s, sems, out_sems, plain_s, biased_s,
):
    halves, half, cols, chan = cent_s.shape
    heads = proj_ref.shape[0]
    copies = copies_in(far_ref, cent_s, sems, block)
    outs = copies_in(out_s, out_ref, out_sems, block)
    for copy in copies:
        copy.start()
    scaled = proj_ref[...].astype(F32) * gain_ref[...]
    scaled = (scaled - jnp.mean(scaled, axis=1, keepdims=True)).astype(BF16)
    none = jnp.zeros((heads, chan), BF16)
    ones = jnp.ones((heads, chan), BF16)
    right = jnp.concatenate(
        [jnp.concatenate([scaled, none], axis=1), jnp.concatenate([none, ones], axis=1)], axis=0
    )
    inv_std = inv_ref[...]
    for h in range(heads):
        plain = gathered(groups, mates, heads, h, got_ref) * inv_std
        biased = plain * inv_std * bias_ref[place(mates, heads, h)].astype(F32) * (1.0 / chan)
        plain_s[h * half : (h + 1) * half, :] = to_halves(plain)
        biased_s[h * half : (h + 1) * half, :] = to_halves(biased)
    for step, copy in enumerate(copies):
        copy.wait()
        for p in range(step * block, (step + 1) * block):
            take = pl.ds(p, heads, stride=half)
            left = jnp.concatenate([plain_s[take, :], biased_s[take, :]], axis=0).astype(BF16)
            both = dot(left, right, TN)
            for h in range(halves):
                part = slice(h * cols, (h + 1) * cols)
                out_s[h, p] = (both[part, :chan] - cent_s[h, p].astype(F32) * both[part, chan:]).astype(BF16)
        outs[step].start()
    for copy in outs:
        copy.wait()


def final_kernel(scale, sums_ref, gain_ref, proj_ref, weight_ref, gain_grad_ref):
    total = sums_ref[0].astype(F32)
    for n in range(1, sums_ref.shape[0]):
        total += sums_ref[n].astype(F32)
    total = total * scale
    weight_ref[...] = total * gain_ref[...]
    gain_grad_ref[...] = jnp.sum(total * proj_ref[...].astype(F32), axis=0, keepdims=True)


def local(groups, mates, axes, queries, keys, values, out_grad, pair, ln_gain, proj_weight, token_mask, atom_map):
    _, width, count = queries.shape
    rows, cols, chan = pair.shape
    heads = proj_weight.shape[1]
    dim = width // mates
    head_parts = heads // mates
    devices = groups * mates * head_parts
    entries = rows * cols
    half = rows // 2
    gain_row = ln_gain.reshape(1, chan)
    proj_rows = proj_weight.T
    mask_row = token_mask.reshape(1, count)
    pair = pair.reshape(2, half, cols, chan)
    mate = lax.axis_index(axes[1]).astype(jnp.int32).reshape(1)
    whole = lambda *shape: pl.BlockSpec(shape, lambda *_: (0,) * len(shape))
    scalar = pl.BlockSpec(memory_space=pltpu.SMEM)
    vector = pl.BlockSpec(memory_space=pltpu.VMEM)

    def swap(chunks):
        return [
            lax.ppermute(x, axes[1], [(i, i ^ k) for i in range(mates)]) if k else x
            for k, x in enumerate(chunks)
        ]

    block = step_of(half, 16)
    far = pl.BlockSpec(memory_space=pltpu.HBM)
    tiles = jax.ShapeDtypeStruct((devices, cols, rows), BF16)
    by_head = pltpu.VMEM((heads * half, 2 * cols), F32)
    near = pltpu.VMEM(pair.shape, BF16)
    sems = pltpu.SemaphoreType.DMA((half // block,))

    bias_send = call(
        functools.partial(norm_kernel, groups, mates, block), "norm", 2 * entries * chan * heads,
        2 * entries * chan, BIG,
        out_shape=tiles,
        in_specs=[far, vector, vector],
        out_specs=vector,
        scratch_shapes=[near, sems, by_head],
    )(pair, gain_row, proj_rows)
    bias = lax.all_to_all(bias_send, axes, 0, 0, tiled=True)

    chunks = (jax.ShapeDtypeStruct((4 * dim, count), BF16),) * mates
    send = call(
        functools.partial(pack_kernel, dim), "pack", 2 * 16 * 128 * atom_map.shape[0],
        16 * width * count, BIG, out_shape=chunks, in_specs=[scalar] + [vector] * 6,
    )(mate, queries, keys, values, out_grad, atom_map.reshape(1, -1), mask_row)
    got = swap(send)

    cent, inv_std = call(
        functools.partial(prepare_kernel, block), "prepare", 2 * entries * chan * heads, 4 * entries * chan, BIG,
        out_shape=(
            jax.ShapeDtypeStruct(pair.shape, BF16),
            jax.ShapeDtypeStruct((cols, rows), F32),
        ),
        in_specs=[far],
        out_specs=(far, vector),
        scratch_shapes=[near, near, sems, sems, pltpu.VMEM((half, 2 * cols), F32)],
    )(pair)

    fine = rows % 128 == 0
    samp = groups * mates
    bias = bias.reshape(samp, head_parts, cols, rows)
    if not fine:
        bias = bias.transpose(0, 2, 1, 3).reshape(1, 1, count, count)
    wide = max(rows, step_of(count, 256)) if fine else count
    *back, grads = call(
        functools.partial(attend_kernel, mates, wide), "attend", 12 * mates * dim * count * count,
        8 * mates * dim * count * 2 + 4 * count * count, BIG,
        out_shape=chunks + (jax.ShapeDtypeStruct(bias.shape, BF16),),
        scratch_shapes=[
            pltpu.VMEM((mates, count, 2 * dim + 16), BF16),
            pltpu.VMEM((mates, count, dim), BF16),
            pltpu.VMEM((mates, dim, count), F32),
            pltpu.VMEM((mates, dim, count), F32),
        ],
    )(*got, bias, mask_row)
    if not fine:
        grads = grads.reshape(samp, cols, head_parts, rows).transpose(0, 2, 1, 3)
    grads = lax.all_to_all(grads.reshape(devices, cols, rows), axes, 0, 0, tiled=True)
    swapped = swap(back)
    parts = call(
        functools.partial(reduce_kernel, groups, mates, block), "reduce", 2 * entries * chan * heads,
        2 * entries * chan, BIG,
        out_shape=jax.ShapeDtypeStruct((devices, heads, chan), BF16),
        in_specs=[vector, vector, far],
        out_specs=vector,
        scratch_shapes=[near, sems, by_head],
    )(grads, inv_std, cent)
    sums = lax.all_to_all(parts, axes, 0, 0, tiled=True)

    pair_grad = call(
        functools.partial(pair_kernel, groups, mates, block), "pair_grad", 8 * entries * chan * heads,
        4 * entries * chan, BIG,
        out_shape=jax.ShapeDtypeStruct(pair.shape, BF16),
        in_specs=[vector] * 5 + [far],
        out_specs=far,
        scratch_shapes=[near, near, sems, sems, by_head, by_head],
    )(grads, bias_send, inv_std, gain_row, proj_rows, cent)
    pair_grad, swapped = lax.optimization_barrier((pair_grad, swapped))
    attended, query_grad, key_grad, value_grad = call(
        functools.partial(unpack_kernel, mates, dim), "unpack", 0, 16 * width * count, BIG,
        out_shape=(jax.ShapeDtypeStruct(queries.shape, BF16),) * 4,
        in_specs=[scalar] + [vector] * mates,
    )(mate, *swapped)
    weight_rows, gain_grad = call(
        functools.partial(final_kernel, 1.0 / count), "final", 0, 2 * devices * heads * chan, BIG,
        out_shape=(
            jax.ShapeDtypeStruct((heads, chan), F32),
            jax.ShapeDtypeStruct((1, chan), F32),
        ),
    )(sums, gain_row, proj_rows)
    return (
        attended, query_grad, key_grad, value_grad,
        pair_grad.reshape(rows, cols, chan), weight_rows.T, gain_grad.reshape(chan),
    )


def solution(mesh):
    samp, head = mesh.axis_names
    samp_size, head_size = mesh.shape[samp], mesh.shape[head]

    def run(*args):
        heads = args[6].shape[1]
        mates = math.gcd(heads // head_size, samp_size)
        groups = samp_size // mates
        axes = ("group", "mate", "part")
        fine = Mesh(mesh.devices.reshape(groups, mates, head_size), axes)
        by_sample = P(("group", "mate"), "part", None)
        by_pair = P("part", ("group", "mate"), None)
        return jax.shard_map(
            functools.partial(local, groups, mates, axes),
            mesh=fine,
            in_specs=(by_sample,) * 4 + (by_pair,) + (P(),) * 4,
            out_specs=(by_sample,) * 4 + (by_pair, P(), P()),
            check_vma=False,
        )(*args)

    return run
```

time: 102 us -> 90.6 us (0.89)
  blocking collectives: 31.7 us -> 0 us
  Pallas kernels: 23.3 us -> 33.7 us
  waiting for transfers between devices: 21.4 us -> 31.2 us
  starting transfers between devices: 13.5 us -> 21.3 us
  local copies, waits for them, and re-layouts: 10.2 us -> 3.01 us
    all_to_all x2 -> x0, blocking collectives: 31.7 us -> none  [the longest x1 17.6 us: local(): lax.all_to_all(grads.reshape(devices, cols, rows), axes, 0, 0, tiled=True)]
    ppermute x0 -> x6, waiting for transfers between devices: none -> 20 us  [swap(): lax.ppermute(x, axes[1], [(i, i ^ k) for i in range(mates)])]
    all_to_all x1, waiting for transfers between devices: 11.4 us -> 0.01 us  [local(): bias = lax.all_to_all(bias_send, axes, 0, 0, tiled=True)]
    pallas_call x6 -> x7, Pallas kernels: 22.4 us -> 31.6 us  [the longest x1 8.01 us: local(): call(functools.partial(attend_kernel, mates, wide), 'attend', 12 * mates...]
    ppermute x0 -> x6, starting transfers between devices: none -> 7.04 us  [swap(): lax.ppermute(x, axes[1], [(i, i ^ k) for i in range(mates)])]
    unnamed x31 -> x24, local copies, waits for them, and re-layouts: 9.52 us -> 3.01 us
    all_to_all x1, waiting for transfers between devices: 6.17 us -> 11.2 us  [local(): lax.all_to_all(grads.reshape(devices, cols, rows), axes, 0, 0, tiled=True)]
    all_to_all x1, waiting for transfers between devices: 3.86 us -> 0.01 us  [local(): sums = lax.all_to_all(parts, axes, 0, 0, tiled=True)]
  transfers between devices with their start and end apart: 3 -> 9, of which waited for: 3 -> 6; matrix products, arithmetic and copies ran while one was open for 0% -> 0% of each run, Pallas kernels for 10% -> 16%
where the time goes in v2:
time: 90.6 us; the launch traced here: 90 us
  Pallas kernels  33.7 us (37%)
  waiting for transfers between devices  31.2 us (34%)
  starting transfers between devices  21.3 us (24%)
  local copies, waits for them, and re-layouts  3.01 us (3%)
    ppermute x6, waiting for transfers between devices, swap(): lax.ppermute(x, axes[1], [(i, i ^ k) for i in range(mates)])  20 us
    all_to_all x1, waiting for transfers between devices, local(): lax.all_to_all(grads.reshape(devices, cols, rows), axes, 0, 0, tiled=True)  11.2 us
    pallas_call x1, Pallas kernels, local(): call(functools.partial(attend_kernel, mates, wide), 'attend', 12 * mates...  8.01 us
    all_to_all x1, starting transfers between devices, local(): bias = lax.all_to_all(bias_send, axes, 0, 0, tiled=True)  7.3 us
    ppermute x6, starting transfers between devices, swap(): lax.ppermute(x, axes[1], [(i, i ^ k) for i in range(mates)])  7.04 us
    pallas_call x1, Pallas kernels, local(): call(functools.partial(norm_kernel, groups, mates, block), 'norm', 2 * en...  5.98 us
    pallas_call x1, Pallas kernels, local(): call(functools.partial(pair_kernel, groups, mates, block), 'pair_grad', 8...  5.11 us
    pallas_call x1, Pallas kernels, local(): call(functools.partial(prepare_kernel, block), 'prepare', 2 * entries * c...  4.36 us
  transfers between devices with their start and end apart: 9, of which 6 were waited for; matrix products, arithmetic and copies ran while one was open for 0% of the time, Pallas kernels for 16%

profile of v2, /device:TPU:0, one launch (start us, length us, event | category | flops | bytes accessed | tf_op | source)
XLA Modules:
  0.0 90.0 jit_solution(4911159509359712076)
XLA Ops:
  0.6 6.0 %norm.1.bias_ref = bf16[32,64,128]{2,1,0:T(8,128)(2,1)} custom-call(bf16[2,64,64,128]{3,2,1,0:T(8,128)(2,1)} %bitcast.11, f32[1,128]{1,0:T(1,128)} %bitcast.20, bf16[16,128]{1,0:T(8,128)(2,1)} %bitcast.16), custom_call_target="tpu_custom_call" | custom-call | flops 33554432 | bytes 2097152 | tf_op jit(solution)/shard_map/norm/pallas_call | solution.py:311
  6.6 7.3 %all-to-all-start = ((bf16[32,64,128]{2,1,0:T(8,128)(2,1)}), bf16[32,64,128]{2,1,0:T(8,128)(2,1)S(1)}, u32[]{:S(2)}, u32[]{:S(2)}) async-start(bf16[32,64,128]{2,1,0:T(8,128)(2,1)} %norm.1.bias_ref), calls=%async_computation | async-start | bytes 1048576 | tf_op jit(solution)/shard_map/all_to_all | solution.py:319
  13.9 2.5 %pack.1 = (bf16[192,512]{1,0:T(8,128)(2,1)}, bf16[192,512]{1,0:T(8,128)(2,1)}, bf16[192,512]{1,0:T(8,128)(2,1)}, bf16[192,512]{1,0:T(8,128)(2,1)}) custom-call(s32[1]{0:T(128)} %bitcast.mate_ref, bf16[1,192,512]{2,1,0:T(8,128)(2,1)} %q_ref.1, bf16[1,192,512]{2,1,0:T(8,128)(2,1)} %k_ref.1, bf16[1,192,512]{2,1,0:T(8,128)(2,1)} %v_ref.1, ...), custom_call_target="tpu_custom_call" | custom-call | flops 16777216 | bytes 1572864 | tf_op jit(solution)/shard_map/pack/pallas_call | solution.py:322
  16.4 1.8 %collective-permute-start = (bf16[192,512]{1,0:T(8,128)(2,1)}, bf16[192,512]{1,0:T(8,128)(2,1)S(1)}, u32[]{:S(2)}, u32[]{:S(2)}) collective-permute-start(bf16[192,512]{1,0:T(8,128)(2,1)} %get-tuple-element.30), channel_id=1, source_target_pairs={{0,4},{4,0},{8,12},{12,8},{1,5},{5,1},{9,13},{13,9},{2,6},{6,2},{1... | collective-permute-start | bytes 589832 | tf_op jit(solution)/shard_map/ppermute | solution.py:300
  18.2 1.5 %collective-permute-start.1 = (bf16[192,512]{1,0:T(8,128)(2,1)}, bf16[192,512]{1,0:T(8,128)(2,1)S(1)}, u32[]{:S(2)}, u32[]{:S(2)}) collective-permute-start(bf16[192,512]{1,0:T(8,128)(2,1)} %get-tuple-element.31), channel_id=1, source_target_pairs={{0,8},{4,12},{8,0},{12,4},{1,9},{5,13},{9,1},{13,5},{2,10},{6,14},... | collective-permute-start | bytes 589832 | tf_op jit(solution)/shard_map/ppermute | solution.py:300
  19.9 6.3 %collective-permute-done.refs_1_ = bf16[192,512]{1,0:T(8,128)(2,1)S(1)} collective-permute-done((bf16[192,512]{1,0:T(8,128)(2,1)}, bf16[192,512]{1,0:T(8,128)(2,1)S(1)}, u32[]{:S(2)}, u32[]{:S(2)}) %collective-permute-start) | collective-permute-done | bytes 196640 | tf_op jit(solution)/shard_map/ppermute | solution.py:300
  26.3 3.5 %collective-permute-done.1.refs_2_ = bf16[192,512]{1,0:T(8,128)(2,1)S(1)} collective-permute-done((bf16[192,512]{1,0:T(8,128)(2,1)}, bf16[192,512]{1,0:T(8,128)(2,1)S(1)}, u32[]{:S(2)}, u32[]{:S(2)}) %collective-permute-start.1) | collective-permute-done | bytes 196640 | tf_op jit(solution)/shard_map/ppermute | solution.py:300
  29.8 4.8 %collective-permute-done.2.refs_3_ = bf16[192,512]{1,0:T(8,128)(2,1)S(1)} collective-permute-done((bf16[192,512]{1,0:T(8,128)(2,1)}, bf16[192,512]{1,0:T(8,128)(2,1)S(1)}, u32[]{:S(2)}, u32[]{:S(2)}) %collective-permute-start.2) | collective-permute-done | bytes 196640 | tf_op jit(solution)/shard_map/ppermute | solution.py:300
  35.4 8.0 %attend.1 = (bf16[192,512]{1,0:T(8,128)(2,1)}, bf16[192,512]{1,0:T(8,128)(2,1)}, bf16[192,512]{1,0:T(8,128)(2,1)}, bf16[192,512]{1,0:T(8,128)(2,1)}, bf16[8,4,64,128]{3,2,1,0:T(8,128)(2,1)}) custom-call(bf16[192,512]{1,0:T(8,128)(2,1)} %get-tuple-element.29.refs_0_, bf16[192,512]{1,0:T(8,128)(2,1)} %copy-done.9, bf16[192,512]{1,0:T(8,128)(2,1)} %copy-done.10, ...), custom_call_target="tpu_custom_call" | custom-call | flops 603979776 | bytes 2621440 | tf_op jit(solution)/shard_map/attend/pallas_call | solution.py:345
  43.4 3.7 %all-to-all-start.1 = ((bf16[32,64,128]{2,1,0:T(8,128)(2,1)}), bf16[32,64,128]{2,1,0:T(8,128)(2,1)S(1)}, u32[]{:S(2)}, u32[]{:S(2)}) async-start(bf16[32,64,128]{2,1,0:T(8,128)(2,1)} %bitcast.15), calls=%async_computation.1 | async-start | bytes 1048576 | tf_op jit(solution)/shard_map/all_to_all | solution.py:358
  47.2 4.4 %prepare.1 = (bf16[2,64,64,128]{3,2,1,0:T(8,128)(2,1)}, f32[64,128]{1,0:T(8,128)}) custom-call(bf16[2,64,64,128]{3,2,1,0:T(8,128)(2,1)} %bitcast.12), custom_call_target="tpu_custom_call" | custom-call | flops 33554432 | bytes 4194304 | tf_op jit(solution)/shard_map/prepare/pallas_call | solution.py:328
  51.5 11.2 %all-to-all-done.1.got_ref = bf16[32,64,128]{2,1,0:T(8,128)(2,1)S(1)} async-done(((bf16[32,64,128]{2,1,0:T(8,128)(2,1)}), bf16[32,64,128]{2,1,0:T(8,128)(2,1)S(1)}, u32[]{:S(2)}, u32[]{:S(2)}) %all-to-all-start.1) | async-done | bytes 524320 | tf_op jit(solution)/shard_map/all_to_all | solution.py:358
  62.7 0.8 copy-done
  63.5 4.1 %reduce.1 = bf16[32,16,128]{2,1,0:T(8,128)(2,1)} custom-call(bf16[32,64,128]{2,1,0:T(8,128)(2,1)} %copy-done, f32[64,128]{1,0:T(8,128)} %get-tuple-element.34.inv_ref, bf16[2,64,64,128]{3,2,1,0:T(8,128)(2,1)} %get-tuple-element.35.far_ref), custom_call_target="tpu_custom_call" | custom-call | flops 33554432 | bytes 2097152 | tf_op jit(solution)/shard_map/reduce/pallas_call | solution.py:360
  67.6 3.3 %all-to-all-start.2 = ((bf16[32,16,128]{2,1,0:T(8,128)(2,1)}), bf16[32,16,128]{2,1,0:T(8,128)(2,1)S(1)}, u32[]{:S(2)}, u32[]{:S(2)}) async-start(bf16[32,16,128]{2,1,0:T(8,128)(2,1)} %reduce.1), calls=%async_computation.2 | async-start | bytes 262144 | tf_op jit(solution)/shard_map/all_to_all | solution.py:368
  70.9 1.7 %collective-permute-start.3 = (bf16[192,512]{1,0:T(8,128)(2,1)S(1)}, bf16[192,512]{1,0:T(8,128)(2,1)S(1)}, u32[]{:S(2)}, u32[]{:S(2)}) collective-permute-start(bf16[192,512]{1,0:T(8,128)(2,1)S(1)} %copy-done.8), channel_id=1, source_target_pairs={{0,4},{4,0},{8,12},{12,8},{1,5},{5,1},{9,13},{13,9},{2,6},{6,2},{1... | collective-permute-start | bytes 589832 | tf_op jit(solution)/shard_map/ppermute | solution.py:300
  72.5 1.5 %collective-permute-start.4 = (bf16[192,512]{1,0:T(8,128)(2,1)S(1)}, bf16[192,512]{1,0:T(8,128)(2,1)S(1)}, u32[]{:S(2)}, u32[]{:S(2)}) collective-permute-start(bf16[192,512]{1,0:T(8,128)(2,1)S(1)} %copy-done.7), channel_id=1, source_target_pairs={{0,8},{4,12},{8,0},{12,4},{1,9},{5,13},{9,1},{13,5},{2,10},{6,14},... | collective-permute-start | bytes 589832 | tf_op jit(solution)/shard_map/ppermute | solution.py:300
  74.4 5.1 %pair_grad.1 = bf16[2,64,64,128]{3,2,1,0:T(8,128)(2,1)} custom-call(bf16[32,64,128]{2,1,0:T(8,128)(2,1)} %copy-done, bf16[32,64,128]{2,1,0:T(8,128)(2,1)} %norm.1.bias_ref, f32[64,128]{1,0:T(8,128)} %get-tuple-element.34.inv_ref, f32[1,128]{1,0:T(1,128)} %bitcast.21, bf16[16,128]{1,0:T(8,128)(2,1)} %bitcast.17, ...), custom_call_target="tpu_custom_call" | custom-call | flops 134217728 | bytes 4194304 | tf_op jit(solution)/shard_map/pair_grad/pallas_call | solution.py:370
  79.6 1.3 %collective-permute-done.4.refs_2_ = bf16[192,512]{1,0:T(8,128)(2,1)S(1)} collective-permute-done((bf16[192,512]{1,0:T(8,128)(2,1)S(1)}, bf16[192,512]{1,0:T(8,128)(2,1)S(1)}, u32[]{:S(2)}, u32[]{:S(2)}) %collective-permute-start.4) | collective-permute-done | bytes 196640 | tf_op jit(solution)/shard_map/ppermute | solution.py:300
  80.9 4.1 %collective-permute-done.5.refs_3_ = bf16[192,512]{1,0:T(8,128)(2,1)S(1)} collective-permute-done((bf16[192,512]{1,0:T(8,128)(2,1)S(1)}, bf16[192,512]{1,0:T(8,128)(2,1)S(1)}, u32[]{:S(2)}, u32[]{:S(2)}) %collective-permute-start.5) | collective-permute-done | bytes 196640 | tf_op jit(solution)/shard_map/ppermute | solution.py:300
  85.0 0.7 copy-done.5
  85.7 2.1 %unpack.1 = (bf16[1,192,512]{2,1,0:T(8,128)(2,1)}, bf16[1,192,512]{2,1,0:T(8,128)(2,1)}, bf16[1,192,512]{2,1,0:T(8,128)(2,1)}, bf16[1,192,512]{2,1,0:T(8,128)(2,1)}) custom-call(s32[1]{0:T(128)} %bitcast.mate_ref, bf16[192,512]{1,0:T(8,128)(2,1)} %get-tuple-element.40.refs_0_, bf16[192,512]{1,0:T(8,128)(2,1)} %copy-done.3, bf16[192,512]{1,0:T(8,128)(2,1)} %copy-done.4, ...), custom_call_target="tpu_custom_call" | custom-call | bytes 1572864 | tf_op jit(solution)/shard_map/unpack/pallas_call | solution.py:379
  87.8 0.7 copy-done.2
  88.5 1.6 %final.1 = (f32[16,128]{1,0:T(8,128)}, f32[1,128]{1,0:T(1,128)}) custom-call(bf16[32,16,128]{2,1,0:T(8,128)(2,1)} %copy-done.2, f32[1,128]{1,0:T(1,128)} %bitcast.22, bf16[16,128]{1,0:T(8,128)(2,1)} %bitcast.18), custom_call_target="tpu_custom_call" | custom-call | bytes 131072 | tf_op jit(solution)/shard_map/final/pallas_call | solution.py:384
  (26 shorter events, 1.6 us)
Async XLA Ops:
  6.6 27.9 %all-to-all-start = ((bf16[32,64,128]{2,1,0:T(8,128)(2,1)}), bf16[32,64,128]{2,1,0:T(8,128)(2,1)S(1)}, u32[]{:S(2)}, u32[]{:S(2)}) async-start(bf16[32,64,128]{2,1,0:T(8,128)(2,1)} %norm.1.bias_ref), calls=%async_computation | async-start | bytes 1048576 | tf_op jit(solution)/shard_map/all_to_all | solution.py:319
  16.4 9.8 %collective-permute-start = (bf16[192,512]{1,0:T(8,128)(2,1)}, bf16[192,512]{1,0:T(8,128)(2,1)S(1)}, u32[]{:S(2)}, u32[]{:S(2)}) collective-permute-start(bf16[192,512]{1,0:T(8,128)(2,1)} %get-tuple-element.30), channel_id=1, source_target_pairs={{0,4},{4,0},{8,12},{12,8},{1,5},{5,1},{9,13},{13,9},{2,6},{6,2},{1... | collective-permute-start | bytes 589832 | tf_op jit(solution)/shard_map/ppermute | solution.py:300
  18.2 11.6 %collective-permute-start.1 = (bf16[192,512]{1,0:T(8,128)(2,1)}, bf16[192,512]{1,0:T(8,128)(2,1)S(1)}, u32[]{:S(2)}, u32[]{:S(2)}) collective-permute-start(bf16[192,512]{1,0:T(8,128)(2,1)} %get-tuple-element.31), channel_id=1, source_target_pairs={{0,8},{4,12},{8,0},{12,4},{1,9},{5,13},{9,1},{13,5},{2,10},{6,14},... | collective-permute-start | bytes 589832 | tf_op jit(solution)/shard_map/ppermute | solution.py:300
  19.7 14.9 %collective-permute-start.2 = (bf16[192,512]{1,0:T(8,128)(2,1)}, bf16[192,512]{1,0:T(8,128)(2,1)S(1)}, u32[]{:S(2)}, u32[]{:S(2)}) collective-permute-start(bf16[192,512]{1,0:T(8,128)(2,1)} %get-tuple-element.32), channel_id=1, source_target_pairs={{0,12},{4,8},{8,4},{12,0},{1,13},{5,9},{9,5},{13,1},{2,14},{6,10},... | collective-permute-start | bytes 589832 | tf_op jit(solution)/shard_map/ppermute | solution.py:300
  26.2 8.3 %copy-start.9 = (bf16[192,512]{1,0:T(8,128)(2,1)}, bf16[192,512]{1,0:T(8,128)(2,1)S(1)}, u32[]{:S(2)}) copy-start(bf16[192,512]{1,0:T(8,128)(2,1)S(1)} %collective-permute-done.refs_1_) | copy-start | bytes 589828
  29.8 4.8 %copy-start.10 = (bf16[192,512]{1,0:T(8,128)(2,1)}, bf16[192,512]{1,0:T(8,128)(2,1)S(1)}, u32[]{:S(2)}) copy-start(bf16[192,512]{1,0:T(8,128)(2,1)S(1)} %collective-permute-done.1.refs_2_) | copy-start | bytes 589828
  34.5 0.7 copy-start.11
  34.6 0.9 copy-start.1
  43.4 19.3 %all-to-all-start.1 = ((bf16[32,64,128]{2,1,0:T(8,128)(2,1)}), bf16[32,64,128]{2,1,0:T(8,128)(2,1)S(1)}, u32[]{:S(2)}, u32[]{:S(2)}) async-start(bf16[32,64,128]{2,1,0:T(8,128)(2,1)} %bitcast.15), calls=%async_computation.1 | async-start | bytes 1048576 | tf_op jit(solution)/shard_map/all_to_all | solution.py:358
  47.1 23.7 %copy-start.8 = (bf16[192,512]{1,0:T(8,128)(2,1)S(1)}, bf16[192,512]{1,0:T(8,128)(2,1)}, u32[]{:S(2)}) copy-start(bf16[192,512]{1,0:T(8,128)(2,1)} %get-tuple-element.37) | copy-start | bytes 589828
  47.2 25.4 %copy-start.7 = (bf16[192,512]{1,0:T(8,128)(2,1)S(1)}, bf16[192,512]{1,0:T(8,128)(2,1)}, u32[]{:S(2)}) copy-start(bf16[192,512]{1,0:T(8,128)(2,1)} %get-tuple-element.38) | copy-start | bytes 589828
  47.2 26.8 %copy-start.6 = (bf16[192,512]{1,0:T(8,128)(2,1)S(1)}, bf16[192,512]{1,0:T(8,128)(2,1)}, u32[]{:S(2)}) copy-start(bf16[192,512]{1,0:T(8,128)(2,1)} %get-tuple-element.39) | copy-start | bytes 589828
  62.7 0.8 copy-start
  67.6 20.2 %all-to-all-start.2 = ((bf16[32,16,128]{2,1,0:T(8,128)(2,1)}), bf16[32,16,128]{2,1,0:T(8,128)(2,1)S(1)}, u32[]{:S(2)}, u32[]{:S(2)}) async-start(bf16[32,16,128]{2,1,0:T(8,128)(2,1)} %reduce.1), calls=%async_computation.2 | async-start | bytes 262144 | tf_op jit(solution)/shard_map/all_to_all | solution.py:368
  70.9 8.7 %collective-permute-start.3 = (bf16[192,512]{1,0:T(8,128)(2,1)S(1)}, bf16[192,512]{1,0:T(8,128)(2,1)S(1)}, u32[]{:S(2)}, u32[]{:S(2)}) collective-permute-start(bf16[192,512]{1,0:T(8,128)(2,1)S(1)} %copy-done.8), channel_id=1, source_target_pairs={{0,4},{4,0},{8,12},{12,8},{1,5},{5,1},{9,13},{13,9},{2,6},{6,2},{1... | collective-permute-start | bytes 589832 | tf_op jit(solution)/shard_map/ppermute | solution.py:300
  72.5 8.3 %collective-permute-start.4 = (bf16[192,512]{1,0:T(8,128)(2,1)S(1)}, bf16[192,512]{1,0:T(8,128)(2,1)S(1)}, u32[]{:S(2)}, u32[]{:S(2)}) collective-permute-start(bf16[192,512]{1,0:T(8,128)(2,1)S(1)} %copy-done.7), channel_id=1, source_target_pairs={{0,8},{4,12},{8,0},{12,4},{1,9},{5,13},{9,1},{13,5},{2,10},{6,14},... | collective-permute-start | bytes 589832 | tf_op jit(solution)/shard_map/ppermute | solution.py:300
  74.0 11.0 %collective-permute-start.5 = (bf16[192,512]{1,0:T(8,128)(2,1)S(1)}, bf16[192,512]{1,0:T(8,128)(2,1)S(1)}, u32[]{:S(2)}, u32[]{:S(2)}) collective-permute-start(bf16[192,512]{1,0:T(8,128)(2,1)S(1)} %copy-done.6), channel_id=1, source_target_pairs={{0,12},{4,8},{8,4},{12,0},{1,13},{5,9},{9,5},{13,1},{2,14},{6,10},... | collective-permute-start | bytes 589832 | tf_op jit(solution)/shard_map/ppermute | solution.py:300
  79.6 5.4 %copy-start.3 = (bf16[192,512]{1,0:T(8,128)(2,1)}, bf16[192,512]{1,0:T(8,128)(2,1)S(1)}, u32[]{:S(2)}) copy-start(bf16[192,512]{1,0:T(8,128)(2,1)S(1)} %collective-permute-done.3.refs_1_) | copy-start | bytes 589828
  80.9 4.1 %copy-start.4 = (bf16[192,512]{1,0:T(8,128)(2,1)}, bf16[192,512]{1,0:T(8,128)(2,1)S(1)}, u32[]{:S(2)}) copy-start(bf16[192,512]{1,0:T(8,128)(2,1)S(1)} %collective-permute-done.4.refs_2_) | copy-start | bytes 589828
  85.0 0.7 copy-start.5
  87.8 0.7 copy-start.2

commit v3 on v2

v3 whole, which is shorter than its diff:
```python
import functools
import math

import jax
import jax.numpy as jnp
from jax import lax
from jax.experimental import pallas as pl
from jax.experimental.pallas import tpu as pltpu
from jax.sharding import Mesh
from jax.sharding import PartitionSpec as P

F32 = jnp.float32
BF16 = jnp.bfloat16
LOG2E = math.log2(math.e)
EPS = 1e-05
MASKED = -1000000000.0
BIG = 60
SMALL = 24
SPLIT = 1
ORDER = (0, 2, 1, 3)
FIRST = (2,)
EARLY = (1, 3)
NT = (((1,), (1,)), ((), ()))
TN = (((0,), (0,)), ((), ()))


def dot(a, b, dims=(((1,), (0,)), ((), ()))):
    return lax.dot_general(a, b, dims, preferred_element_type=F32)


def call(kernel, name, flops, moved, mebi, **kw):
    return pl.pallas_call(
        kernel,
        name=name,
        compiler_params=pltpu.CompilerParams(vmem_limit_bytes=mebi * 1024 * 1024),
        cost_estimate=pl.CostEstimate(flops=flops, bytes_accessed=moved, transcendentals=0),
        **kw,
    )


def together(value, chunks, some):
    some = [k for k in some if k < len(chunks)]
    if not some:
        return value, chunks
    value, taken = lax.optimization_barrier((value, [chunks[k] for k in some]))
    return value, [taken[some.index(k)] if k in some else x for k, x in enumerate(chunks)]


def step_of(count, most):
    return max(n for n in range(1, most + 1) if count % n == 0)


def pack_kernel(dim, mate_ref, q_ref, k_ref, v_ref, g_ref, map_ref, mask_ref, *refs):
    *send_refs, grad_s, sems = refs
    copies = []
    for k, send_ref in enumerate(send_refs):
        part = pl.ds(pl.multiple_of(jnp.bitwise_xor(mate_ref[0], k) * dim, 16), dim)
        for n, from_ref in enumerate((q_ref, k_ref, v_ref, g_ref)):
            to_ref = grad_s.at[k] if n == 3 else send_ref.at[n * dim : (n + 1) * dim]
            copies.append(pltpu.make_async_copy(from_ref.at[0, part], to_ref, sems.at[k, n]))
    for copy in copies:
        copy.start()
    count = mask_ref.shape[1]
    atoms = map_ref.shape[1]
    rows = pl.cdiv(count, 128)
    tall = pl.cdiv(rows, 16) * 16
    token = map_ref[...]
    high = lax.shift_right_logical(token, 7)
    low = jnp.bitwise_and(token, 127)
    is_row = (lax.broadcasted_iota(jnp.int32, (tall, atoms), 0) == high).astype(F32).astype(BF16)
    is_lane = (lax.broadcasted_iota(jnp.int32, (128, atoms), 0) == low).astype(F32).astype(BF16)
    counts = dot(is_row, is_lane, NT)
    line = jnp.concatenate([counts[r : r + 1, :] for r in range(rows)], axis=1)[:, :count]
    weight = line * (count / atoms) * mask_ref[...].astype(F32)
    for copy in copies:
        copy.wait()
    for k, send_ref in enumerate(send_refs):
        send_ref[3 * dim : 4 * dim, :] = (grad_s[k].astype(F32) * weight).astype(BF16)


def unpack_kernel(mates, dim, mate_ref, *refs):
    for k in range(mates):
        part = pl.ds(pl.multiple_of(jnp.bitwise_xor(mate_ref[0], k) * dim, 16), dim)
        for n, out_ref in enumerate(refs[mates:]):
            out_ref[0, part, :] = refs[k][n * dim : (n + 1) * dim, :]


def copies_of(near_ref, far_ref, sems, block):
    return [
        pltpu.make_async_copy(near_ref.at[:, pl.ds(p, block)], far_ref.at[:, pl.ds(p, block)], sems.at[n])
        for n, p in enumerate(range(0, near_ref.shape[1], block))
    ]


def centred(pair):
    halves, block, cols, chan = pair.shape
    rows = pair.reshape(halves * block * cols, chan)
    return rows.astype(F32) - dot(rows, jnp.full((chan, chan), 1.0, BF16)) * (1.0 / chan)


def pieces(values, halves, block, cols):
    many = 2 if block % 2 == 0 else 1
    for p in range(0, block, many):
        starts = [(h * block + p + n) * cols for n in range(many) for h in range(halves)]
        yield p, many, jnp.concatenate([values[x : x + cols] for x in starts], axis=0)


def from_halves(block, cols):
    turned = block.T
    return jnp.concatenate([turned[:cols], turned[cols:]], axis=1)


def to_halves(block):
    half = block.shape[1] // 2
    return jnp.concatenate([block[:, :half], block[:, half:]], axis=0).T


def norm_kernel(groups, mates, block, pair_ref, gain_ref, proj_ref, send_ref, bias_s):
    halves, half, cols, chan = pair_ref.shape
    heads = proj_ref.shape[0]
    for first in range(0, half, block):
        cent = centred(pair_ref[:, first : first + block])
        inv_std = lax.rsqrt(jnp.mean(cent * cent, axis=-1, keepdims=True) + EPS)
        lnout = (cent * inv_std * gain_ref[...]).astype(BF16)
        for p, many, piece in pieces(lnout, halves, block, cols):
            bias = dot(proj_ref[...], piece, NT)
            for n in range(many):
                bias_s[pl.ds(first + p + n, heads, stride=half), :] = bias[
                    :, n * halves * cols : (n + 1) * halves * cols
                ]
    pairs = 2 if heads % 2 == 0 else 1
    for h in range(0, heads, pairs):
        turned = bias_s[h * half : (h + pairs) * half, :].T.astype(BF16)
        for n in range(pairs):
            part = slice(n * half, (n + 1) * half)
            tile = jnp.concatenate([turned[:cols, part], turned[cols:, part]], axis=1)
            for g in range(groups):
                send_ref[g * heads + place(mates, heads, h + n)] = tile


def prepare_kernel(block, pair_ref, inv_ref, var_s):
    halves, half, cols, chan = pair_ref.shape
    ones = jnp.full((16, chan), 1.0, BF16)
    for start in range(0, half, block):
        part = slice(start, start + block)
        cent = centred(pair_ref[:, part])
        for p, many, piece in pieces((cent * cent).astype(BF16), halves, block, cols):
            var = dot(ones, piece, NT)[:1] * (1.0 / chan)
            for n in range(many):
                var_s[pl.ds(start + p + n, 1), :] = var[:, n * halves * cols : (n + 1) * halves * cols]
    inv_ref[...] = lax.rsqrt(from_halves(var_s[...], cols) + EPS)


def attend_kernel(samples, wide, last, *refs):
    got_refs, refs = refs[:samples], refs[samples:]
    bias_ref, mask_ref, refs = refs[0], refs[1], refs[2:]
    before_ref, refs = (None, refs) if len(refs) == samples + 5 else (refs[0], refs[1:])
    back_refs, refs = refs[:samples], refs[samples:]
    grad_ref, key_s, value_s, dk_s, dv_s = refs
    four, count = got_refs[0].shape
    dim = four // 4
    root = 1.0 / math.sqrt(dim)
    samp, heads, cols, rows = bias_ref.shape
    first = lax.broadcasted_iota(jnp.int32, (16, count), 0) == 0
    mask_rows = jnp.where(first & (mask_ref[...] <= 0), MASKED, 0.0).astype(BF16)
    one_rows = jnp.where(lax.broadcasted_iota(jnp.int32, (16, wide), 0) == 0, 1.0, 0.0).astype(BF16)
    for s, got_ref in enumerate(got_refs):
        keys = got_ref[dim : 2 * dim, :]
        key_s[s] = jnp.concatenate([keys, keys, mask_rows], axis=0).T
        value_s[s] = got_ref[2 * dim : 3 * dim, :].T
    per = wide // rows
    for a in range(count // wide):
        lanes = slice(a * wide, (a + 1) * wide)
        bias = jnp.concatenate(
            [bias_ref[:, a * per + p].reshape(count, rows) for p in range(per)], axis=1
        ).astype(F32) * LOG2E
        total = None if before_ref is None else before_ref[:, lanes]
        for s, (got_ref, back_ref) in enumerate(zip(got_refs, back_refs)):
            query = got_ref[0:dim, lanes]
            scaled = query.astype(F32) * (LOG2E * root)
            upper = scaled.astype(BF16)
            lower = (scaled - upper.astype(F32)).astype(BF16)
            scores = dot(key_s[s], jnp.concatenate([upper, lower, one_rows], axis=0)) + bias
            expo = jnp.exp2(scores - jnp.max(scores, axis=0, keepdims=True))
            inv_sum = 1.0 / jnp.sum(expo, axis=0, keepdims=True)
            expo_b = expo.astype(BF16)
            out = dot(got_ref[2 * dim : 3 * dim, :], expo_b) * inv_sum
            back_ref[0:dim, lanes] = out.astype(BF16)
            grad = (got_ref[3 * dim : 4 * dim, lanes].astype(F32) * inv_sum).astype(BF16)
            row_dot = jnp.sum(grad.astype(F32) * out, axis=0, keepdims=True)
            dscore = expo * (dot(value_s[s], grad) - row_dot)
            total = dscore if total is None else total + dscore
            dscore_b = dscore.astype(BF16)
            back_ref[dim : 2 * dim, lanes] = (dot(got_ref[dim : 2 * dim, :], dscore_b) * root).astype(BF16)
            dk = dot(query, dscore_b, NT)
            dv = dot(grad, expo_b, NT)
            if a == 0:
                dk_s[s] = dk
                dv_s[s] = dv
            else:
                dk_s[s] += dk
                dv_s[s] += dv
        if not last:
            grad_ref[:, lanes] = total
            continue
        total = total.astype(BF16)
        for p in range(per):
            grad_ref[:, a * per + p] = total[:, p * rows : (p + 1) * rows].reshape(samp, cols, rows)
    for s, back_ref in enumerate(back_refs):
        back_ref[2 * dim : 3 * dim, :] = (dk_s[s] * root).astype(BF16)
        back_ref[3 * dim : 4 * dim, :] = dv_s[s].astype(BF16)


def reduce_kernel(groups, mates, got_ref, inv_ref, pair_ref, sum_ref, plain_s):
    halves, half, cols, chan = pair_ref.shape
    devices, heads, _ = sum_ref.shape
    for h in range(heads):
        plain = gathered(groups, mates, heads, h, got_ref) * inv_ref[...]
        plain_s[h * half : (h + 1) * half, :] = to_halves(plain)
    total = jnp.zeros((heads, chan), F32)
    for p in range(half):
        plain = plain_s[pl.ds(p, heads, stride=half), :].astype(BF16)
        total += dot(plain, jnp.concatenate([pair_ref[h, p] for h in range(halves)], axis=0))
    total = (total - jnp.mean(total, axis=1, keepdims=True)).astype(BF16)
    for n in range(devices):
        sum_ref[n] = total


def place(mates, heads, h):
    return (h % mates) * (heads // mates) + h // mates


def gathered(groups, mates, heads, h, got_ref):
    at = place(mates, heads, h)
    grad = got_ref[at].astype(F32)
    for g in range(1, groups):
        grad += got_ref[g * heads + at].astype(F32)
    return grad


def pair_kernel(
    groups, mates, block, got_ref, bias_ref, inv_ref, gain_ref, proj_ref, pair_ref, out_ref,
    out_s, sems, plain_s, biased_s,
):
    halves, half, cols, chan = pair_ref.shape
    heads = proj_ref.shape[0]
    outs = copies_of(out_s, out_ref, sems, block)
    scaled = proj_ref[...].astype(F32) * gain_ref[...]
    scaled = (scaled - jnp.mean(scaled, axis=1, keepdims=True)).astype(BF16)
    none = jnp.zeros((heads, chan), BF16)
    ones = jnp.ones((heads, chan), BF16)
    right = jnp.concatenate(
        [jnp.concatenate([scaled, none], axis=1), jnp.concatenate([none, ones], axis=1)], axis=0
    )
    inv_std = inv_ref[...]
    for h in range(heads):
        plain = gathered(groups, mates, heads, h, got_ref) * inv_std
        biased = plain * inv_std * bias_ref[place(mates, heads, h)].astype(F32) * (1.0 / chan)
        plain_s[h * half : (h + 1) * half, :] = to_halves(plain)
        biased_s[h * half : (h + 1) * half, :] = to_halves(biased)
    for step, copy in enumerate(outs):
        first = step * block
        cent = centred(pair_ref[:, first : first + block]).reshape(halves, block, cols, chan)
        for p in range(first, first + block):
            take = pl.ds(p, heads, stride=half)
            left = jnp.concatenate([plain_s[take, :], biased_s[take, :]], axis=0).astype(BF16)
            both = dot(left, right, TN)
            for h in range(halves):
                part = slice(h * cols, (h + 1) * cols)
                out_s[h, p] = (both[part, :chan] - cent[h, p - first] * both[part, chan:]).astype(BF16)
        copy.start()
    for copy in outs:
        copy.wait()


def final_kernel(scale, sums_ref, gain_ref, proj_ref, weight_ref, gain_grad_ref):
    total = sums_ref[0].astype(F32)
    for n in range(1, sums_ref.shape[0]):
        total += sums_ref[n].astype(F32)
    total = total * scale
    weight_ref[...] = total * gain_ref[...]
    gain_grad_ref[...] = jnp.sum(total * proj_ref[...].astype(F32), axis=0, keepdims=True)


def local(groups, mates, axes, queries, keys, values, out_grad, pair, ln_gain, proj_weight, token_mask, atom_map):
    _, width, count = queries.shape
    rows, cols, chan = pair.shape
    heads = proj_weight.shape[1]
    dim = width // mates
    head_parts = heads // mates
    devices = groups * mates * head_parts
    entries = rows * cols
    half = rows // 2
    gain_row = ln_gain.reshape(1, chan)
    proj_rows = proj_weight.T
    mask_row = token_mask.reshape(1, count)
    pair = pair.reshape(2, half, cols, chan)
    mate = lax.axis_index(axes[1]).astype(jnp.int32).reshape(1)
    whole = lambda *shape: pl.BlockSpec(shape, lambda *_: (0,) * len(shape))
    scalar = pl.BlockSpec(memory_space=pltpu.SMEM)
    vector = pl.BlockSpec(memory_space=pltpu.VMEM)

    def swap(chunks):
        return [
            lax.ppermute(x, axes[1], [(i, i ^ k) for i in range(mates)]) if k else x
            for k, x in enumerate(chunks)
        ]

    block = step_of(half, 16)
    far = pl.BlockSpec(memory_space=pltpu.HBM)
    tiles = jax.ShapeDtypeStruct((devices, cols, rows), BF16)
    by_head = pltpu.VMEM((heads * half, 2 * cols), F32)
    near = pltpu.VMEM(pair.shape, BF16)
    sems = pltpu.SemaphoreType.DMA((half // block,))

    chunks = (jax.ShapeDtypeStruct((4 * dim, count), BF16),) * mates
    send = call(
        functools.partial(pack_kernel, dim), "pack", 2 * 16 * 128 * atom_map.shape[0],
        16 * width * count, SMALL, out_shape=chunks,
        in_specs=[scalar] + [far] * 4 + [vector] * 2,
        out_specs=(vector,) * mates,
        scratch_shapes=[pltpu.VMEM((mates, dim, count), BF16), pltpu.SemaphoreType.DMA((mates, 4))],
    )(mate, queries, keys, values, out_grad, atom_map.reshape(1, -1), mask_row)
    got = swap(send)

    bias_send = call(
        functools.partial(norm_kernel, groups, mates, block), "norm", 2 * entries * chan * heads,
        2 * entries * chan, BIG,
        out_shape=tiles,
        in_specs=[vector] * 3,
        out_specs=vector,
        scratch_shapes=[by_head],
    )(pair, gain_row, proj_rows)
    bias = lax.all_to_all(bias_send, axes, 0, 0, tiled=True)

    inv_std = call(
        functools.partial(prepare_kernel, block), "prepare", 2 * entries * chan * heads, 2 * entries * chan, SMALL,
        out_shape=jax.ShapeDtypeStruct((cols, rows), F32),
        in_specs=[vector],
        out_specs=vector,
        scratch_shapes=[pltpu.VMEM((half, 2 * cols), F32)],
    )(pair)

    fine = rows % 128 == 0
    samp = groups * mates
    bias = bias.reshape(samp, head_parts, cols, rows)
    if not fine:
        bias = bias.transpose(0, 2, 1, 3).reshape(1, 1, count, count)
    wide = max(rows, step_of(count, 256)) if fine else count
    order = sorted(range(mates), key=lambda k: ORDER.index(k) if k in ORDER else k)
    back, before = [None] * mates, ()
    for n in range(0, mates, SPLIT):
        part = order[n : n + SPLIT]
        many, last = len(part), n + SPLIT >= mates
        *outs, grads = call(
            functools.partial(attend_kernel, many, wide, last), "attend", 12 * many * dim * count * count,
            8 * many * dim * count * 2 + 4 * count * count, SMALL,
            out_shape=chunks[:many]
            + (jax.ShapeDtypeStruct(bias.shape, BF16) if last else jax.ShapeDtypeStruct((count, count), F32),),
            scratch_shapes=[
                pltpu.VMEM((many, count, 2 * dim + 16), BF16),
                pltpu.VMEM((many, count, dim), BF16),
                pltpu.VMEM((many, dim, count), F32),
                pltpu.VMEM((many, dim, count), F32),
            ],
        )(*[got[k] for k in part], bias, mask_row, *before)
        before = (grads,)
        for k, x in zip(part, outs):
            back[k] = x
    if not fine:
        grads = grads.reshape(samp, cols, head_parts, rows).transpose(0, 2, 1, 3)
    swapped = swap(back)
    grads, swapped = together(grads, swapped, FIRST)
    grads = lax.all_to_all(grads.reshape(devices, cols, rows), axes, 0, 0, tiled=True)
    parts = call(
        functools.partial(reduce_kernel, groups, mates), "reduce", 2 * entries * chan * heads,
        2 * entries * chan, SMALL,
        out_shape=jax.ShapeDtypeStruct((devices, heads, chan), BF16),
        in_specs=[vector] * 3,
        out_specs=vector,
        scratch_shapes=[by_head],
    )(grads, inv_std, pair)
    parts, swapped = together(parts, swapped, EARLY)
    sums = lax.all_to_all(parts, axes, 0, 0, tiled=True)

    pair_grad = call(
        functools.partial(pair_kernel, groups, mates, block), "pair_grad", 8 * entries * chan * heads,
        4 * entries * chan, SMALL,
        out_shape=jax.ShapeDtypeStruct(pair.shape, BF16),
        in_specs=[vector] * 6,
        out_specs=far,
        scratch_shapes=[near, sems, by_head, by_head],
    )(grads, bias_send, inv_std, gain_row, proj_rows, pair)
    pair_grad, swapped = lax.optimization_barrier((pair_grad, swapped))
    attended, query_grad, key_grad, value_grad = call(
        functools.partial(unpack_kernel, mates, dim), "unpack", 0, 16 * width * count, SMALL,
        out_shape=(jax.ShapeDtypeStruct(queries.shape, BF16),) * 4,
        in_specs=[scalar] + [vector] * mates,
    )(mate, *swapped)
    weight_rows, gain_grad = call(
        functools.partial(final_kernel, 1.0 / count), "final", 0, 2 * devices * heads * chan, SMALL,
        out_shape=(
            jax.ShapeDtypeStruct((heads, chan), F32),
            jax.ShapeDtypeStruct((1, chan), F32),
        ),
    )(sums, gain_row, proj_rows)
    return (
        attended, query_grad, key_grad, value_grad,
        pair_grad.reshape(rows, cols, chan), weight_rows.T, gain_grad.reshape(chan),
    )


def solution(mesh):
    samp, head = mesh.axis_names
    samp_size, head_size = mesh.shape[samp], mesh.shape[head]

    def run(*args):
        heads = args[6].shape[1]
        mates = math.gcd(heads // head_size, samp_size)
        groups = samp_size // mates
        axes = ("group", "mate", "part")
        fine = Mesh(mesh.devices.reshape(groups, mates, head_size), axes)
        by_sample = P(("group", "mate"), "part", None)
        by_pair = P("part", ("group", "mate"), None)
        return jax.shard_map(
            functools.partial(local, groups, mates, axes),
            mesh=fine,
            in_specs=(by_sample,) * 4 + (by_pair,) + (P(),) * 4,
            out_specs=(by_sample,) * 4 + (by_pair, P(), P()),
            check_vma=False,
        )(*args)

    return run
```

time: 90.6 us -> 72.1 us (0.80)
  Pallas kernels: 33.7 us -> 24.5 us
  waiting for transfers between devices: 31.2 us -> 23.7 us
  local copies, waits for them, and re-layouts: 3.01 us -> 0.05 us
  starting transfers between devices: 21.3 us -> 22.6 us
    ppermute x6, waiting for transfers between devices: 20 us -> 1.38 us  [swap(): lax.ppermute(x, axes[1], [(i, i ^ k) for i in range(mates)])]
    all_to_all x1, waiting for transfers between devices: 0.01 us -> 9.59 us  [local(): bias = lax.all_to_all(bias_send, axes, 0, 0, tiled=True)]
    unnamed x24 -> x26, local copies, waits for them, and re-layouts: 3.01 us -> 0.05 us
    pallas_call x2 -> x5, Pallas kernels: 12.1 us -> 9.32 us  [the longest x4 7.4 us: local(): call(functools.partial(attend_kernel, many, wide, last), 'attend', 12 * m...]
    pallas_call x1, Pallas kernels: 4.36 us -> 1.65 us  [local(): call(functools.partial(prepare_kernel, block), 'prepare', 2 * entries * c...]
    all_to_all x1, waiting for transfers between devices: 0.01 us -> 2.13 us  [local(): sums = lax.all_to_all(parts, axes, 0, 0, tiled=True)]
    pallas_call x1, Pallas kernels: 5.98 us -> 4.72 us  [local(): call(functools.partial(norm_kernel, groups, mates, block), 'norm', 2 * en...]
    ppermute x6, starting transfers between devices: 7.04 us -> 8.24 us  [swap(): lax.ppermute(x, axes[1], [(i, i ^ k) for i in range(mates)])]
  transfers between devices with their start and end apart: 9 -> 9, of which waited for: 6 -> 4; matrix products, arithmetic and copies ran while one was open for 0% -> 0% of each run, Pallas kernels for 16% -> 27%
where the time goes in v3:
time: 72.1 us; the launch traced here: 71.7 us
  Pallas kernels  24.5 us (34%)
  waiting for transfers between devices  23.7 us (33%)
  starting transfers between devices  22.6 us (31%)
  between operations  0.86 us (1%)
    all_to_all x1, waiting for transfers between devices, local(): lax.all_to_all(grads.reshape(devices, cols, rows), axes, 0, 0, tiled=True)  10.6 us
    all_to_all x1, waiting for transfers between devices, local(): bias = lax.all_to_all(bias_send, axes, 0, 0, tiled=True)  9.59 us
    ppermute x6, starting transfers between devices, swap(): lax.ppermute(x, axes[1], [(i, i ^ k) for i in range(mates)])  8.24 us
    pallas_call x4, Pallas kernels, local(): call(functools.partial(attend_kernel, many, wide, last), 'attend', 12 * m...  7.4 us
    all_to_all x1, starting transfers between devices, local(): bias = lax.all_to_all(bias_send, axes, 0, 0, tiled=True)  7.3 us
    pallas_call x1, Pallas kernels, local(): call(functools.partial(norm_kernel, groups, mates, block), 'norm', 2 * en...  4.72 us
    all_to_all x1, starting transfers between devices, local(): sums = lax.all_to_all(parts, axes, 0, 0, tiled=True)  4.15 us
    pallas_call x1, Pallas kernels, local(): call(functools.partial(pair_kernel, groups, mates, block), 'pair_grad', 8...  3.92 us
  transfers between devices with their start and end apart: 9, of which 4 were waited for; matrix products, arithmetic and copies ran while one was open for 0% of the time, Pallas kernels for 27%

profile of v3, /device:TPU:0, one launch (start us, length us, event | category | flops | bytes accessed | tf_op | source)
XLA Modules:
  0.0 71.7 jit_solution(7898243955186637988)
XLA Ops:
  0.7 4.7 %norm.1.bias_ref = bf16[32,64,128]{2,1,0:T(8,128)(2,1)} custom-call(bf16[2,64,64,128]{3,2,1,0:T(8,128)(2,1)} %bitcast.11, f32[1,128]{1,0:T(1,128)} %bitcast.28, bf16[16,128]{1,0:T(8,128)(2,1)} %bitcast.24), custom_call_target="tpu_custom_call" | custom-call | flops 33554432 | bytes 2097152 | tf_op jit(solution)/shard_map/norm/pallas_call | solution.py:326
  5.4 7.3 %all-to-all-start = ((bf16[32,64,128]{2,1,0:T(8,128)(2,1)}), bf16[32,64,128]{2,1,0:T(8,128)(2,1)S(1)}, u32[]{:S(2)}, u32[]{:S(2)}) async-start(bf16[32,64,128]{2,1,0:T(8,128)(2,1)} %norm.1.bias_ref), calls=%async_computation | async-start | bytes 1048576 | tf_op jit(solution)/shard_map/all_to_all | solution.py:334
  12.8 2.3 %pack.1 = (bf16[192,512]{1,0:T(8,128)(2,1)S(1)}, bf16[192,512]{1,0:T(8,128)(2,1)S(1)}, bf16[192,512]{1,0:T(8,128)(2,1)}, bf16[192,512]{1,0:T(8,128)(2,1)}) custom-call(s32[1]{0:T(128)} %bitcast.mate_ref, bf16[1,192,512]{2,1,0:T(8,128)(2,1)S(1)} %copy-done.2, bf16[1,192,512]{2,1,0:T(8,128)(2,1)S(1)} %copy-done.3, bf16[1,192,512]{2,1,0:T(8,128)(2,1)S(1)} %copy-done.4, ...), custom_call_target="tpu_custom_call" | custom-call | flops 16777216 | bytes 1572864 | tf_op jit(solution)/shard_map/pack/pallas_call | solution.py:317
  15.1 1.8 %collective-permute-start.2 = (bf16[192,512]{1,0:T(8,128)(2,1)}, bf16[192,512]{1,0:T(8,128)(2,1)S(1)}, u32[]{:S(2)}, u32[]{:S(2)}) collective-permute-start(bf16[192,512]{1,0:T(8,128)(2,1)} %get-tuple-element.37), channel_id=1, source_target_pairs={{0,8},{4,12},{8,0},{12,4},{1,9},{5,13},{9,1},{13,5},{2,10},{6,14},... | collective-permute-start | bytes 589832 | tf_op jit(solution)/shard_map/ppermute | solution.py:305
  17.0 1.5 %collective-permute-start = (bf16[192,512]{1,0:T(8,128)(2,1)}, bf16[192,512]{1,0:T(8,128)(2,1)S(1)}, u32[]{:S(2)}, u32[]{:S(2)}) collective-permute-start(bf16[192,512]{1,0:T(8,128)(2,1)} %get-tuple-element.35), channel_id=1, source_target_pairs={{0,12},{4,8},{8,4},{12,0},{1,13},{5,9},{9,5},{13,1},{2,14},{6,10},... | collective-permute-start | bytes 589832 | tf_op jit(solution)/shard_map/ppermute | solution.py:305
  18.4 0.3 collective-permute-start.1
  18.7 9.6 %all-to-all-done = bf16[32,64,128]{2,1,0:T(8,128)(2,1)S(1)} async-done(((bf16[32,64,128]{2,1,0:T(8,128)(2,1)}), bf16[32,64,128]{2,1,0:T(8,128)(2,1)S(1)}, u32[]{:S(2)}, u32[]{:S(2)}) %all-to-all-start) | async-done | bytes 524320 | tf_op jit(solution)/shard_map/all_to_all | solution.py:334
  28.3 1.7 %attend.4 = (bf16[192,512]{1,0:T(8,128)(2,1)S(1)}, f32[512,512]{1,0:T(8,128)S(1)}) custom-call(bf16[192,512]{1,0:T(8,128)(2,1)S(1)} %get-tuple-element.38.refs_0_, bf16[8,4,64,128]{3,2,1,0:T(8,128)(2,1)S(1)} %bitcast.15, s32[1,512]{1,0:T(1,128)S(1)} %bitcast.20), custom_call_target="tpu_custom_call" | custom-call | flops 150994944 | bytes 1441792 | tf_op jit(solution)/shard_map/attend/pallas_call | solution.py:355
  30.0 1.7 %attend.5 = (bf16[192,512]{1,0:T(8,128)(2,1)S(1)}, f32[512,512]{1,0:T(8,128)S(1)}) custom-call(bf16[192,512]{1,0:T(8,128)(2,1)S(1)} %collective-permute-done.2.refs_0_, bf16[8,4,64,128]{3,2,1,0:T(8,128)(2,1)S(1)} %bitcast.16, s32[1,512]{1,0:T(1,128)S(1)} %bitcast.21, f32[512,512]{1,0:T(8,128)S(1)} %get-tuple-element.39.refs_3_), custom_call_target="tpu_custom_call" | custom-call | flops 150994944 | bytes 1441792 | tf_op jit(solution)/shard_map/attend/pallas_call | solution.py:355
  31.6 1.3 %collective-permute-start.3 = (bf16[192,512]{1,0:T(8,128)(2,1)S(1)}, bf16[192,512]{1,0:T(8,128)(2,1)S(1)}, u32[]{:S(2)}, u32[]{:S(2)}) collective-permute-start(bf16[192,512]{1,0:T(8,128)(2,1)S(1)} %get-tuple-element.43), channel_id=1, source_target_pairs={{0,8},{4,12},{8,0},{12,4},{1,9},{5,13},{9,1},{13,5},{2,10},{6,14},... | collective-permute-start | bytes 589832 | tf_op jit(solution)/shard_map/ppermute | solution.py:305
  33.0 1.7 %attend.6 = (bf16[192,512]{1,0:T(8,128)(2,1)S(1)}, f32[512,512]{1,0:T(8,128)S(1)}) custom-call(bf16[192,512]{1,0:T(8,128)(2,1)S(1)} %collective-permute-done.1.refs_0_, bf16[8,4,64,128]{3,2,1,0:T(8,128)(2,1)S(1)} %bitcast.17, s32[1,512]{1,0:T(1,128)S(1)} %bitcast.22, f32[512,512]{1,0:T(8,128)S(1)} %get-tuple-element.40.refs_3_), custom_call_target="tpu_custom_call" | custom-call | flops 150994944 | bytes 1441792 | tf_op jit(solution)/shard_map/attend/pallas_call | solution.py:355
  34.7 2.4 %attend.7 = (bf16[192,512]{1,0:T(8,128)(2,1)}, bf16[8,4,64,128]{3,2,1,0:T(8,128)(2,1)}) custom-call(bf16[192,512]{1,0:T(8,128)(2,1)S(1)} %collective-permute-done.refs_0_, bf16[8,4,64,128]{3,2,1,0:T(8,128)(2,1)S(1)} %bitcast.18, s32[1,512]{1,0:T(1,128)S(1)} %bitcast.23, f32[512,512]{1,0:T(8,128)S(1)} %get-tuple-element.41.refs_3_), custom_call_target="tpu_custom_call" | custom-call | flops 150994944 | bytes 1441792 | tf_op jit(solution)/shard_map/attend/pallas_call | solution.py:355
  37.0 1.4 %collective-permute-done.3.refs_2_ = bf16[192,512]{1,0:T(8,128)(2,1)S(1)} collective-permute-done((bf16[192,512]{1,0:T(8,128)(2,1)S(1)}, bf16[192,512]{1,0:T(8,128)(2,1)S(1)}, u32[]{:S(2)}, u32[]{:S(2)}) %collective-permute-start.3) | collective-permute-done | bytes 196640 | tf_op jit(solution)/shard_map/ppermute | solution.py:305
  38.4 2.9 %all-to-all-start.1 = ((bf16[32,64,128]{2,1,0:T(8,128)(2,1)}), bf16[32,64,128]{2,1,0:T(8,128)(2,1)S(1)}, u32[]{:S(2)}, u32[]{:S(2)}) async-start(bf16[32,64,128]{2,1,0:T(8,128)(2,1)} %bitcast.7), calls=%async_computation.1 | async-start | bytes 1048576 | tf_op jit(solution)/shard_map/all_to_all | solution.py:374
  41.3 1.8 %collective-permute-start.4 = (bf16[192,512]{1,0:T(8,128)(2,1)}, bf16[192,512]{1,0:T(8,128)(2,1)}, u32[]{:S(2)}, u32[]{:S(2)}) collective-permute-start(bf16[192,512]{1,0:T(8,128)(2,1)} %copy-done.12), channel_id=1, source_target_pairs={{0,4},{4,0},{8,12},{12,8},{1,5},{5,1},{9,13},{13,9},{2,6},{6,2},{1... | collective-permute-start | bytes 589832 | tf_op jit(solution)/shard_map/ppermute | solution.py:305
  43.1 1.5 %collective-permute-start.5 = (bf16[192,512]{1,0:T(8,128)(2,1)}, bf16[192,512]{1,0:T(8,128)(2,1)}, u32[]{:S(2)}, u32[]{:S(2)}) collective-permute-start(bf16[192,512]{1,0:T(8,128)(2,1)} %get-tuple-element.47), channel_id=1, source_target_pairs={{0,12},{4,8},{8,4},{12,0},{1,13},{5,9},{9,5},{13,1},{2,14},{6,10},... | collective-permute-start | bytes 589832 | tf_op jit(solution)/shard_map/ppermute | solution.py:305
  44.7 1.7 %prepare.1.inv_ref = f32[64,128]{1,0:T(8,128)S(1)} custom-call(bf16[2,64,64,128]{3,2,1,0:T(8,128)(2,1)S(1)} %bitcast.12), custom_call_target="tpu_custom_call" | custom-call | flops 33554432 | bytes 2097152 | tf_op jit(solution)/shard_map/prepare/pallas_call | solution.py:336
  46.3 10.6 %all-to-all-done.1.got_ref = bf16[32,64,128]{2,1,0:T(8,128)(2,1)S(1)} async-done(((bf16[32,64,128]{2,1,0:T(8,128)(2,1)}), bf16[32,64,128]{2,1,0:T(8,128)(2,1)S(1)}, u32[]{:S(2)}, u32[]{:S(2)}) %all-to-all-start.1) | async-done | bytes 524320 | tf_op jit(solution)/shard_map/all_to_all | solution.py:374
  57.0 1.9 %reduce.1 = bf16[32,16,128]{2,1,0:T(8,128)(2,1)} custom-call(bf16[32,64,128]{2,1,0:T(8,128)(2,1)S(1)} %all-to-all-done.1.got_ref, f32[64,128]{1,0:T(8,128)S(1)} %prepare.1.inv_ref, bf16[2,64,64,128]{3,2,1,0:T(8,128)(2,1)S(1)} %bitcast.13), custom_call_target="tpu_custom_call" | custom-call | flops 33554432 | bytes 2097152 | tf_op jit(solution)/shard_map/reduce/pallas_call | solution.py:375
  58.9 4.1 %all-to-all-start.2 = ((bf16[32,16,128]{2,1,0:T(8,128)(2,1)}), bf16[32,16,128]{2,1,0:T(8,128)(2,1)S(1)}, u32[]{:S(2)}, u32[]{:S(2)}) async-start(bf16[32,16,128]{2,1,0:T(8,128)(2,1)} %reduce.1), calls=%async_computation.2 | async-start | bytes 262144 | tf_op jit(solution)/shard_map/all_to_all | solution.py:384
  63.1 3.9 %pair_grad.1 = bf16[2,64,64,128]{3,2,1,0:T(8,128)(2,1)} custom-call(bf16[32,64,128]{2,1,0:T(8,128)(2,1)S(1)} %all-to-all-done.1.got_ref, bf16[32,64,128]{2,1,0:T(8,128)(2,1)S(1)} %copy-done.1, f32[64,128]{1,0:T(8,128)S(1)} %prepare.1.inv_ref, f32[1,128]{1,0:T(1,128)S(1)} %bitcast.29, bf16[16,128]{1,0:T(8,128)(2,1)S(1)} %bitcast.25, ...), custom_call_target="tpu_custom_call" | custom-call | flops 134217728 | bytes 4194304 | tf_op jit(solution)/shard_map/pair_grad/pallas_call | solution.py:386
  67.0 1.9 %unpack.1 = (bf16[1,192,512]{2,1,0:T(8,128)(2,1)}, bf16[1,192,512]{2,1,0:T(8,128)(2,1)}, bf16[1,192,512]{2,1,0:T(8,128)(2,1)}, bf16[1,192,512]{2,1,0:T(8,128)(2,1)}) custom-call(s32[1]{0:T(128)} %bitcast.mate_ref, bf16[192,512]{1,0:T(8,128)(2,1)S(1)} %get-tuple-element.51.refs_0_, bf16[192,512]{1,0:T(8,128)(2,1)} %collective-permute-done.4.refs_1_, ...), custom_call_target="tpu_custom_call" | custom-call | bytes 1572864 | tf_op jit(solution)/shard_map/unpack/pallas_call | solution.py:395
  69.0 2.1 %all-to-all-done.2.sums_ref = bf16[32,16,128]{2,1,0:T(8,128)(2,1)S(1)} async-done(((bf16[32,16,128]{2,1,0:T(8,128)(2,1)}), bf16[32,16,128]{2,1,0:T(8,128)(2,1)S(1)}, u32[]{:S(2)}, u32[]{:S(2)}) %all-to-all-start.2) | async-done | bytes 131104 | tf_op jit(solution)/shard_map/all_to_all | solution.py:384
  71.1 0.6 final.1
  (31 shorter events, 0.1 us)
Async XLA Ops:
  0.6 12.1 %copy-start.2 = (bf16[1,192,512]{2,1,0:T(8,128)(2,1)S(1)}, bf16[1,192,512]{2,1,0:T(8,128)(2,1)}, u32[]{:S(2)}) copy-start(bf16[1,192,512]{2,1,0:T(8,128)(2,1)} %q_ref.1) | copy-start | bytes 589828
  0.6 12.1 %copy-start.3 = (bf16[1,192,512]{2,1,0:T(8,128)(2,1)S(1)}, bf16[1,192,512]{2,1,0:T(8,128)(2,1)}, u32[]{:S(2)}) copy-start(bf16[1,192,512]{2,1,0:T(8,128)(2,1)} %k_ref.1) | copy-start | bytes 589828
  0.7 12.1 %copy-start.4 = (bf16[1,192,512]{2,1,0:T(8,128)(2,1)S(1)}, bf16[1,192,512]{2,1,0:T(8,128)(2,1)}, u32[]{:S(2)}) copy-start(bf16[1,192,512]{2,1,0:T(8,128)(2,1)} %v_ref.1) | copy-start | bytes 589828
  0.7 12.1 %copy-start.5 = (bf16[1,192,512]{2,1,0:T(8,128)(2,1)S(1)}, bf16[1,192,512]{2,1,0:T(8,128)(2,1)}, u32[]{:S(2)}) copy-start(bf16[1,192,512]{2,1,0:T(8,128)(2,1)} %g_ref.1) | copy-start | bytes 589828
  0.7 12.1 %copy-start.10 = (s32[4096]{0:T(1024)S(1)}, s32[4096]{0:T(1024)}, u32[]{:S(2)}) copy-start(s32[4096]{0:T(1024)} %param.17) | copy-start | bytes 49156
  0.7 12.1 %copy-start.8 = (s32[512]{0:T(512)S(1)}, s32[512]{0:T(512)}, u32[]{:S(2)}) copy-start(s32[512]{0:T(512)} %param.16) | copy-start | bytes 6148
  5.4 22.9 %all-to-all-start = ((bf16[32,64,128]{2,1,0:T(8,128)(2,1)}), bf16[32,64,128]{2,1,0:T(8,128)(2,1)S(1)}, u32[]{:S(2)}, u32[]{:S(2)}) async-start(bf16[32,64,128]{2,1,0:T(8,128)(2,1)} %norm.1.bias_ref), calls=%async_computation | async-start | bytes 1048576 | tf_op jit(solution)/shard_map/all_to_all | solution.py:334
  15.1 14.8 %collective-permute-start.2 = (bf16[192,512]{1,0:T(8,128)(2,1)}, bf16[192,512]{1,0:T(8,128)(2,1)S(1)}, u32[]{:S(2)}, u32[]{:S(2)}) collective-permute-start(bf16[192,512]{1,0:T(8,128)(2,1)} %get-tuple-element.37), channel_id=1, source_target_pairs={{0,8},{4,12},{8,0},{12,4},{1,9},{5,13},{9,1},{13,5},{2,10},{6,14},... | collective-permute-start | bytes 589832 | tf_op jit(solution)/shard_map/ppermute | solution.py:305
  17.0 17.7 %collective-permute-start = (bf16[192,512]{1,0:T(8,128)(2,1)}, bf16[192,512]{1,0:T(8,128)(2,1)S(1)}, u32[]{:S(2)}, u32[]{:S(2)}) collective-permute-start(bf16[192,512]{1,0:T(8,128)(2,1)} %get-tuple-element.35), channel_id=1, source_target_pairs={{0,12},{4,8},{8,4},{12,0},{1,13},{5,9},{9,5},{13,1},{2,14},{6,10},... | collective-permute-start | bytes 589832 | tf_op jit(solution)/shard_map/ppermute | solution.py:305
  18.4 14.5 %collective-permute-start.1 = (bf16[192,512]{1,0:T(8,128)(2,1)S(1)}, bf16[192,512]{1,0:T(8,128)(2,1)S(1)}, u32[]{:S(2)}, u32[]{:S(2)}) collective-permute-start(bf16[192,512]{1,0:T(8,128)(2,1)S(1)} %get-tuple-element.36), channel_id=1, source_target_pairs={{0,4},{4,0},{8,12},{12,8},{1,5},{5,1},{9,13},{13,9},{2,6},{6,2},{1... | collective-permute-start | bytes 589832 | tf_op jit(solution)/shard_map/ppermute | solution.py:305
  31.6 6.8 %collective-permute-start.3 = (bf16[192,512]{1,0:T(8,128)(2,1)S(1)}, bf16[192,512]{1,0:T(8,128)(2,1)S(1)}, u32[]{:S(2)}, u32[]{:S(2)}) collective-permute-start(bf16[192,512]{1,0:T(8,128)(2,1)S(1)} %get-tuple-element.43), channel_id=1, source_target_pairs={{0,8},{4,12},{8,0},{12,4},{1,9},{5,13},{9,1},{13,5},{2,10},{6,14},... | collective-permute-start | bytes 589832 | tf_op jit(solution)/shard_map/ppermute | solution.py:305
  33.0 11.7 %copy-start = (bf16[128,64,128]{2,1,0:T(8,128)(2,1)S(1)}, bf16[128,64,128]{2,1,0:T(8,128)(2,1)}, u32[]{:S(2)}) copy-start(bf16[128,64,128]{2,1,0:T(8,128)(2,1)} %param.13) | copy-start | bytes 6291460
  34.6 3.8 %copy-start.12 = (bf16[192,512]{1,0:T(8,128)(2,1)}, bf16[192,512]{1,0:T(8,128)(2,1)S(1)}, u32[]{:S(2)}) copy-start(bf16[192,512]{1,0:T(8,128)(2,1)S(1)} %get-tuple-element.46) | copy-start | bytes 589828
  38.4 4.7 %copy-start.6 = (bf16[192,512]{1,0:T(8,128)(2,1)}, bf16[192,512]{1,0:T(8,128)(2,1)S(1)}, u32[]{:S(2)}) copy-start(bf16[192,512]{1,0:T(8,128)(2,1)S(1)} %collective-permute-done.3.refs_2_) | copy-start | bytes 589828
  38.4 18.6 %all-to-all-start.1 = ((bf16[32,64,128]{2,1,0:T(8,128)(2,1)}), bf16[32,64,128]{2,1,0:T(8,128)(2,1)S(1)}, u32[]{:S(2)}, u32[]{:S(2)}) async-start(bf16[32,64,128]{2,1,0:T(8,128)(2,1)} %bitcast.7), calls=%async_computation.1 | async-start | bytes 1048576 | tf_op jit(solution)/shard_map/all_to_all | solution.py:374
  41.3 17.6 %collective-permute-start.4 = (bf16[192,512]{1,0:T(8,128)(2,1)}, bf16[192,512]{1,0:T(8,128)(2,1)}, u32[]{:S(2)}, u32[]{:S(2)}) collective-permute-start(bf16[192,512]{1,0:T(8,128)(2,1)} %copy-done.12), channel_id=1, source_target_pairs={{0,4},{4,0},{8,12},{12,8},{1,5},{5,1},{9,13},{13,9},{2,6},{6,2},{1... | collective-permute-start | bytes 589832 | tf_op jit(solution)/shard_map/ppermute | solution.py:305
  43.1 19.9 %copy-start.1 = (bf16[32,64,128]{2,1,0:T(8,128)(2,1)S(1)}, bf16[32,64,128]{2,1,0:T(8,128)(2,1)}, u32[]{:S(2)}) copy-start(bf16[32,64,128]{2,1,0:T(8,128)(2,1)} %norm.1.bias_ref) | copy-start | bytes 1572868
  43.1 19.9 %copy-start.9 = (bf16[128,16]{0,1:T(8,128)(2,1)S(1)}, bf16[128,16]{0,1:T(8,128)(2,1)}, u32[]{:S(2)}) copy-start(bf16[128,16]{0,1:T(8,128)(2,1)} %param.15) | copy-start | bytes 12292
  43.1 19.9 %copy-start.11 = (f32[128]{0:T(128)S(1)}, f32[128]{0:T(128)}, u32[]{:S(2)}) copy-start(f32[128]{0:T(128)} %param.14) | copy-start | bytes 1540
  43.1 15.7 %collective-permute-start.5 = (bf16[192,512]{1,0:T(8,128)(2,1)}, bf16[192,512]{1,0:T(8,128)(2,1)}, u32[]{:S(2)}, u32[]{:S(2)}) collective-permute-start(bf16[192,512]{1,0:T(8,128)(2,1)} %get-tuple-element.47), channel_id=1, source_target_pairs={{0,12},{4,8},{8,4},{12,0},{1,13},{5,9},{9,5},{13,1},{2,14},{6,10},... | collective-permute-start | bytes 589832 | tf_op jit(solution)/shard_map/ppermute | solution.py:305
  58.9 12.2 %all-to-all-start.2 = ((bf16[32,16,128]{2,1,0:T(8,128)(2,1)}), bf16[32,16,128]{2,1,0:T(8,128)(2,1)S(1)}, u32[]{:S(2)}, u32[]{:S(2)}) async-start(bf16[32,16,128]{2,1,0:T(8,128)(2,1)} %reduce.1), calls=%async_computation.2 | async-start | bytes 262144 | tf_op jit(solution)/shard_map/all_to_all | solution.py:384
  63.1 3.9 %copy-start.7 = (bf16[192,512]{1,0:T(8,128)(2,1)S(1)}, bf16[192,512]{1,0:T(8,128)(2,1)}, u32[]{:S(2)}) copy-start(bf16[192,512]{1,0:T(8,128)(2,1)} %copy-done.6) | copy-start | bytes 589828

commit v4 on v3

--- a/solution.py
+++ b/solution.py
@@ -17,9 +17,11 @@
 BIG = 60
 SMALL = 24
 SPLIT = 1
-ORDER = (0, 2, 1, 3)
-FIRST = (2,)
-EARLY = (1, 3)
+ORDER = (0, 1, 2, 3)
+FIRST = ()
+NEXT = ()
+EARLY = (3,)
+LATE = (1, 2)
 NT = (((1,), (1,)), ((), ()))
 TN = (((0,), (0,)), ((), ()))
 
@@ -50,16 +52,41 @@
     return max(n for n in range(1, most + 1) if count % n == 0)
 
 
-def pack_kernel(dim, mate_ref, q_ref, k_ref, v_ref, g_ref, map_ref, mask_ref, *refs):
-    *send_refs, grad_s, sems = refs
-    copies = []
-    for k, send_ref in enumerate(send_refs):
-        part = pl.ds(pl.multiple_of(jnp.bitwise_xor(mate_ref[0], k) * dim, 16), dim)
-        for n, from_ref in enumerate((q_ref, k_ref, v_ref, g_ref)):
-            to_ref = grad_s.at[k] if n == 3 else send_ref.at[n * dim : (n + 1) * dim]
-            copies.append(pltpu.make_async_copy(from_ref.at[0, part], to_ref, sems.at[k, n]))
+def head_part(mate_ref, k, dim):
+    return pl.ds(pl.multiple_of(jnp.bitwise_xor(mate_ref[0], k) * dim, 16), dim)
+
+
+def pack_kernel(dim, mate_ref, *refs):
+    from_refs, send_refs, sems = refs[:4], refs[4:-1], refs[-1]
+    copies = [
+        pltpu.make_async_copy(
+            from_ref.at[0, head_part(mate_ref, k, dim)], send_ref.at[n * dim : (n + 1) * dim], sems.at[k, n]
+        )
+        for k, send_ref in enumerate(send_refs)
+        for n, from_ref in enumerate(from_refs)
+    ]
     for copy in copies:
         copy.start()
+    for copy in copies:
+        copy.wait()
+
+
+def unpack_kernel(some, dim, mate_ref, *refs):
+    *refs, sems = refs
+    copies = [
+        pltpu.make_async_copy(
+            got_ref.at[n * dim : (n + 1) * dim], out_ref.at[0, head_part(mate_ref, k, dim)], sems.at[m, n]
+        )
+        for m, (k, got_ref) in enumerate(zip(some, refs))
+        for n, out_ref in enumerate(refs[-4:])
+    ]
+    for copy in copies:
+        copy.start()
+    for copy in copies:
+        copy.wait()
+
+
+def weight_kernel(map_ref, mask_ref, weight_ref):
     count = mask_ref.shape[1]
     atoms = map_ref.shape[1]
     rows = pl.cdiv(count, 128)
@@ -71,18 +98,7 @@
     is_lane = (lax.broadcasted_iota(jnp.int32, (128, atoms), 0) == low).astype(F32).astype(BF16)
     counts = dot(is_row, is_lane, NT)
     line = jnp.concatenate([counts[r : r + 1, :] for r in range(rows)], axis=1)[:, :count]
-    weight = line * (count / atoms) * mask_ref[...].astype(F32)
-    for copy in copies:
-        copy.wait()
-    for k, send_ref in enumerate(send_refs):
-        send_ref[3 * dim : 4 * dim, :] = (grad_s[k].astype(F32) * weight).astype(BF16)
-
-
-def unpack_kernel(mates, dim, mate_ref, *refs):
-    for k in range(mates):
-        part = pl.ds(pl.multiple_of(jnp.bitwise_xor(mate_ref[0], k) * dim, 16), dim)
-        for n, out_ref in enumerate(refs[mates:]):
-            out_ref[0, part, :] = refs[k][n * dim : (n + 1) * dim, :]
+    weight_ref[...] = line * (count / atoms) * mask_ref[...].astype(F32)
 
 
 def copies_of(near_ref, far_ref, sems, block):
@@ -153,7 +169,7 @@
 
 def attend_kernel(samples, wide, last, *refs):
     got_refs, refs = refs[:samples], refs[samples:]
-    bias_ref, mask_ref, refs = refs[0], refs[1], refs[2:]
+    bias_ref, mask_ref, weight_ref, refs = refs[0], refs[1], refs[2], refs[3:]
     before_ref, refs = (None, refs) if len(refs) == samples + 5 else (refs[0], refs[1:])
     back_refs, refs = refs[:samples], refs[samples:]
     grad_ref, key_s, value_s, dk_s, dv_s = refs
@@ -186,7 +202,8 @@
             expo_b = expo.astype(BF16)
             out = dot(got_ref[2 * dim : 3 * dim, :], expo_b) * inv_sum
             back_ref[0:dim, lanes] = out.astype(BF16)
-            grad = (got_ref[3 * dim : 4 * dim, lanes].astype(F32) * inv_sum).astype(BF16)
+            grad_in = (got_ref[3 * dim : 4 * dim, lanes].astype(F32) * weight_ref[:, lanes]).astype(BF16)
+            grad = (grad_in.astype(F32) * inv_sum).astype(BF16)
             row_dot = jnp.sum(grad.astype(F32) * out, axis=0, keepdims=True)
             dscore = expo * (dot(value_s[s], grad) - row_dot)
             total = dscore if total is None else total + dscore
@@ -218,9 +235,13 @@
         plain = gathered(groups, mates, heads, h, got_ref) * inv_ref[...]
         plain_s[h * half : (h + 1) * half, :] = to_halves(plain)
     total = jnp.zeros((heads, chan), F32)
-    for p in range(half):
-        plain = plain_s[pl.ds(p, heads, stride=half), :].astype(BF16)
-        total += dot(plain, jnp.concatenate([pair_ref[h, p] for h in range(halves)], axis=0))
+    many = step_of(half, 8)
+    for first in range(0, half, many):
+        some = range(first, first + many)
+        plain = jnp.concatenate([plain_s[pl.ds(p, heads, stride=half), :] for p in some], axis=1)
+        total += dot(
+            plain.astype(BF16), jnp.concatenate([pair_ref[h, p] for p in some for h in range(halves)], axis=0)
+        )
     total = (total - jnp.mean(total, axis=1, keepdims=True)).astype(BF16)
     for n in range(devices):
         sum_ref[n] = total
@@ -315,12 +336,12 @@
 
     chunks = (jax.ShapeDtypeStruct((4 * dim, count), BF16),) * mates
     send = call(
-        functools.partial(pack_kernel, dim), "pack", 2 * 16 * 128 * atom_map.shape[0],
-        16 * width * count, SMALL, out_shape=chunks,
-        in_specs=[scalar] + [far] * 4 + [vector] * 2,
+        functools.partial(pack_kernel, dim), "pack", 0, 16 * width * count, SMALL,
+        out_shape=chunks,
+        in_specs=[scalar] + [far] * 4,
         out_specs=(vector,) * mates,
-        scratch_shapes=[pltpu.VMEM((mates, dim, count), BF16), pltpu.SemaphoreType.DMA((mates, 4))],
-    )(mate, queries, keys, values, out_grad, atom_map.reshape(1, -1), mask_row)
+        scratch_shapes=[pltpu.SemaphoreType.DMA((mates, 4))],
+    )(mate, queries, keys, values, out_grad)
     got = swap(send)
 
     bias_send = call(
@@ -333,20 +354,17 @@
     )(pair, gain_row, proj_rows)
     bias = lax.all_to_all(bias_send, axes, 0, 0, tiled=True)
 
-    inv_std = call(
-        functools.partial(prepare_kernel, block), "prepare", 2 * entries * chan * heads, 2 * entries * chan, SMALL,
-        out_shape=jax.ShapeDtypeStruct((cols, rows), F32),
-        in_specs=[vector],
-        out_specs=vector,
-        scratch_shapes=[pltpu.VMEM((half, 2 * cols), F32)],
-    )(pair)
+    weight = call(
+        weight_kernel, "weight", 2 * 144 * atom_map.shape[0], 0, SMALL,
+        out_shape=jax.ShapeDtypeStruct((1, count), F32),
+    )(atom_map.reshape(1, -1), mask_row)
 
     fine = rows % 128 == 0
     samp = groups * mates
     bias = bias.reshape(samp, head_parts, cols, rows)
     if not fine:
         bias = bias.transpose(0, 2, 1, 3).reshape(1, 1, count, count)
-    wide = max(rows, step_of(count, 256)) if fine else count
+    wide = max(rows, step_of(count, 512)) if fine else count
     order = sorted(range(mates), key=lambda k: ORDER.index(k) if k in ORDER else k)
     back, before = [None] * mates, ()
     for n in range(0, mates, SPLIT):
@@ -363,13 +381,21 @@
                 pltpu.VMEM((many, dim, count), F32),
                 pltpu.VMEM((many, dim, count), F32),
             ],
-        )(*[got[k] for k in part], bias, mask_row, *before)
+        )(*[got[k] for k in part], bias, mask_row, weight, *before)
         before = (grads,)
         for k, x in zip(part, outs):
             back[k] = x
     if not fine:
         grads = grads.reshape(samp, cols, head_parts, rows).transpose(0, 2, 1, 3)
     swapped = swap(back)
+    pair_later, swapped = together(pair, swapped, NEXT)
+    inv_std = call(
+        functools.partial(prepare_kernel, block), "prepare", 2 * entries * chan * heads, 2 * entries * chan, SMALL,
+        out_shape=jax.ShapeDtypeStruct((cols, rows), F32),
+        in_specs=[vector],
+        out_specs=vector,
+        scratch_shapes=[pltpu.VMEM((half, 2 * cols), F32)],
+    )(pair_later)
     grads, swapped = together(grads, swapped, FIRST)
     grads = lax.all_to_all(grads.reshape(devices, cols, rows), axes, 0, 0, tiled=True)
     parts = call(
@@ -383,6 +409,21 @@
     parts, swapped = together(parts, swapped, EARLY)
     sums = lax.all_to_all(parts, axes, 0, 0, tiled=True)
 
+    def unpacked(some, wholes):
+        some = [k for k in some if k < mates]
+        if not some:
+            return wholes
+        return call(
+            functools.partial(unpack_kernel, some, dim), "unpack", 0, 16 * width * count, SMALL,
+            out_shape=(jax.ShapeDtypeStruct(queries.shape, BF16),) * 4,
+            in_specs=[scalar] + [vector] * len(some) + [far] * len(wholes),
+            out_specs=(far,) * 4,
+            scratch_shapes=[pltpu.SemaphoreType.DMA((len(some), 4))],
+            input_output_aliases={1 + len(some) + n: n for n in range(len(wholes))},
+        )(mate, *[swapped[k] for k in some], *wholes)
+
+    wholes = unpacked([k for k in range(mates) if k not in LATE], ())
+    grads, wholes = lax.optimization_barrier((grads, wholes))
     pair_grad = call(
         functools.partial(pair_kernel, groups, mates, block), "pair_grad", 8 * entries * chan * heads,
         4 * entries * chan, SMALL,
@@ -391,12 +432,8 @@
         out_specs=far,
         scratch_shapes=[near, sems, by_head, by_head],
     )(grads, bias_send, inv_std, gain_row, proj_rows, pair)
-    pair_grad, swapped = lax.optimization_barrier((pair_grad, swapped))
-    attended, query_grad, key_grad, value_grad = call(
-        functools.partial(unpack_kernel, mates, dim), "unpack", 0, 16 * width * count, SMALL,
-        out_shape=(jax.ShapeDtypeStruct(queries.shape, BF16),) * 4,
-        in_specs=[scalar] + [vector] * mates,
-    )(mate, *swapped)
+    pair_grad, swapped = together(pair_grad, swapped, LATE)
+    attended, query_grad, key_grad, value_grad = unpacked(LATE, wholes)
     weight_rows, gain_grad = call(
         functools.partial(final_kernel, 1.0 / count), "final", 0, 2 * devices * heads * chan, SMALL,
         out_shape=(

time: 72.1 us -> 71 us (0.985)
  Pallas kernels: 24.5 us -> 22.3 us
  starting transfers between devices: 22.6 us -> 23.8 us
  waiting for transfers between devices: 23.7 us -> 22.9 us
    all_to_all x1, waiting for transfers between devices: 2.13 us -> 0.01 us  [local(): sums = lax.all_to_all(parts, axes, 0, 0, tiled=True)]
    pallas_call x4, Pallas kernels: 7.4 us -> 5.61 us  [local(): call(functools.partial(attend_kernel, many, wide, last), 'attend', 12 * m...]
    ppermute x6, starting transfers between devices: 8.24 us -> 9.42 us  [swap(): lax.ppermute(x, axes[1], [(i, i ^ k) for i in range(mates)])]
    all_to_all x1, starting transfers between devices: 2.88 us -> 3.73 us  [local(): lax.all_to_all(grads.reshape(devices, cols, rows), axes, 0, 0, tiled=True)]
    all_to_all x1, starting transfers between devices: 4.15 us -> 3.32 us  [local(): sums = lax.all_to_all(parts, axes, 0, 0, tiled=True)]
    all_to_all x1, waiting for transfers between devices: 9.59 us -> 10.4 us  [local(): bias = lax.all_to_all(bias_send, axes, 0, 0, tiled=True)]
    pallas_call x2 -> x4, Pallas kernels: 4.28 us -> 4.1 us  [the longest x2 2.53 us: unpacked(): call(functools.partial(unpack_kernel, some, dim), 'unpack', 0, 16 * width...]
  transfers between devices with their start and end apart: 9 -> 9, of which waited for: 4 -> 5; matrix products, arithmetic and copies ran while one was open for 0% -> 0% of each run, Pallas kernels for 27% -> 21%
where the time goes in v4:
time: 71 us; the launch traced here: 70.6 us
  starting transfers between devices  23.8 us (34%)
  waiting for transfers between devices  22.9 us (32%)
  Pallas kernels  22.3 us (31%)
  between operations  0.92 us (1%)
  local copies, waits for them, and re-layouts  0.74 us (1%)
    all_to_all x1, waiting for transfers between devices, local(): lax.all_to_all(grads.reshape(devices, cols, rows), axes, 0, 0, tiled=True)  11.2 us
    all_to_all x1, waiting for transfers between devices, local(): bias = lax.all_to_all(bias_send, axes, 0, 0, tiled=True)  10.4 us
    ppermute x6, starting transfers between devices, swap(): lax.ppermute(x, axes[1], [(i, i ^ k) for i in range(mates)])  9.42 us
    all_to_all x1, starting transfers between devices, local(): bias = lax.all_to_all(bias_send, axes, 0, 0, tiled=True)  7.3 us
    pallas_call x4, Pallas kernels, local(): call(functools.partial(attend_kernel, many, wide, last), 'attend', 12 * m...  5.61 us
    pallas_call x1, Pallas kernels, local(): call(functools.partial(norm_kernel, groups, mates, block), 'norm', 2 * en...  4.72 us
    pallas_call x1, Pallas kernels, local(): call(functools.partial(pair_kernel, groups, mates, block), 'pair_grad', 8...  3.91 us
    all_to_all x1, starting transfers between devices, local(): lax.all_to_all(grads.reshape(devices, cols, rows), axes, 0, 0, tiled=True)  3.73 us
  transfers between devices with their start and end apart: 9, of which 5 were waited for; matrix products, arithmetic and copies ran while one was open for 0% of the time, Pallas kernels for 21%

profile of v4, /device:TPU:0, one launch (start us, length us, event | category | flops | bytes accessed | tf_op | source)
XLA Modules:
  0.0 70.6 jit_solution(13403490761146419388)
XLA Ops:
  0.7 4.7 %norm.1.bias_ref = bf16[32,64,128]{2,1,0:T(8,128)(2,1)} custom-call(bf16[2,64,64,128]{3,2,1,0:T(8,128)(2,1)} %bitcast.11, f32[1,128]{1,0:T(1,128)} %bitcast.28, bf16[16,128]{1,0:T(8,128)(2,1)} %bitcast.24), custom_call_target="tpu_custom_call" | custom-call | flops 33554432 | bytes 2097152 | tf_op jit(solution)/shard_map/norm/pallas_call | solution.py:347
  5.4 7.3 %all-to-all-start = ((bf16[32,64,128]{2,1,0:T(8,128)(2,1)}), bf16[32,64,128]{2,1,0:T(8,128)(2,1)S(1)}, u32[]{:S(2)}, u32[]{:S(2)}) async-start(bf16[32,64,128]{2,1,0:T(8,128)(2,1)} %norm.1.bias_ref), calls=%async_computation | async-start | bytes 1048576 | tf_op jit(solution)/shard_map/all_to_all | solution.py:355
  12.8 1.2 %pack.1 = (bf16[192,512]{1,0:T(8,128)(2,1)S(1)}, bf16[192,512]{1,0:T(8,128)(2,1)S(1)}, bf16[192,512]{1,0:T(8,128)(2,1)S(1)}, bf16[192,512]{1,0:T(8,128)(2,1)S(1)}) custom-call(s32[1]{0:T(128)} %bitcast.mate_ref, bf16[1,192,512]{2,1,0:T(8,128)(2,1)S(1)} %copy-done.2, bf16[1,192,512]{2,1,0:T(8,128)(2,1)S(1)} %copy-done.3, bf16[1,192,512]{2,1,0:T(8,128)(2,1)S(1)} %copy-done.4, ...), custom_call_target="tpu_custom_call" | custom-call | bytes 1572864 | tf_op jit(solution)/shard_map/pack/pallas_call | solution.py:338
  14.0 1.8 %collective-permute-start.2 = (bf16[192,512]{1,0:T(8,128)(2,1)S(1)}, bf16[192,512]{1,0:T(8,128)(2,1)S(1)}, u32[]{:S(2)}, u32[]{:S(2)}) collective-permute-start(bf16[192,512]{1,0:T(8,128)(2,1)S(1)} %get-tuple-element.41), channel_id=1, source_target_pairs={{0,4},{4,0},{8,12},{12,8},{1,5},{5,1},{9,13},{13,9},{2,6},{6,2},{1... | collective-permute-start | bytes 589832 | tf_op jit(solution)/shard_map/ppermute | solution.py:326
  15.8 1.5 %collective-permute-start.1 = (bf16[192,512]{1,0:T(8,128)(2,1)S(1)}, bf16[192,512]{1,0:T(8,128)(2,1)S(1)}, u32[]{:S(2)}, u32[]{:S(2)}) collective-permute-start(bf16[192,512]{1,0:T(8,128)(2,1)S(1)} %get-tuple-element.40), channel_id=1, source_target_pairs={{0,8},{4,12},{8,0},{12,4},{1,9},{5,13},{9,1},{13,5},{2,10},{6,14},... | collective-permute-start | bytes 589832 | tf_op jit(solution)/shard_map/ppermute | solution.py:326
  17.9 10.4 %all-to-all-done = bf16[32,64,128]{2,1,0:T(8,128)(2,1)S(1)} async-done(((bf16[32,64,128]{2,1,0:T(8,128)(2,1)}), bf16[32,64,128]{2,1,0:T(8,128)(2,1)S(1)}, u32[]{:S(2)}, u32[]{:S(2)}) %all-to-all-start) | async-done | bytes 524320 | tf_op jit(solution)/shard_map/all_to_all | solution.py:355
  28.3 1.2 %attend.4 = (bf16[192,512]{1,0:T(8,128)(2,1)S(1)}, f32[512,512]{1,0:T(8,128)S(1)}) custom-call(bf16[192,512]{1,0:T(8,128)(2,1)S(1)} %get-tuple-element.42.refs_0_, bf16[8,4,64,128]{3,2,1,0:T(8,128)(2,1)S(1)} %bitcast.15, s32[1,512]{1,0:T(1,128)S(1)} %bitcast.20, f32[1,512]{1,0:T(1,128)S(1)} %weight.1.refs_3_), custom_call_target="tpu_custom_call" | custom-call | flops 150994944 | bytes 1441792 | tf_op jit(solution)/shard_map/attend/pallas_call | solution.py:373
  29.5 1.2 %attend.5 = (bf16[192,512]{1,0:T(8,128)(2,1)S(1)}, f32[512,512]{1,0:T(8,128)S(1)}) custom-call(bf16[192,512]{1,0:T(8,128)(2,1)S(1)} %collective-permute-done.2.refs_0_, bf16[8,4,64,128]{3,2,1,0:T(8,128)(2,1)S(1)} %bitcast.16, s32[1,512]{1,0:T(1,128)S(1)} %bitcast.21, f32[1,512]{1,0:T(1,128)S(1)} %weight.1.refs_3_, f32[512,512]{1,0:T(8,128)S(1)} %get-tuple-element.43.refs_4_), custom_call_target="tpu_custom_call" | custom-call | flops 150994944 | bytes 1441792 | tf_op jit(solution)/shard_map/attend/pallas_call | solution.py:373
  30.8 0.7 copy-done.10
  31.5 1.2 %attend.6 = (bf16[192,512]{1,0:T(8,128)(2,1)S(1)}, f32[512,512]{1,0:T(8,128)S(1)}) custom-call(bf16[192,512]{1,0:T(8,128)(2,1)S(1)} %collective-permute-done.1.refs_0_, bf16[8,4,64,128]{3,2,1,0:T(8,128)(2,1)S(1)} %bitcast.17, s32[1,512]{1,0:T(1,128)S(1)} %bitcast.22, f32[1,512]{1,0:T(1,128)S(1)} %weight.1.refs_3_, f32[512,512]{1,0:T(8,128)S(1)} %get-tuple-element.44.refs_4_), custom_call_target="tpu_custom_call" | custom-call | flops 150994944 | bytes 1441792 | tf_op jit(solution)/shard_map/attend/pallas_call | solution.py:373
  32.7 0.6 collective-permute-done.refs_0_
  33.3 1.9 %attend.7 = (bf16[192,512]{1,0:T(8,128)(2,1)}, bf16[8,4,64,128]{3,2,1,0:T(8,128)(2,1)}) custom-call(bf16[192,512]{1,0:T(8,128)(2,1)S(1)} %collective-permute-done.refs_0_, bf16[8,4,64,128]{3,2,1,0:T(8,128)(2,1)S(1)} %bitcast.18, s32[1,512]{1,0:T(1,128)S(1)} %bitcast.23, f32[1,512]{1,0:T(1,128)S(1)} %weight.1.refs_3_, f32[512,512]{1,0:T(8,128)S(1)} %get-tuple-element.45.refs_4_), custom_call_target="tpu_custom_call" | custom-call | flops 150994944 | bytes 1441792 | tf_op jit(solution)/shard_map/attend/pallas_call | solution.py:373
  35.3 3.7 %all-to-all-start.1 = ((bf16[32,64,128]{2,1,0:T(8,128)(2,1)}), bf16[32,64,128]{2,1,0:T(8,128)(2,1)S(1)}, u32[]{:S(2)}, u32[]{:S(2)}) async-start(bf16[32,64,128]{2,1,0:T(8,128)(2,1)} %bitcast.7), calls=%async_computation.1 | async-start | bytes 1048576 | tf_op jit(solution)/shard_map/all_to_all | solution.py:400
  39.0 2.7 %collective-permute-start.3 = (bf16[192,512]{1,0:T(8,128)(2,1)}, bf16[192,512]{1,0:T(8,128)(2,1)}, u32[]{:S(2)}, u32[]{:S(2)}) collective-permute-start(bf16[192,512]{1,0:T(8,128)(2,1)} %get-tuple-element.48), channel_id=1, source_target_pairs={{0,12},{4,8},{8,4},{12,0},{1,13},{5,9},{9,5},{13,1},{2,14},{6,10},... | collective-permute-start | bytes 589832 | tf_op jit(solution)/shard_map/ppermute | solution.py:326
  41.7 1.7 %prepare.1.inv_ref = f32[64,128]{1,0:T(8,128)S(1)} custom-call(bf16[2,64,64,128]{3,2,1,0:T(8,128)(2,1)S(1)} %bitcast.12), custom_call_target="tpu_custom_call" | custom-call | flops 33554432 | bytes 2097152 | tf_op jit(solution)/shard_map/prepare/pallas_call | solution.py:392
  43.4 11.2 %all-to-all-done.1.got_ref = bf16[32,64,128]{2,1,0:T(8,128)(2,1)S(1)} async-done(((bf16[32,64,128]{2,1,0:T(8,128)(2,1)}), bf16[32,64,128]{2,1,0:T(8,128)(2,1)S(1)}, u32[]{:S(2)}, u32[]{:S(2)}) %all-to-all-start.1) | async-done | bytes 524320 | tf_op jit(solution)/shard_map/all_to_all | solution.py:400
  54.6 1.7 %reduce.1 = bf16[32,16,128]{2,1,0:T(8,128)(2,1)} custom-call(bf16[32,64,128]{2,1,0:T(8,128)(2,1)S(1)} %all-to-all-done.1.got_ref, f32[64,128]{1,0:T(8,128)S(1)} %prepare.1.inv_ref, bf16[2,64,64,128]{3,2,1,0:T(8,128)(2,1)S(1)} %bitcast.13), custom_call_target="tpu_custom_call" | custom-call | flops 33554432 | bytes 2097152 | tf_op jit(solution)/shard_map/reduce/pallas_call | solution.py:401
  56.3 3.3 %all-to-all-start.2 = ((bf16[32,16,128]{2,1,0:T(8,128)(2,1)}), bf16[32,16,128]{2,1,0:T(8,128)(2,1)S(1)}, u32[]{:S(2)}, u32[]{:S(2)}) async-start(bf16[32,16,128]{2,1,0:T(8,128)(2,1)} %reduce.1), calls=%async_computation.2 | async-start | bytes 262144 | tf_op jit(solution)/shard_map/all_to_all | solution.py:410
  59.7 1.7 %collective-permute-start.5 = (bf16[192,512]{1,0:T(8,128)(2,1)}, bf16[192,512]{1,0:T(8,128)(2,1)S(1)}, u32[]{:S(2)}, u32[]{:S(2)}) collective-permute-start(bf16[192,512]{1,0:T(8,128)(2,1)} %copy-done.11), channel_id=1, source_target_pairs={{0,8},{4,12},{8,0},{12,4},{1,9},{5,13},{9,1},{13,5},{2,10},{6,14},... | collective-permute-start | bytes 589832 | tf_op jit(solution)/shard_map/ppermute | solution.py:326
  61.3 1.5 %collective-permute-start.4 = (bf16[192,512]{1,0:T(8,128)(2,1)}, bf16[192,512]{1,0:T(8,128)(2,1)S(1)}, u32[]{:S(2)}, u32[]{:S(2)}) collective-permute-start(bf16[192,512]{1,0:T(8,128)(2,1)} %copy-done.10), channel_id=1, source_target_pairs={{0,4},{4,0},{8,12},{12,8},{1,5},{5,1},{9,13},{13,9},{2,6},{6,2},{1... | collective-permute-start | bytes 589832 | tf_op jit(solution)/shard_map/ppermute | solution.py:326
  62.8 1.7 %unpack.2 = (bf16[1,192,512]{2,1,0:T(8,128)(2,1)}, bf16[1,192,512]{2,1,0:T(8,128)(2,1)}, bf16[1,192,512]{2,1,0:T(8,128)(2,1)}, bf16[1,192,512]{2,1,0:T(8,128)(2,1)}) custom-call(s32[1]{0:T(128)} %bitcast.mate_ref, bf16[192,512]{1,0:T(8,128)(2,1)S(1)} %get-tuple-element.47.refs_0_, bf16[192,512]{1,0:T(8,128)(2,1)} %collective-permute-done.3.refs_1_), custom_call_target="tpu_custom_call" | custom-call | bytes 1572864 | tf_op jit(solution)/shard_map/unpack/pallas_call | solution.py:416
  64.6 3.9 %pair_grad.1 = bf16[2,64,64,128]{3,2,1,0:T(8,128)(2,1)} custom-call(bf16[32,64,128]{2,1,0:T(8,128)(2,1)S(1)} %all-to-all-done.1.got_ref, bf16[32,64,128]{2,1,0:T(8,128)(2,1)S(1)} %copy-done.1, f32[64,128]{1,0:T(8,128)S(1)} %prepare.1.inv_ref, f32[1,128]{1,0:T(1,128)S(1)} %bitcast.29, bf16[16,128]{1,0:T(8,128)(2,1)S(1)} %bitcast.25, ...), custom_call_target="tpu_custom_call" | custom-call | flops 134217728 | bytes 4194304 | tf_op jit(solution)/shard_map/pair_grad/pallas_call | solution.py:427
  69.2 0.8 %unpack.3 = (bf16[1,192,512]{2,1,0:T(8,128)(2,1)}, bf16[1,192,512]{2,1,0:T(8,128)(2,1)}, bf16[1,192,512]{2,1,0:T(8,128)(2,1)}, bf16[1,192,512]{2,1,0:T(8,128)(2,1)}) custom-call(s32[1]{0:T(128)} %bitcast.mate_ref, bf16[192,512]{1,0:T(8,128)(2,1)S(1)} %collective-permute-done.4.refs_0_, ...), custom_call_target="tpu_custom_call", output_to_operand_aliasing={{0}: (3, {}), {1}: (4, {}), {2}: (5, {}), {3}: (6, {})} | custom-call | bytes 1572864 | tf_op jit(solution)/shard_map/unpack/pallas_call | solution.py:416
  70.0 0.6 final.1
  (31 shorter events, 1.4 us)
Async XLA Ops:
  0.6 12.1 %copy-start.5 = (bf16[1,192,512]{2,1,0:T(8,128)(2,1)S(1)}, bf16[1,192,512]{2,1,0:T(8,128)(2,1)}, u32[]{:S(2)}) copy-start(bf16[1,192,512]{2,1,0:T(8,128)(2,1)} %refs_3_.1) | copy-start | bytes 589828
  0.6 12.1 %copy-start.4 = (bf16[1,192,512]{2,1,0:T(8,128)(2,1)S(1)}, bf16[1,192,512]{2,1,0:T(8,128)(2,1)}, u32[]{:S(2)}) copy-start(bf16[1,192,512]{2,1,0:T(8,128)(2,1)} %refs_2_.1) | copy-start | bytes 589828
  0.7 12.1 %copy-start.3 = (bf16[1,192,512]{2,1,0:T(8,128)(2,1)S(1)}, bf16[1,192,512]{2,1,0:T(8,128)(2,1)}, u32[]{:S(2)}) copy-start(bf16[1,192,512]{2,1,0:T(8,128)(2,1)} %refs_1_.1) | copy-start | bytes 589828
  0.7 12.1 %copy-start.2 = (bf16[1,192,512]{2,1,0:T(8,128)(2,1)S(1)}, bf16[1,192,512]{2,1,0:T(8,128)(2,1)}, u32[]{:S(2)}) copy-start(bf16[1,192,512]{2,1,0:T(8,128)(2,1)} %refs_0_.1) | copy-start | bytes 589828
  0.7 16.9 %copy-start.6 = (s32[512]{0:T(512)S(1)}, s32[512]{0:T(512)}, u32[]{:S(2)}) copy-start(s32[512]{0:T(512)} %param.16) | copy-start | bytes 6148
  0.7 16.8 %copy-start.8 = (s32[4096]{0:T(1024)S(1)}, s32[4096]{0:T(1024)}, u32[]{:S(2)}) copy-start(s32[4096]{0:T(1024)} %param.17) | copy-start | bytes 49156
  5.4 22.9 %all-to-all-start = ((bf16[32,64,128]{2,1,0:T(8,128)(2,1)}), bf16[32,64,128]{2,1,0:T(8,128)(2,1)S(1)}, u32[]{:S(2)}, u32[]{:S(2)}) async-start(bf16[32,64,128]{2,1,0:T(8,128)(2,1)} %norm.1.bias_ref), calls=%async_computation | async-start | bytes 1048576 | tf_op jit(solution)/shard_map/all_to_all | solution.py:355
  14.0 15.5 %collective-permute-start.2 = (bf16[192,512]{1,0:T(8,128)(2,1)S(1)}, bf16[192,512]{1,0:T(8,128)(2,1)S(1)}, u32[]{:S(2)}, u32[]{:S(2)}) collective-permute-start(bf16[192,512]{1,0:T(8,128)(2,1)S(1)} %get-tuple-element.41), channel_id=1, source_target_pairs={{0,4},{4,0},{8,12},{12,8},{1,5},{5,1},{9,13},{13,9},{2,6},{6,2},{1... | collective-permute-start | bytes 589832 | tf_op jit(solution)/shard_map/ppermute | solution.py:326
  15.8 15.7 %collective-permute-start.1 = (bf16[192,512]{1,0:T(8,128)(2,1)S(1)}, bf16[192,512]{1,0:T(8,128)(2,1)S(1)}, u32[]{:S(2)}, u32[]{:S(2)}) collective-permute-start(bf16[192,512]{1,0:T(8,128)(2,1)S(1)} %get-tuple-element.40), channel_id=1, source_target_pairs={{0,8},{4,12},{8,0},{12,4},{1,9},{5,13},{9,1},{13,5},{2,10},{6,14},... | collective-permute-start | bytes 589832 | tf_op jit(solution)/shard_map/ppermute | solution.py:326
  17.3 16.1 %collective-permute-start = (bf16[192,512]{1,0:T(8,128)(2,1)S(1)}, bf16[192,512]{1,0:T(8,128)(2,1)S(1)}, u32[]{:S(2)}, u32[]{:S(2)}) collective-permute-start(bf16[192,512]{1,0:T(8,128)(2,1)S(1)} %get-tuple-element.39), channel_id=1, source_target_pairs={{0,12},{4,8},{8,4},{12,0},{1,13},{5,9},{9,5},{13,1},{2,14},{6,10},... | collective-permute-start | bytes 589832 | tf_op jit(solution)/shard_map/ppermute | solution.py:326
  30.8 0.7 copy-start.10
  31.5 10.3 %copy-start = (bf16[128,64,128]{2,1,0:T(8,128)(2,1)S(1)}, bf16[128,64,128]{2,1,0:T(8,128)(2,1)}, u32[]{:S(2)}) copy-start(bf16[128,64,128]{2,1,0:T(8,128)(2,1)} %param.13) | copy-start | bytes 6291460
  32.7 2.6 %copy-start.11 = (bf16[192,512]{1,0:T(8,128)(2,1)}, bf16[192,512]{1,0:T(8,128)(2,1)S(1)}, u32[]{:S(2)}) copy-start(bf16[192,512]{1,0:T(8,128)(2,1)S(1)} %get-tuple-element.56) | copy-start | bytes 589828
  35.3 19.3 %all-to-all-start.1 = ((bf16[32,64,128]{2,1,0:T(8,128)(2,1)}), bf16[32,64,128]{2,1,0:T(8,128)(2,1)S(1)}, u32[]{:S(2)}, u32[]{:S(2)}) async-start(bf16[32,64,128]{2,1,0:T(8,128)(2,1)} %bitcast.7), calls=%async_computation.1 | async-start | bytes 1048576 | tf_op jit(solution)/shard_map/all_to_all | solution.py:400
  39.0 17.3 %collective-permute-start.3 = (bf16[192,512]{1,0:T(8,128)(2,1)}, bf16[192,512]{1,0:T(8,128)(2,1)}, u32[]{:S(2)}, u32[]{:S(2)}) collective-permute-start(bf16[192,512]{1,0:T(8,128)(2,1)} %get-tuple-element.48), channel_id=1, source_target_pairs={{0,12},{4,8},{8,4},{12,0},{1,13},{5,9},{9,5},{13,1},{2,14},{6,10},... | collective-permute-start | bytes 589832 | tf_op jit(solution)/shard_map/ppermute | solution.py:326
  43.4 21.1 %copy-start.1 = (bf16[32,64,128]{2,1,0:T(8,128)(2,1)S(1)}, bf16[32,64,128]{2,1,0:T(8,128)(2,1)}, u32[]{:S(2)}) copy-start(bf16[32,64,128]{2,1,0:T(8,128)(2,1)} %norm.1.bias_ref) | copy-start | bytes 1572868
  43.4 21.1 %copy-start.7 = (bf16[128,16]{0,1:T(8,128)(2,1)S(1)}, bf16[128,16]{0,1:T(8,128)(2,1)}, u32[]{:S(2)}) copy-start(bf16[128,16]{0,1:T(8,128)(2,1)} %param.15) | copy-start | bytes 12292
  43.4 21.1 %copy-start.9 = (f32[128]{0:T(128)S(1)}, f32[128]{0:T(128)}, u32[]{:S(2)}) copy-start(f32[128]{0:T(128)} %param.14) | copy-start | bytes 1540
  56.3 13.7 %all-to-all-start.2 = ((bf16[32,16,128]{2,1,0:T(8,128)(2,1)}), bf16[32,16,128]{2,1,0:T(8,128)(2,1)S(1)}, u32[]{:S(2)}, u32[]{:S(2)}) async-start(bf16[32,16,128]{2,1,0:T(8,128)(2,1)} %reduce.1), calls=%async_computation.2 | async-start | bytes 262144 | tf_op jit(solution)/shard_map/all_to_all | solution.py:410
  59.7 9.0 %collective-permute-start.5 = (bf16[192,512]{1,0:T(8,128)(2,1)}, bf16[192,512]{1,0:T(8,128)(2,1)S(1)}, u32[]{:S(2)}, u32[]{:S(2)}) collective-permute-start(bf16[192,512]{1,0:T(8,128)(2,1)} %copy-done.11), channel_id=1, source_target_pairs={{0,8},{4,12},{8,0},{12,4},{1,9},{5,13},{9,1},{13,5},{2,10},{6,14},... | collective-permute-start | bytes 589832 | tf_op jit(solution)/shard_map/ppermute | solution.py:326
  61.3 7.9 %collective-permute-start.4 = (bf16[192,512]{1,0:T(8,128)(2,1)}, bf16[192,512]{1,0:T(8,128)(2,1)S(1)}, u32[]{:S(2)}, u32[]{:S(2)}) collective-permute-start(bf16[192,512]{1,0:T(8,128)(2,1)} %copy-done.10), channel_id=1, source_target_pairs={{0,4},{4,0},{8,12},{12,8},{1,5},{5,1},{9,13},{13,9},{2,6},{6,2},{1... | collective-permute-start | bytes 589832 | tf_op jit(solution)/shard_map/ppermute | solution.py:326

commit v5 on v4

--- a/solution.py
+++ b/solution.py
@@ -71,15 +71,18 @@
         copy.wait()
 
 
-def unpack_kernel(some, dim, mate_ref, *refs):
-    *refs, sems = refs
-    copies = [
+def unpack_copies(some, dim, mate_ref, got_refs, out_refs, sems):
+    return [
         pltpu.make_async_copy(
             got_ref.at[n * dim : (n + 1) * dim], out_ref.at[0, head_part(mate_ref, k, dim)], sems.at[m, n]
         )
-        for m, (k, got_ref) in enumerate(zip(some, refs))
-        for n, out_ref in enumerate(refs[-4:])
+        for m, (k, got_ref) in enumerate(zip(some, got_refs))
+        for n, out_ref in enumerate(out_refs)
     ]
+
+
+def unpack_kernel(some, dim, mate_ref, *refs):
+    copies = unpack_copies(some, dim, mate_ref, refs[: len(some)], refs[-5:-1], refs[-1])
     for copy in copies:
         copy.start()
     for copy in copies:
@@ -259,10 +262,13 @@
     return grad
 
 
-def pair_kernel(
-    groups, mates, block, got_ref, bias_ref, inv_ref, gain_ref, proj_ref, pair_ref, out_ref,
-    out_s, sems, plain_s, biased_s,
-):
+def pair_kernel(groups, mates, block, some, dim, mate_ref, *refs):
+    chunk_refs, refs = refs[: len(some)], refs[len(some) :]
+    got_ref, bias_ref, inv_ref, gain_ref, proj_ref, pair_ref, out_ref, *refs = refs
+    *whole_refs, out_s, sems, plain_s, biased_s, chunk_sems = refs
+    chunks = unpack_copies(some, dim, mate_ref, chunk_refs, whole_refs, chunk_sems)
+    for copy in chunks:
+        copy.start()
     halves, half, cols, chan = pair_ref.shape
     heads = proj_ref.shape[0]
     outs = copies_of(out_s, out_ref, sems, block)
@@ -290,7 +296,7 @@
                 part = slice(h * cols, (h + 1) * cols)
                 out_s[h, p] = (both[part, :chan] - cent[h, p - first] * both[part, chan:]).astype(BF16)
         copy.start()
-    for copy in outs:
+    for copy in outs + chunks:
         copy.wait()
 
 
@@ -330,7 +336,7 @@
     block = step_of(half, 16)
     far = pl.BlockSpec(memory_space=pltpu.HBM)
     tiles = jax.ShapeDtypeStruct((devices, cols, rows), BF16)
-    by_head = pltpu.VMEM((heads * half, 2 * cols), F32)
+    by_head = pltpu.VMEM(((heads + 1) * half, 2 * cols), F32)
     near = pltpu.VMEM(pair.shape, BF16)
     sems = pltpu.SemaphoreType.DMA((half // block,))
 
@@ -409,31 +415,27 @@
     parts, swapped = together(parts, swapped, EARLY)
     sums = lax.all_to_all(parts, axes, 0, 0, tiled=True)
 
-    def unpacked(some, wholes):
-        some = [k for k in some if k < mates]
-        if not some:
-            return wholes
-        return call(
-            functools.partial(unpack_kernel, some, dim), "unpack", 0, 16 * width * count, SMALL,
-            out_shape=(jax.ShapeDtypeStruct(queries.shape, BF16),) * 4,
-            in_specs=[scalar] + [vector] * len(some) + [far] * len(wholes),
+    early, late = [k for k in range(mates) if k not in LATE], [k for k in LATE if k < mates]
+    whole_outs = (jax.ShapeDtypeStruct(queries.shape, BF16),) * 4
+    pair_grad, *wholes = call(
+        functools.partial(pair_kernel, groups, mates, block, early, dim), "pair_grad", 8 * entries * chan * heads,
+        4 * entries * chan, SMALL,
+        out_shape=(jax.ShapeDtypeStruct(pair.shape, BF16),) + whole_outs,
+        in_specs=[scalar] + [vector] * (len(early) + 6),
+        out_specs=(far,) * 5,
+        scratch_shapes=[near, sems, by_head, by_head, pltpu.SemaphoreType.DMA((len(early), 4))],
+    )(mate, *[swapped[k] for k in early], grads, bias_send, inv_std, gain_row, proj_rows, pair)
+    pair_grad, swapped = together(pair_grad, swapped, LATE)
+    if late:
+        wholes = call(
+            functools.partial(unpack_kernel, late, dim), "unpack", 0, 16 * width * count, SMALL,
+            out_shape=whole_outs,
+            in_specs=[scalar] + [vector] * len(late) + [far] * 4,
             out_specs=(far,) * 4,
-            scratch_shapes=[pltpu.SemaphoreType.DMA((len(some), 4))],
-            input_output_aliases={1 + len(some) + n: n for n in range(len(wholes))},
-        )(mate, *[swapped[k] for k in some], *wholes)
-
-    wholes = unpacked([k for k in range(mates) if k not in LATE], ())
-    grads, wholes = lax.optimization_barrier((grads, wholes))
-    pair_grad = call(
-        functools.partial(pair_kernel, groups, mates, block), "pair_grad", 8 * entries * chan * heads,
-        4 * entries * chan, SMALL,
-        out_shape=jax.ShapeDtypeStruct(pair.shape, BF16),
-        in_specs=[vector] * 6,
-        out_specs=far,
-        scratch_shapes=[near, sems, by_head, by_head],
-    )(grads, bias_send, inv_std, gain_row, proj_rows, pair)
-    pair_grad, swapped = together(pair_grad, swapped, LATE)
-    attended, query_grad, key_grad, value_grad = unpacked(LATE, wholes)
+            scratch_shapes=[pltpu.SemaphoreType.DMA((len(late), 4))],
+            input_output_aliases={1 + len(late) + n: n for n in range(4)},
+        )(mate, *[swapped[k] for k in late], *wholes)
+    attended, query_grad, key_grad, value_grad = wholes
     weight_rows, gain_grad = call(
         functools.partial(final_kernel, 1.0 / count), "final", 0, 2 * devices * heads * chan, SMALL,
         out_shape=(

time: 71 us -> 70.8 us (level)
    ppermute x6, waiting for transfers between devices: 1.33 us -> 2.19 us  [swap(): lax.ppermute(x, axes[1], [(i, i ^ k) for i in range(mates)])]
    pallas_call x3 -> x2, Pallas kernels: 6.44 us -> 5.64 us  [the longest x1 4.84 us: local(): call(functools.partial(pair_kernel, groups, mates, block, early, dim), 'p...]
where the time goes in v5:
time: 70.8 us; the launch traced here: 70.4 us
  starting transfers between devices  23.8 us (34%)
  waiting for transfers between devices  23 us (32%)
  Pallas kernels  21.8 us (31%)
  between operations  0.91 us (1%)
  local copies, waits for them, and re-layouts  0.73 us (1%)
    all_to_all x1, waiting for transfers between devices, local(): lax.all_to_all(grads.reshape(devices, cols, rows), axes, 0, 0, tiled=True)  11.2 us
    all_to_all x1, waiting for transfers between devices, local(): bias = lax.all_to_all(bias_send, axes, 0, 0, tiled=True)  9.69 us
    ppermute x6, starting transfers between devices, swap(): lax.ppermute(x, axes[1], [(i, i ^ k) for i in range(mates)])  9.42 us
    all_to_all x1, starting transfers between devices, local(): bias = lax.all_to_all(bias_send, axes, 0, 0, tiled=True)  7.3 us
    pallas_call x4, Pallas kernels, local(): call(functools.partial(attend_kernel, many, wide, last), 'attend', 12 * m...  5.29 us
    pallas_call x1, Pallas kernels, local(): call(functools.partial(pair_kernel, groups, mates, block, early, dim), 'p...  4.84 us
    pallas_call x1, Pallas kernels, local(): call(functools.partial(norm_kernel, groups, mates, block), 'norm', 2 * en...  4.72 us
    all_to_all x1, starting transfers between devices, local(): lax.all_to_all(grads.reshape(devices, cols, rows), axes, 0, 0, tiled=True)  3.73 us
  transfers between devices with their start and end apart: 9, of which 5 were waited for; matrix products, arithmetic and copies ran while one was open for 0% of the time, Pallas kernels for 21%

profile of v5, /device:TPU:0, one launch (start us, length us, event | category | flops | bytes accessed | tf_op | source)
XLA Modules:
  0.0 70.4 jit_solution(10479288524404296699)
XLA Ops:
  0.7 4.7 %norm.1.refs_3_ = bf16[32,64,128]{2,1,0:T(8,128)(2,1)} custom-call(bf16[2,64,64,128]{3,2,1,0:T(8,128)(2,1)} %bitcast.11, f32[1,128]{1,0:T(1,128)} %bitcast.28, bf16[16,128]{1,0:T(8,128)(2,1)} %bitcast.24), custom_call_target="tpu_custom_call" | custom-call | flops 33554432 | bytes 2097152 | tf_op jit(solution)/shard_map/norm/pallas_call | solution.py:353
  5.4 7.3 %all-to-all-start = ((bf16[32,64,128]{2,1,0:T(8,128)(2,1)}), bf16[32,64,128]{2,1,0:T(8,128)(2,1)S(1)}, u32[]{:S(2)}, u32[]{:S(2)}) async-start(bf16[32,64,128]{2,1,0:T(8,128)(2,1)} %norm.1.refs_3_), calls=%async_computation | async-start | bytes 1048576 | tf_op jit(solution)/shard_map/all_to_all | solution.py:361
  12.8 1.9 %pack.1 = (bf16[192,512]{1,0:T(8,128)(2,1)S(1)}, bf16[192,512]{1,0:T(8,128)(2,1)S(1)}, bf16[192,512]{1,0:T(8,128)(2,1)S(1)}, bf16[192,512]{1,0:T(8,128)(2,1)}) custom-call(s32[1]{0:T(128)} %bitcast.mate_ref, bf16[1,192,512]{2,1,0:T(8,128)(2,1)S(1)} %copy-done.2, bf16[1,192,512]{2,1,0:T(8,128)(2,1)S(1)} %copy-done.3, bf16[1,192,512]{2,1,0:T(8,128)(2,1)S(1)} %copy-done.4, ...), custom_call_target="tpu_custom_call" | custom-call | bytes 1572864 | tf_op jit(solution)/shard_map/pack/pallas_call | solution.py:344
  14.6 1.8 %collective-permute-start.2 = (bf16[192,512]{1,0:T(8,128)(2,1)S(1)}, bf16[192,512]{1,0:T(8,128)(2,1)S(1)}, u32[]{:S(2)}, u32[]{:S(2)}) collective-permute-start(bf16[192,512]{1,0:T(8,128)(2,1)S(1)} %get-tuple-element.39), channel_id=1, source_target_pairs={{0,4},{4,0},{8,12},{12,8},{1,5},{5,1},{9,13},{13,9},{2,6},{6,2},{1... | collective-permute-start | bytes 589832 | tf_op jit(solution)/shard_map/ppermute | solution.py:332
  16.5 1.5 %collective-permute-start.1 = (bf16[192,512]{1,0:T(8,128)(2,1)S(1)}, bf16[192,512]{1,0:T(8,128)(2,1)S(1)}, u32[]{:S(2)}, u32[]{:S(2)}) collective-permute-start(bf16[192,512]{1,0:T(8,128)(2,1)S(1)} %get-tuple-element.38), channel_id=1, source_target_pairs={{0,8},{4,12},{8,0},{12,4},{1,9},{5,13},{9,1},{13,5},{2,10},{6,14},... | collective-permute-start | bytes 589832 | tf_op jit(solution)/shard_map/ppermute | solution.py:332
  18.6 9.7 %all-to-all-done = bf16[32,64,128]{2,1,0:T(8,128)(2,1)S(1)} async-done(((bf16[32,64,128]{2,1,0:T(8,128)(2,1)}), bf16[32,64,128]{2,1,0:T(8,128)(2,1)S(1)}, u32[]{:S(2)}, u32[]{:S(2)}) %all-to-all-start) | async-done | bytes 524320 | tf_op jit(solution)/shard_map/all_to_all | solution.py:361
  28.3 1.2 %attend.4 = (bf16[192,512]{1,0:T(8,128)(2,1)S(1)}, f32[512,512]{1,0:T(8,128)S(1)}) custom-call(bf16[192,512]{1,0:T(8,128)(2,1)S(1)} %get-tuple-element.35.refs_0_, bf16[8,4,64,128]{3,2,1,0:T(8,128)(2,1)S(1)} %bitcast.15, s32[1,512]{1,0:T(1,128)S(1)} %bitcast.20, f32[1,512]{1,0:T(1,128)S(1)} %weight.1.refs_3_), custom_call_target="tpu_custom_call" | custom-call | flops 150994944 | bytes 1441792 | tf_op jit(solution)/shard_map/attend/pallas_call | solution.py:379
  29.5 1.2 %attend.5 = (bf16[192,512]{1,0:T(8,128)(2,1)S(1)}, f32[512,512]{1,0:T(8,128)S(1)}) custom-call(bf16[192,512]{1,0:T(8,128)(2,1)S(1)} %collective-permute-done.2.refs_0_, bf16[8,4,64,128]{3,2,1,0:T(8,128)(2,1)S(1)} %bitcast.16, s32[1,512]{1,0:T(1,128)S(1)} %bitcast.21, f32[1,512]{1,0:T(1,128)S(1)} %weight.1.refs_3_, f32[512,512]{1,0:T(8,128)S(1)} %get-tuple-element.40.refs_4_), custom_call_target="tpu_custom_call" | custom-call | flops 150994944 | bytes 1441792 | tf_op jit(solution)/shard_map/attend/pallas_call | solution.py:379
  30.8 0.7 copy-done.10
  31.4 1.2 %attend.6 = (bf16[192,512]{1,0:T(8,128)(2,1)S(1)}, f32[512,512]{1,0:T(8,128)S(1)}) custom-call(bf16[192,512]{1,0:T(8,128)(2,1)S(1)} %collective-permute-done.1.refs_0_, bf16[8,4,64,128]{3,2,1,0:T(8,128)(2,1)S(1)} %bitcast.17, s32[1,512]{1,0:T(1,128)S(1)} %bitcast.22, f32[1,512]{1,0:T(1,128)S(1)} %weight.1.refs_3_, f32[512,512]{1,0:T(8,128)S(1)} %get-tuple-element.41.refs_4_), custom_call_target="tpu_custom_call" | custom-call | flops 150994944 | bytes 1441792 | tf_op jit(solution)/shard_map/attend/pallas_call | solution.py:379
  32.7 0.6 collective-permute-done.refs_0_
  33.3 1.6 %attend.7 = (bf16[192,512]{1,0:T(8,128)(2,1)S(1)}, bf16[8,4,64,128]{3,2,1,0:T(8,128)(2,1)}) custom-call(bf16[192,512]{1,0:T(8,128)(2,1)S(1)} %collective-permute-done.refs_0_, bf16[8,4,64,128]{3,2,1,0:T(8,128)(2,1)S(1)} %bitcast.18, s32[1,512]{1,0:T(1,128)S(1)} %bitcast.23, f32[1,512]{1,0:T(1,128)S(1)} %weight.1.refs_3_, ...), custom_call_target="tpu_custom_call" | custom-call | flops 150994944 | bytes 1441792 | tf_op jit(solution)/shard_map/attend/pallas_call | solution.py:379
  35.0 3.7 %all-to-all-start.1 = ((bf16[32,64,128]{2,1,0:T(8,128)(2,1)}), bf16[32,64,128]{2,1,0:T(8,128)(2,1)S(1)}, u32[]{:S(2)}, u32[]{:S(2)}) async-start(bf16[32,64,128]{2,1,0:T(8,128)(2,1)} %bitcast.7), calls=%async_computation.1 | async-start | bytes 1048576 | tf_op jit(solution)/shard_map/all_to_all | solution.py:406
  38.8 2.7 %collective-permute-start.3 = (bf16[192,512]{1,0:T(8,128)(2,1)}, bf16[192,512]{1,0:T(8,128)(2,1)}, u32[]{:S(2)}, u32[]{:S(2)}) collective-permute-start(bf16[192,512]{1,0:T(8,128)(2,1)} %copy-done.12), channel_id=1, source_target_pairs={{0,12},{4,8},{8,4},{12,0},{1,13},{5,9},{9,5},{13,1},{2,14},{6,10},... | collective-permute-start | bytes 589832 | tf_op jit(solution)/shard_map/ppermute | solution.py:332
  41.5 1.6 %prepare.1.inv_ref.refs_4_ = f32[64,128]{1,0:T(8,128)S(1)} custom-call(bf16[2,64,64,128]{3,2,1,0:T(8,128)(2,1)S(1)} %bitcast.12), custom_call_target="tpu_custom_call" | custom-call | flops 33554432 | bytes 2097152 | tf_op jit(solution)/shard_map/prepare/pallas_call | solution.py:398
  43.2 11.2 %all-to-all-done.1.got_ref.refs_2_ = bf16[32,64,128]{2,1,0:T(8,128)(2,1)S(1)} async-done(((bf16[32,64,128]{2,1,0:T(8,128)(2,1)}), bf16[32,64,128]{2,1,0:T(8,128)(2,1)S(1)}, u32[]{:S(2)}, u32[]{:S(2)}) %all-to-all-start.1) | async-done | bytes 524320 | tf_op jit(solution)/shard_map/all_to_all | solution.py:406
  54.3 1.6 %reduce.1 = bf16[32,16,128]{2,1,0:T(8,128)(2,1)} custom-call(bf16[32,64,128]{2,1,0:T(8,128)(2,1)S(1)} %all-to-all-done.1.got_ref.refs_2_, f32[64,128]{1,0:T(8,128)S(1)} %prepare.1.inv_ref.refs_4_, bf16[2,64,64,128]{3,2,1,0:T(8,128)(2,1)S(1)} %bitcast.13), custom_call_target="tpu_custom_call" | custom-call | flops 33554432 | bytes 2097152 | tf_op jit(solution)/shard_map/reduce/pallas_call | solution.py:407
  56.0 3.4 %all-to-all-start.2 = ((bf16[32,16,128]{2,1,0:T(8,128)(2,1)}), bf16[32,16,128]{2,1,0:T(8,128)(2,1)S(1)}, u32[]{:S(2)}, u32[]{:S(2)}) async-start(bf16[32,16,128]{2,1,0:T(8,128)(2,1)} %reduce.1), calls=%async_computation.2 | async-start | bytes 262144 | tf_op jit(solution)/shard_map/all_to_all | solution.py:416
  59.4 1.7 %collective-permute-start.5 = (bf16[192,512]{1,0:T(8,128)(2,1)}, bf16[192,512]{1,0:T(8,128)(2,1)S(1)}, u32[]{:S(2)}, u32[]{:S(2)}) collective-permute-start(bf16[192,512]{1,0:T(8,128)(2,1)} %copy-done.11), channel_id=1, source_target_pairs={{0,8},{4,12},{8,0},{12,4},{1,9},{5,13},{9,1},{13,5},{2,10},{6,14},... | collective-permute-start | bytes 589832 | tf_op jit(solution)/shard_map/ppermute | solution.py:332
  61.0 1.5 %collective-permute-start.4 = (bf16[192,512]{1,0:T(8,128)(2,1)}, bf16[192,512]{1,0:T(8,128)(2,1)S(1)}, u32[]{:S(2)}, u32[]{:S(2)}) collective-permute-start(bf16[192,512]{1,0:T(8,128)(2,1)} %copy-done.10), channel_id=1, source_target_pairs={{0,4},{4,0},{8,12},{12,8},{1,5},{5,1},{9,13},{13,9},{2,6},{6,2},{1... | collective-permute-start | bytes 589832 | tf_op jit(solution)/shard_map/ppermute | solution.py:332
  62.5 4.8 %pair_grad.1 = (bf16[2,64,64,128]{3,2,1,0:T(8,128)(2,1)}, bf16[1,192,512]{2,1,0:T(8,128)(2,1)}, bf16[1,192,512]{2,1,0:T(8,128)(2,1)}, bf16[1,192,512]{2,1,0:T(8,128)(2,1)}, bf16[1,192,512]{2,1,0:T(8,128)(2,1)}) custom-call(s32[1]{0:T(128)} %bitcast.mate_ref, bf16[192,512]{1,0:T(8,128)(2,1)S(1)} %get-tuple-element.36.refs_0_, ...), custom_call_target="tpu_custom_call" | custom-call | flops 134217728 | bytes 4194304 | tf_op jit(solution)/shard_map/pair_grad/pallas_call | solution.py:420
  67.4 1.0 %collective-permute-done.5.refs_1_ = bf16[192,512]{1,0:T(8,128)(2,1)S(1)} collective-permute-done((bf16[192,512]{1,0:T(8,128)(2,1)}, bf16[192,512]{1,0:T(8,128)(2,1)S(1)}, u32[]{:S(2)}, u32[]{:S(2)}) %collective-permute-start.5) | collective-permute-done | bytes 196640 | tf_op jit(solution)/shard_map/ppermute | solution.py:332
  68.9 0.8 %unpack.1 = (bf16[1,192,512]{2,1,0:T(8,128)(2,1)}, bf16[1,192,512]{2,1,0:T(8,128)(2,1)}, bf16[1,192,512]{2,1,0:T(8,128)(2,1)}, bf16[1,192,512]{2,1,0:T(8,128)(2,1)}) custom-call(s32[1]{0:T(128)} %bitcast.mate_ref, bf16[192,512]{1,0:T(8,128)(2,1)S(1)} %collective-permute-done.4.refs_0_, ...), custom_call_target="tpu_custom_call", output_to_operand_aliasing={{0}: (3, {}), {1}: (4, {}), {2}: (5, {}), {3}: (6, {})} | custom-call | bytes 1572864 | tf_op jit(solution)/shard_map/unpack/pallas_call | solution.py:430
  69.7 0.6 final.1
  (32 shorter events, 1.2 us)
Async XLA Ops:
  0.6 12.1 %copy-start.5 = (bf16[1,192,512]{2,1,0:T(8,128)(2,1)S(1)}, bf16[1,192,512]{2,1,0:T(8,128)(2,1)}, u32[]{:S(2)}) copy-start(bf16[1,192,512]{2,1,0:T(8,128)(2,1)} %refs_3_.1) | copy-start | bytes 589828
  0.6 12.1 %copy-start.4 = (bf16[1,192,512]{2,1,0:T(8,128)(2,1)S(1)}, bf16[1,192,512]{2,1,0:T(8,128)(2,1)}, u32[]{:S(2)}) copy-start(bf16[1,192,512]{2,1,0:T(8,128)(2,1)} %refs_2_.1) | copy-start | bytes 589828
  0.7 12.1 %copy-start.3 = (bf16[1,192,512]{2,1,0:T(8,128)(2,1)S(1)}, bf16[1,192,512]{2,1,0:T(8,128)(2,1)}, u32[]{:S(2)}) copy-start(bf16[1,192,512]{2,1,0:T(8,128)(2,1)} %refs_1_.1) | copy-start | bytes 589828
  0.7 12.1 %copy-start.2 = (bf16[1,192,512]{2,1,0:T(8,128)(2,1)S(1)}, bf16[1,192,512]{2,1,0:T(8,128)(2,1)}, u32[]{:S(2)}) copy-start(bf16[1,192,512]{2,1,0:T(8,128)(2,1)} %refs_0_.1) | copy-start | bytes 589828
  0.7 17.5 %copy-start.6 = (s32[512]{0:T(512)S(1)}, s32[512]{0:T(512)}, u32[]{:S(2)}) copy-start(s32[512]{0:T(512)} %param.16) | copy-start | bytes 6148
  0.7 17.5 %copy-start.8 = (s32[4096]{0:T(1024)S(1)}, s32[4096]{0:T(1024)}, u32[]{:S(2)}) copy-start(s32[4096]{0:T(1024)} %param.17) | copy-start | bytes 49156
  5.4 22.9 %all-to-all-start = ((bf16[32,64,128]{2,1,0:T(8,128)(2,1)}), bf16[32,64,128]{2,1,0:T(8,128)(2,1)S(1)}, u32[]{:S(2)}, u32[]{:S(2)}) async-start(bf16[32,64,128]{2,1,0:T(8,128)(2,1)} %norm.1.refs_3_), calls=%async_computation | async-start | bytes 1048576 | tf_op jit(solution)/shard_map/all_to_all | solution.py:361
  14.6 14.9 %collective-permute-start.2 = (bf16[192,512]{1,0:T(8,128)(2,1)S(1)}, bf16[192,512]{1,0:T(8,128)(2,1)S(1)}, u32[]{:S(2)}, u32[]{:S(2)}) collective-permute-start(bf16[192,512]{1,0:T(8,128)(2,1)S(1)} %get-tuple-element.39), channel_id=1, source_target_pairs={{0,4},{4,0},{8,12},{12,8},{1,5},{5,1},{9,13},{13,9},{2,6},{6,2},{1... | collective-permute-start | bytes 589832 | tf_op jit(solution)/shard_map/ppermute | solution.py:332
  16.5 14.3 %collective-permute-start.1 = (bf16[192,512]{1,0:T(8,128)(2,1)S(1)}, bf16[192,512]{1,0:T(8,128)(2,1)S(1)}, u32[]{:S(2)}, u32[]{:S(2)}) collective-permute-start(bf16[192,512]{1,0:T(8,128)(2,1)S(1)} %get-tuple-element.38), channel_id=1, source_target_pairs={{0,8},{4,12},{8,0},{12,4},{1,9},{5,13},{9,1},{13,5},{2,10},{6,14},... | collective-permute-start | bytes 589832 | tf_op jit(solution)/shard_map/ppermute | solution.py:332
  17.9 15.4 %collective-permute-start = (bf16[192,512]{1,0:T(8,128)(2,1)}, bf16[192,512]{1,0:T(8,128)(2,1)S(1)}, u32[]{:S(2)}, u32[]{:S(2)}) collective-permute-start(bf16[192,512]{1,0:T(8,128)(2,1)} %get-tuple-element.37), channel_id=1, source_target_pairs={{0,12},{4,8},{8,4},{12,0},{1,13},{5,9},{9,5},{13,1},{2,14},{6,10},... | collective-permute-start | bytes 589832 | tf_op jit(solution)/shard_map/ppermute | solution.py:332
  30.8 0.7 copy-start.10
  31.4 10.1 %copy-start = (bf16[128,64,128]{2,1,0:T(8,128)(2,1)S(1)}, bf16[128,64,128]{2,1,0:T(8,128)(2,1)}, u32[]{:S(2)}) copy-start(bf16[128,64,128]{2,1,0:T(8,128)(2,1)} %param.13) | copy-start | bytes 6291460
  32.7 6.0 %copy-start.11 = (bf16[192,512]{1,0:T(8,128)(2,1)}, bf16[192,512]{1,0:T(8,128)(2,1)S(1)}, u32[]{:S(2)}) copy-start(bf16[192,512]{1,0:T(8,128)(2,1)S(1)} %get-tuple-element.48) | copy-start | bytes 589828
  35.0 3.8 %copy-start.12 = (bf16[192,512]{1,0:T(8,128)(2,1)}, bf16[192,512]{1,0:T(8,128)(2,1)S(1)}, u32[]{:S(2)}) copy-start(bf16[192,512]{1,0:T(8,128)(2,1)S(1)} %get-tuple-element.44) | copy-start | bytes 589828
  35.0 19.3 %all-to-all-start.1 = ((bf16[32,64,128]{2,1,0:T(8,128)(2,1)}), bf16[32,64,128]{2,1,0:T(8,128)(2,1)S(1)}, u32[]{:S(2)}, u32[]{:S(2)}) async-start(bf16[32,64,128]{2,1,0:T(8,128)(2,1)} %bitcast.7), calls=%async_computation.1 | async-start | bytes 1048576 | tf_op jit(solution)/shard_map/all_to_all | solution.py:406
  38.7 23.8 %copy-start.1 = (bf16[32,64,128]{2,1,0:T(8,128)(2,1)S(1)}, bf16[32,64,128]{2,1,0:T(8,128)(2,1)}, u32[]{:S(2)}) copy-start(bf16[32,64,128]{2,1,0:T(8,128)(2,1)} %norm.1.refs_3_) | copy-start | bytes 1572868
  38.8 23.8 %copy-start.7 = (bf16[128,16]{0,1:T(8,128)(2,1)S(1)}, bf16[128,16]{0,1:T(8,128)(2,1)}, u32[]{:S(2)}) copy-start(bf16[128,16]{0,1:T(8,128)(2,1)} %param.15) | copy-start | bytes 12292
  38.8 23.7 %copy-start.9 = (f32[128]{0:T(128)S(1)}, f32[128]{0:T(128)}, u32[]{:S(2)}) copy-start(f32[128]{0:T(128)} %param.14) | copy-start | bytes 1540
  38.8 17.2 %collective-permute-start.3 = (bf16[192,512]{1,0:T(8,128)(2,1)}, bf16[192,512]{1,0:T(8,128)(2,1)}, u32[]{:S(2)}, u32[]{:S(2)}) collective-permute-start(bf16[192,512]{1,0:T(8,128)(2,1)} %copy-done.12), channel_id=1, source_target_pairs={{0,12},{4,8},{8,4},{12,0},{1,13},{5,9},{9,5},{13,1},{2,14},{6,10},... | collective-permute-start | bytes 589832 | tf_op jit(solution)/shard_map/ppermute | solution.py:332
  56.0 13.7 %all-to-all-start.2 = ((bf16[32,16,128]{2,1,0:T(8,128)(2,1)}), bf16[32,16,128]{2,1,0:T(8,128)(2,1)S(1)}, u32[]{:S(2)}, u32[]{:S(2)}) async-start(bf16[32,16,128]{2,1,0:T(8,128)(2,1)} %reduce.1), calls=%async_computation.2 | async-start | bytes 262144 | tf_op jit(solution)/shard_map/all_to_all | solution.py:416
  59.4 9.0 %collective-permute-start.5 = (bf16[192,512]{1,0:T(8,128)(2,1)}, bf16[192,512]{1,0:T(8,128)(2,1)S(1)}, u32[]{:S(2)}, u32[]{:S(2)}) collective-permute-start(bf16[192,512]{1,0:T(8,128)(2,1)} %copy-done.11), channel_id=1, source_target_pairs={{0,8},{4,12},{8,0},{12,4},{1,9},{5,13},{9,1},{13,5},{2,10},{6,14},... | collective-permute-start | bytes 589832 | tf_op jit(solution)/shard_map/ppermute | solution.py:332
  61.0 7.9 %collective-permute-start.4 = (bf16[192,512]{1,0:T(8,128)(2,1)}, bf16[192,512]{1,0:T(8,128)(2,1)S(1)}, u32[]{:S(2)}, u32[]{:S(2)}) collective-permute-start(bf16[192,512]{1,0:T(8,128)(2,1)} %copy-done.10), channel_id=1, source_target_pairs={{0,4},{4,0},{8,12},{12,8},{1,5},{5,1},{9,13},{13,9},{2,6},{6,2},{1... | collective-permute-start | bytes 589832 | tf_op jit(solution)/shard_map/ppermute | solution.py:332

commit v6 on v5

--- a/solution.py
+++ b/solution.py
@@ -17,7 +17,7 @@
 BIG = 60
 SMALL = 24
 SPLIT = 1
-ORDER = (0, 1, 2, 3)
+ORDER = (0, 2, 1, 3)
 FIRST = ()
 NEXT = ()
 EARLY = (3,)

time: 70.8 us -> 70.9 us (level)
  no operation moved by 1% of the time
where the time goes in v6:
time: 70.9 us; the launch traced here: 70.5 us
  starting transfers between devices  23.8 us (34%)
  waiting for transfers between devices  23.2 us (33%)
  Pallas kernels  21.8 us (31%)
  between operations  0.91 us (1%)
  local copies, waits for them, and re-layouts  0.73 us (1%)
    all_to_all x1, waiting for transfers between devices, local(): lax.all_to_all(grads.reshape(devices, cols, rows), axes, 0, 0, tiled=True)  11.2 us
    all_to_all x1, waiting for transfers between devices, local(): bias = lax.all_to_all(bias_send, axes, 0, 0, tiled=True)  9.69 us
    ppermute x6, starting transfers between devices, swap(): lax.ppermute(x, axes[1], [(i, i ^ k) for i in range(mates)])  9.42 us
    all_to_all x1, starting transfers between devices, local(): bias = lax.all_to_all(bias_send, axes, 0, 0, tiled=True)  7.3 us
    pallas_call x4, Pallas kernels, local(): call(functools.partial(attend_kernel, many, wide, last), 'attend', 12 * m...  5.29 us
    pallas_call x1, Pallas kernels, local(): call(functools.partial(pair_kernel, groups, mates, block, early, dim), 'p...  4.84 us
    pallas_call x1, Pallas kernels, local(): call(functools.partial(norm_kernel, groups, mates, block), 'norm', 2 * en...  4.72 us
    all_to_all x1, starting transfers between devices, local(): lax.all_to_all(grads.reshape(devices, cols, rows), axes, 0, 0, tiled=True)  3.73 us
  transfers between devices with their start and end apart: 9, of which 5 were waited for; matrix products, arithmetic and copies ran while one was open for 0% of the time, Pallas kernels for 21%

profile of v6, /device:TPU:0, one launch (start us, length us, event | category | flops | bytes accessed | tf_op | source)
XLA Modules:
  0.0 70.5 jit_solution(2074365789402235466)
XLA Ops:
  0.7 4.7 %norm.1.refs_3_ = bf16[32,64,128]{2,1,0:T(8,128)(2,1)} custom-call(bf16[2,64,64,128]{3,2,1,0:T(8,128)(2,1)} %bitcast.11, f32[1,128]{1,0:T(1,128)} %bitcast.28, bf16[16,128]{1,0:T(8,128)(2,1)} %bitcast.24), custom_call_target="tpu_custom_call" | custom-call | flops 33554432 | bytes 2097152 | tf_op jit(solution)/shard_map/norm/pallas_call | solution.py:353
  5.4 7.3 %all-to-all-start = ((bf16[32,64,128]{2,1,0:T(8,128)(2,1)}), bf16[32,64,128]{2,1,0:T(8,128)(2,1)S(1)}, u32[]{:S(2)}, u32[]{:S(2)}) async-start(bf16[32,64,128]{2,1,0:T(8,128)(2,1)} %norm.1.refs_3_), calls=%async_computation | async-start | bytes 1048576 | tf_op jit(solution)/shard_map/all_to_all | solution.py:361
  12.8 1.9 %pack.1 = (bf16[192,512]{1,0:T(8,128)(2,1)S(1)}, bf16[192,512]{1,0:T(8,128)(2,1)S(1)}, bf16[192,512]{1,0:T(8,128)(2,1)S(1)}, bf16[192,512]{1,0:T(8,128)(2,1)}) custom-call(s32[1]{0:T(128)} %bitcast.mate_ref, bf16[1,192,512]{2,1,0:T(8,128)(2,1)S(1)} %copy-done.2, bf16[1,192,512]{2,1,0:T(8,128)(2,1)S(1)} %copy-done.3, bf16[1,192,512]{2,1,0:T(8,128)(2,1)S(1)} %copy-done.4, ...), custom_call_target="tpu_custom_call" | custom-call | bytes 1572864 | tf_op jit(solution)/shard_map/pack/pallas_call | solution.py:344
  14.6 1.8 %collective-permute-start.2 = (bf16[192,512]{1,0:T(8,128)(2,1)S(1)}, bf16[192,512]{1,0:T(8,128)(2,1)S(1)}, u32[]{:S(2)}, u32[]{:S(2)}) collective-permute-start(bf16[192,512]{1,0:T(8,128)(2,1)S(1)} %get-tuple-element.39), channel_id=1, source_target_pairs={{0,8},{4,12},{8,0},{12,4},{1,9},{5,13},{9,1},{13,5},{2,10},{6,14},... | collective-permute-start | bytes 589832 | tf_op jit(solution)/shard_map/ppermute | solution.py:332
  16.5 1.5 %collective-permute-start.1 = (bf16[192,512]{1,0:T(8,128)(2,1)S(1)}, bf16[192,512]{1,0:T(8,128)(2,1)S(1)}, u32[]{:S(2)}, u32[]{:S(2)}) collective-permute-start(bf16[192,512]{1,0:T(8,128)(2,1)S(1)} %get-tuple-element.38), channel_id=1, source_target_pairs={{0,4},{4,0},{8,12},{12,8},{1,5},{5,1},{9,13},{13,9},{2,6},{6,2},{1... | collective-permute-start | bytes 589832 | tf_op jit(solution)/shard_map/ppermute | solution.py:332
  18.6 9.7 %all-to-all-done = bf16[32,64,128]{2,1,0:T(8,128)(2,1)S(1)} async-done(((bf16[32,64,128]{2,1,0:T(8,128)(2,1)}), bf16[32,64,128]{2,1,0:T(8,128)(2,1)S(1)}, u32[]{:S(2)}, u32[]{:S(2)}) %all-to-all-start) | async-done | bytes 524320 | tf_op jit(solution)/shard_map/all_to_all | solution.py:361
  28.3 1.2 %attend.4 = (bf16[192,512]{1,0:T(8,128)(2,1)S(1)}, f32[512,512]{1,0:T(8,128)S(1)}) custom-call(bf16[192,512]{1,0:T(8,128)(2,1)S(1)} %get-tuple-element.35.refs_0_, bf16[8,4,64,128]{3,2,1,0:T(8,128)(2,1)S(1)} %bitcast.15, s32[1,512]{1,0:T(1,128)S(1)} %bitcast.20, f32[1,512]{1,0:T(1,128)S(1)} %weight.1.refs_3_), custom_call_target="tpu_custom_call" | custom-call | flops 150994944 | bytes 1441792 | tf_op jit(solution)/shard_map/attend/pallas_call | solution.py:379
  29.5 1.2 %attend.5 = (bf16[192,512]{1,0:T(8,128)(2,1)S(1)}, f32[512,512]{1,0:T(8,128)S(1)}) custom-call(bf16[192,512]{1,0:T(8,128)(2,1)S(1)} %collective-permute-done.2.refs_0_, bf16[8,4,64,128]{3,2,1,0:T(8,128)(2,1)S(1)} %bitcast.16, s32[1,512]{1,0:T(1,128)S(1)} %bitcast.21, f32[1,512]{1,0:T(1,128)S(1)} %weight.1.refs_3_, f32[512,512]{1,0:T(8,128)S(1)} %get-tuple-element.40.refs_4_), custom_call_target="tpu_custom_call" | custom-call | flops 150994944 | bytes 1441792 | tf_op jit(solution)/shard_map/attend/pallas_call | solution.py:379
  30.8 0.7 copy-done.10
  31.4 1.2 %attend.6 = (bf16[192,512]{1,0:T(8,128)(2,1)S(1)}, f32[512,512]{1,0:T(8,128)S(1)}) custom-call(bf16[192,512]{1,0:T(8,128)(2,1)S(1)} %collective-permute-done.1.refs_0_, bf16[8,4,64,128]{3,2,1,0:T(8,128)(2,1)S(1)} %bitcast.17, s32[1,512]{1,0:T(1,128)S(1)} %bitcast.22, f32[1,512]{1,0:T(1,128)S(1)} %weight.1.refs_3_, f32[512,512]{1,0:T(8,128)S(1)} %get-tuple-element.41.refs_4_), custom_call_target="tpu_custom_call" | custom-call | flops 150994944 | bytes 1441792 | tf_op jit(solution)/shard_map/attend/pallas_call | solution.py:379
  32.7 0.6 collective-permute-done.refs_0_
  33.3 1.6 %attend.7 = (bf16[192,512]{1,0:T(8,128)(2,1)S(1)}, bf16[8,4,64,128]{3,2,1,0:T(8,128)(2,1)}) custom-call(bf16[192,512]{1,0:T(8,128)(2,1)S(1)} %collective-permute-done.refs_0_, bf16[8,4,64,128]{3,2,1,0:T(8,128)(2,1)S(1)} %bitcast.18, s32[1,512]{1,0:T(1,128)S(1)} %bitcast.23, f32[1,512]{1,0:T(1,128)S(1)} %weight.1.refs_3_, ...), custom_call_target="tpu_custom_call" | custom-call | flops 150994944 | bytes 1441792 | tf_op jit(solution)/shard_map/attend/pallas_call | solution.py:379
  35.0 3.7 %all-to-all-start.1 = ((bf16[32,64,128]{2,1,0:T(8,128)(2,1)}), bf16[32,64,128]{2,1,0:T(8,128)(2,1)S(1)}, u32[]{:S(2)}, u32[]{:S(2)}) async-start(bf16[32,64,128]{2,1,0:T(8,128)(2,1)} %bitcast.7), calls=%async_computation.1 | async-start | bytes 1048576 | tf_op jit(solution)/shard_map/all_to_all | solution.py:406
  38.8 2.7 %collective-permute-start.3 = (bf16[192,512]{1,0:T(8,128)(2,1)}, bf16[192,512]{1,0:T(8,128)(2,1)}, u32[]{:S(2)}, u32[]{:S(2)}) collective-permute-start(bf16[192,512]{1,0:T(8,128)(2,1)} %copy-done.12), channel_id=1, source_target_pairs={{0,12},{4,8},{8,4},{12,0},{1,13},{5,9},{9,5},{13,1},{2,14},{6,10},... | collective-permute-start | bytes 589832 | tf_op jit(solution)/shard_map/ppermute | solution.py:332
  41.5 1.6 %prepare.1.inv_ref.refs_4_ = f32[64,128]{1,0:T(8,128)S(1)} custom-call(bf16[2,64,64,128]{3,2,1,0:T(8,128)(2,1)S(1)} %bitcast.12), custom_call_target="tpu_custom_call" | custom-call | flops 33554432 | bytes 2097152 | tf_op jit(solution)/shard_map/prepare/pallas_call | solution.py:398
  43.2 11.2 %all-to-all-done.1.got_ref.refs_2_ = bf16[32,64,128]{2,1,0:T(8,128)(2,1)S(1)} async-done(((bf16[32,64,128]{2,1,0:T(8,128)(2,1)}), bf16[32,64,128]{2,1,0:T(8,128)(2,1)S(1)}, u32[]{:S(2)}, u32[]{:S(2)}) %all-to-all-start.1) | async-done | bytes 524320 | tf_op jit(solution)/shard_map/all_to_all | solution.py:406
  54.3 1.6 %reduce.1 = bf16[32,16,128]{2,1,0:T(8,128)(2,1)} custom-call(bf16[32,64,128]{2,1,0:T(8,128)(2,1)S(1)} %all-to-all-done.1.got_ref.refs_2_, f32[64,128]{1,0:T(8,128)S(1)} %prepare.1.inv_ref.refs_4_, bf16[2,64,64,128]{3,2,1,0:T(8,128)(2,1)S(1)} %bitcast.13), custom_call_target="tpu_custom_call" | custom-call | flops 33554432 | bytes 2097152 | tf_op jit(solution)/shard_map/reduce/pallas_call | solution.py:407
  56.0 3.4 %all-to-all-start.2 = ((bf16[32,16,128]{2,1,0:T(8,128)(2,1)}), bf16[32,16,128]{2,1,0:T(8,128)(2,1)S(1)}, u32[]{:S(2)}, u32[]{:S(2)}) async-start(bf16[32,16,128]{2,1,0:T(8,128)(2,1)} %reduce.1), calls=%async_computation.2 | async-start | bytes 262144 | tf_op jit(solution)/shard_map/all_to_all | solution.py:416
  59.4 1.7 %collective-permute-start.4 = (bf16[192,512]{1,0:T(8,128)(2,1)}, bf16[192,512]{1,0:T(8,128)(2,1)S(1)}, u32[]{:S(2)}, u32[]{:S(2)}) collective-permute-start(bf16[192,512]{1,0:T(8,128)(2,1)} %copy-done.11), channel_id=1, source_target_pairs={{0,4},{4,0},{8,12},{12,8},{1,5},{5,1},{9,13},{13,9},{2,6},{6,2},{1... | collective-permute-start | bytes 589832 | tf_op jit(solution)/shard_map/ppermute | solution.py:332
  61.0 1.5 %collective-permute-start.5 = (bf16[192,512]{1,0:T(8,128)(2,1)}, bf16[192,512]{1,0:T(8,128)(2,1)S(1)}, u32[]{:S(2)}, u32[]{:S(2)}) collective-permute-start(bf16[192,512]{1,0:T(8,128)(2,1)} %copy-done.10), channel_id=1, source_target_pairs={{0,8},{4,12},{8,0},{12,4},{1,9},{5,13},{9,1},{13,5},{2,10},{6,14},... | collective-permute-start | bytes 589832 | tf_op jit(solution)/shard_map/ppermute | solution.py:332
  62.5 4.8 %pair_grad.1 = (bf16[2,64,64,128]{3,2,1,0:T(8,128)(2,1)}, bf16[1,192,512]{2,1,0:T(8,128)(2,1)}, bf16[1,192,512]{2,1,0:T(8,128)(2,1)}, bf16[1,192,512]{2,1,0:T(8,128)(2,1)}, bf16[1,192,512]{2,1,0:T(8,128)(2,1)}) custom-call(s32[1]{0:T(128)} %bitcast.mate_ref, bf16[192,512]{1,0:T(8,128)(2,1)S(1)} %get-tuple-element.36.refs_0_, ...), custom_call_target="tpu_custom_call" | custom-call | flops 134217728 | bytes 4194304 | tf_op jit(solution)/shard_map/pair_grad/pallas_call | solution.py:420
  67.8 1.2 %collective-permute-done.5.refs_1_ = bf16[192,512]{1,0:T(8,128)(2,1)S(1)} collective-permute-done((bf16[192,512]{1,0:T(8,128)(2,1)}, bf16[192,512]{1,0:T(8,128)(2,1)S(1)}, u32[]{:S(2)}, u32[]{:S(2)}) %collective-permute-start.5) | collective-permute-done | bytes 196640 | tf_op jit(solution)/shard_map/ppermute | solution.py:332
  69.0 0.8 %unpack.1 = (bf16[1,192,512]{2,1,0:T(8,128)(2,1)}, bf16[1,192,512]{2,1,0:T(8,128)(2,1)}, bf16[1,192,512]{2,1,0:T(8,128)(2,1)}, bf16[1,192,512]{2,1,0:T(8,128)(2,1)}) custom-call(s32[1]{0:T(128)} %bitcast.mate_ref, bf16[192,512]{1,0:T(8,128)(2,1)S(1)} %collective-permute-done.4.refs_0_, ...), custom_call_target="tpu_custom_call", output_to_operand_aliasing={{0}: (3, {}), {1}: (4, {}), {2}: (5, {}), {3}: (6, {})} | custom-call | bytes 1572864 | tf_op jit(solution)/shard_map/unpack/pallas_call | solution.py:430
  69.8 0.6 final.1
  (32 shorter events, 1.2 us)
Async XLA Ops:
  0.6 12.1 %copy-start.5 = (bf16[1,192,512]{2,1,0:T(8,128)(2,1)S(1)}, bf16[1,192,512]{2,1,0:T(8,128)(2,1)}, u32[]{:S(2)}) copy-start(bf16[1,192,512]{2,1,0:T(8,128)(2,1)} %refs_3_.1) | copy-start | bytes 589828
  0.6 12.1 %copy-start.4 = (bf16[1,192,512]{2,1,0:T(8,128)(2,1)S(1)}, bf16[1,192,512]{2,1,0:T(8,128)(2,1)}, u32[]{:S(2)}) copy-start(bf16[1,192,512]{2,1,0:T(8,128)(2,1)} %refs_2_.1) | copy-start | bytes 589828
  0.7 12.1 %copy-start.3 = (bf16[1,192,512]{2,1,0:T(8,128)(2,1)S(1)}, bf16[1,192,512]{2,1,0:T(8,128)(2,1)}, u32[]{:S(2)}) copy-start(bf16[1,192,512]{2,1,0:T(8,128)(2,1)} %refs_1_.1) | copy-start | bytes 589828
  0.7 12.1 %copy-start.2 = (bf16[1,192,512]{2,1,0:T(8,128)(2,1)S(1)}, bf16[1,192,512]{2,1,0:T(8,128)(2,1)}, u32[]{:S(2)}) copy-start(bf16[1,192,512]{2,1,0:T(8,128)(2,1)} %refs_0_.1) | copy-start | bytes 589828
  0.7 17.5 %copy-start.6 = (s32[512]{0:T(512)S(1)}, s32[512]{0:T(512)}, u32[]{:S(2)}) copy-start(s32[512]{0:T(512)} %param.16) | copy-start | bytes 6148
  0.7 17.5 %copy-start.8 = (s32[4096]{0:T(1024)S(1)}, s32[4096]{0:T(1024)}, u32[]{:S(2)}) copy-start(s32[4096]{0:T(1024)} %param.17) | copy-start | bytes 49156
  5.4 22.9 %all-to-all-start = ((bf16[32,64,128]{2,1,0:T(8,128)(2,1)}), bf16[32,64,128]{2,1,0:T(8,128)(2,1)S(1)}, u32[]{:S(2)}, u32[]{:S(2)}) async-start(bf16[32,64,128]{2,1,0:T(8,128)(2,1)} %norm.1.refs_3_), calls=%async_computation | async-start | bytes 1048576 | tf_op jit(solution)/shard_map/all_to_all | solution.py:361
  14.6 14.9 %collective-permute-start.2 = (bf16[192,512]{1,0:T(8,128)(2,1)S(1)}, bf16[192,512]{1,0:T(8,128)(2,1)S(1)}, u32[]{:S(2)}, u32[]{:S(2)}) collective-permute-start(bf16[192,512]{1,0:T(8,128)(2,1)S(1)} %get-tuple-element.39), channel_id=1, source_target_pairs={{0,8},{4,12},{8,0},{12,4},{1,9},{5,13},{9,1},{13,5},{2,10},{6,14},... | collective-permute-start | bytes 589832 | tf_op jit(solution)/shard_map/ppermute | solution.py:332
  16.5 14.3 %collective-permute-start.1 = (bf16[192,512]{1,0:T(8,128)(2,1)S(1)}, bf16[192,512]{1,0:T(8,128)(2,1)S(1)}, u32[]{:S(2)}, u32[]{:S(2)}) collective-permute-start(bf16[192,512]{1,0:T(8,128)(2,1)S(1)} %get-tuple-element.38), channel_id=1, source_target_pairs={{0,4},{4,0},{8,12},{12,8},{1,5},{5,1},{9,13},{13,9},{2,6},{6,2},{1... | collective-permute-start | bytes 589832 | tf_op jit(solution)/shard_map/ppermute | solution.py:332
  17.9 15.4 %collective-permute-start = (bf16[192,512]{1,0:T(8,128)(2,1)}, bf16[192,512]{1,0:T(8,128)(2,1)S(1)}, u32[]{:S(2)}, u32[]{:S(2)}) collective-permute-start(bf16[192,512]{1,0:T(8,128)(2,1)} %get-tuple-element.37), channel_id=1, source_target_pairs={{0,12},{4,8},{8,4},{12,0},{1,13},{5,9},{9,5},{13,1},{2,14},{6,10},... | collective-permute-start | bytes 589832 | tf_op jit(solution)/shard_map/ppermute | solution.py:332
  30.8 0.7 copy-start.10
  31.4 10.1 %copy-start = (bf16[128,64,128]{2,1,0:T(8,128)(2,1)S(1)}, bf16[128,64,128]{2,1,0:T(8,128)(2,1)}, u32[]{:S(2)}) copy-start(bf16[128,64,128]{2,1,0:T(8,128)(2,1)} %param.13) | copy-start | bytes 6291460
  32.7 6.0 %copy-start.11 = (bf16[192,512]{1,0:T(8,128)(2,1)}, bf16[192,512]{1,0:T(8,128)(2,1)S(1)}, u32[]{:S(2)}) copy-start(bf16[192,512]{1,0:T(8,128)(2,1)S(1)} %get-tuple-element.47) | copy-start | bytes 589828
  35.0 3.8 %copy-start.12 = (bf16[192,512]{1,0:T(8,128)(2,1)}, bf16[192,512]{1,0:T(8,128)(2,1)S(1)}, u32[]{:S(2)}) copy-start(bf16[192,512]{1,0:T(8,128)(2,1)S(1)} %get-tuple-element.44) | copy-start | bytes 589828
  35.0 19.3 %all-to-all-start.1 = ((bf16[32,64,128]{2,1,0:T(8,128)(2,1)}), bf16[32,64,128]{2,1,0:T(8,128)(2,1)S(1)}, u32[]{:S(2)}, u32[]{:S(2)}) async-start(bf16[32,64,128]{2,1,0:T(8,128)(2,1)} %bitcast.7), calls=%async_computation.1 | async-start | bytes 1048576 | tf_op jit(solution)/shard_map/all_to_all | solution.py:406
  38.7 23.8 %copy-start.1 = (bf16[32,64,128]{2,1,0:T(8,128)(2,1)S(1)}, bf16[32,64,128]{2,1,0:T(8,128)(2,1)}, u32[]{:S(2)}) copy-start(bf16[32,64,128]{2,1,0:T(8,128)(2,1)} %norm.1.refs_3_) | copy-start | bytes 1572868
  38.8 23.8 %copy-start.7 = (bf16[128,16]{0,1:T(8,128)(2,1)S(1)}, bf16[128,16]{0,1:T(8,128)(2,1)}, u32[]{:S(2)}) copy-start(bf16[128,16]{0,1:T(8,128)(2,1)} %param.15) | copy-start | bytes 12292
  38.8 23.7 %copy-start.9 = (f32[128]{0:T(128)S(1)}, f32[128]{0:T(128)}, u32[]{:S(2)}) copy-start(f32[128]{0:T(128)} %param.14) | copy-start | bytes 1540
  38.8 17.2 %collective-permute-start.3 = (bf16[192,512]{1,0:T(8,128)(2,1)}, bf16[192,512]{1,0:T(8,128)(2,1)}, u32[]{:S(2)}, u32[]{:S(2)}) collective-permute-start(bf16[192,512]{1,0:T(8,128)(2,1)} %copy-done.12), channel_id=1, source_target_pairs={{0,12},{4,8},{8,4},{12,0},{1,13},{5,9},{9,5},{13,1},{2,14},{6,10},... | collective-permute-start | bytes 589832 | tf_op jit(solution)/shard_map/ppermute | solution.py:332
  56.0 13.8 %all-to-all-start.2 = ((bf16[32,16,128]{2,1,0:T(8,128)(2,1)}), bf16[32,16,128]{2,1,0:T(8,128)(2,1)S(1)}, u32[]{:S(2)}, u32[]{:S(2)}) async-start(bf16[32,16,128]{2,1,0:T(8,128)(2,1)} %reduce.1), calls=%async_computation.2 | async-start | bytes 262144 | tf_op jit(solution)/shard_map/all_to_all | solution.py:416
  59.4 8.4 %collective-permute-start.4 = (bf16[192,512]{1,0:T(8,128)(2,1)}, bf16[192,512]{1,0:T(8,128)(2,1)S(1)}, u32[]{:S(2)}, u32[]{:S(2)}) collective-permute-start(bf16[192,512]{1,0:T(8,128)(2,1)} %copy-done.11), channel_id=1, source_target_pairs={{0,4},{4,0},{8,12},{12,8},{1,5},{5,1},{9,13},{13,9},{2,6},{6,2},{1... | collective-permute-start | bytes 589832 | tf_op jit(solution)/shard_map/ppermute | solution.py:332
  61.0 8.0 %collective-permute-start.5 = (bf16[192,512]{1,0:T(8,128)(2,1)}, bf16[192,512]{1,0:T(8,128)(2,1)S(1)}, u32[]{:S(2)}, u32[]{:S(2)}) collective-permute-start(bf16[192,512]{1,0:T(8,128)(2,1)} %copy-done.10), channel_id=1, source_target_pairs={{0,8},{4,12},{8,0},{12,4},{1,9},{5,13},{9,1},{13,5},{2,10},{6,14},... | collective-permute-start | bytes 589832 | tf_op jit(solution)/shard_map/ppermute | solution.py:332
